TPU v7x, 32 devices: a whole 2x2x4 slice. The times are simulated.
32 devices in a mesh: seq: 8 (over y, x, core), head: 4 (over z).
Axes of the slice: x: 2, y: 2, z: 4, core: 2. Of those that a mesh axis runs over, the one named last changes fastest.
Arguments:
- layer_input: bfloat16 [4096, 5376], P('seq'), may hold values from -6 to 6
- query: bfloat16 [4096, 4096], P('seq', 'head'), may hold values from -6 to 6
- keys: bfloat16 [4096, 2048], P('seq', 'head'), may hold values from -6 to 6
- values: bfloat16 [4096, 2048], P('seq', 'head'), may hold values from -6 to 6
- out_grad: bfloat16 [4096, 4096], P('seq', 'head'), may hold values from -6 to 6
- w_query: bfloat16 [5376, 4096], P(None, 'head'), may hold values from -0.078125 to 0.078125
- w_key: bfloat16 [5376, 2048], P(None, 'head'), may hold values from -0.078125 to 0.078125
- w_value: bfloat16 [5376, 2048], P(None, 'head'), may hold values from -0.078125 to 0.078125
- proof_lengths: int32 [8], replicated, may hold values from 1 to 2048, 4096 in all
Outputs:
- input_grad: bfloat16 [4096, 5376], P('seq', 'head')
- wq_grad: bfloat16 [5376, 4096], P('seq', 'head')
- wk_grad: bfloat16 [5376, 2048], P('seq', 'head')
- wv_grad: bfloat16 [5376, 2048], P('seq', 'head')
Inputs may be any that keep to these rules, and one draw needn't show every extreme that they name: `proof_lengths`: the lengths of the 8 proofs packed in order; they sum to 4096 and the longest has exactly 2048 tokens.
All inputs are finite; a program needn't handle non-finite values.
Results may differ from a plain program's by a relative error of at most 0.015.
Values may be sent and summed in bfloat16 or wider, within the bound.
No kernel may reach another device: no remote copies, remote signals or barrier semaphores. Data moves between devices by JAX's collectives and lax.ppermute only.
A program may use at most 128 MiB of HBM per device.

v0:
```python
import jax
import jax.numpy as jnp
from jax import lax
from jax.sharding import PartitionSpec as P

D = 5376
H = 32
HD = 128
WINDOW = 1024


def shifted(block, axis, distance):
    devices = range(lax.axis_size(axis))
    route = [(i - distance, i) for i in devices if i - distance in devices]
    return lax.ppermute(block, axis, route)


def proof_index(positions, proof_lengths):
    lengths_sum = jnp.cumsum(proof_lengths)
    starts_at = lengths_sum - proof_lengths
    counted = jnp.sum((positions[:, None] >= starts_at[None, :]).astype(jnp.int32), axis=1)
    return counted - 1


def build_mask(query_pos, key_pos, query_seg, key_seg):
    before = key_pos[None, :] <= query_pos[:, None]
    inside = query_pos[:, None] - key_pos[None, :] < WINDOW
    present = key_pos[None, :] >= 0
    same_proof = query_seg[:, None] == key_seg[None, :]
    return before & inside & present & same_proof


def block_grads(q_block, k_block, v_block, g_block, pair_mask, score_scale):
    scores = (
        jnp.einsum("qkgd,lkd->kgql", q_block, k_block, preferred_element_type=jnp.float32)
        * score_scale
    )
    scores = jnp.where(pair_mask, scores, -1e30)
    row_max = jnp.max(scores, axis=-1, keepdims=True)
    weights_exp = jnp.where(pair_mask, jnp.exp(scores - row_max), 0.0)
    probs_full = weights_exp / jnp.sum(weights_exp, axis=-1, keepdims=True)
    probs_low = probs_full.astype(jnp.bfloat16)
    attn_out = jnp.einsum("kgql,lkd->qkgd", probs_low, v_block, preferred_element_type=jnp.float32)
    row_delta = jnp.einsum("qkgd,qkgd->kgq", g_block.astype(jnp.float32), attn_out)
    prob_grad = jnp.einsum("qkgd,lkd->kgql", g_block, v_block, preferred_element_type=jnp.float32)
    score_low = (probs_full * (prob_grad - row_delta[..., None])).astype(jnp.bfloat16)
    query_grad = (
        score_scale
        * jnp.einsum("kgql,lkd->qkgd", score_low, k_block, preferred_element_type=jnp.float32)
    ).astype(jnp.bfloat16)
    key_grad = score_scale * jnp.einsum(
        "kgql,qkgd->lkd", score_low, q_block, preferred_element_type=jnp.float32
    )
    value_grad = jnp.einsum(
        "kgql,qkgd->lkd", probs_low, g_block, preferred_element_type=jnp.float32
    )
    return (query_grad, key_grad, value_grad)


def input_product(layer_input, grads):
    return lax.dot_general(
        layer_input, grads, (((0,), (0,)), ((), ())), preferred_element_type=jnp.float32
    )


def transposed(left, right):
    return lax.dot_general(
        left, right, (((1,), (1,)), ((), ())), preferred_element_type=jnp.float32
    )


def on_device(layer_input, query, keys, values, out_grad, w_query, w_key, w_value, proof_lengths):
    row_count = query.shape[0]
    key_cols = keys.shape[1]
    query_cols = query.shape[1]
    kv_local = key_cols // HD
    groups = query_cols // key_cols
    score_scale = (D // H) ** (-0.5)
    halo_rows = min(row_count, WINDOW)
    halo_depth = max(WINDOW // row_count, 1)
    first_row = lax.axis_index("seq") * row_count
    edge_pair = jnp.stack([keys, values])
    arrived_blocks = []
    moving = edge_pair
    for hop_index in range(halo_depth):
        moving = shifted(moving, "seq", 1)
        arrived_blocks.insert(0, moving)
    ext_keys = jnp.concatenate([member[0] for member in arrived_blocks] + [keys], axis=0)
    ext_values = jnp.concatenate([member[1] for member in arrived_blocks] + [values], axis=0)
    query_pos = first_row + jnp.arange(row_count, dtype=jnp.int32)
    key_pos = first_row - WINDOW + jnp.arange(WINDOW + row_count, dtype=jnp.int32)
    query_seg = proof_index(query_pos, proof_lengths)
    key_seg = proof_index(key_pos, proof_lengths)
    block_rows = min(row_count, 512)
    span_rows = block_rows + WINDOW
    key_acc = jnp.zeros((WINDOW + row_count, kv_local, HD), jnp.float32)
    value_acc = jnp.zeros((WINDOW + row_count, kv_local, HD), jnp.float32)
    q_block = query.reshape(block_rows, kv_local, groups, HD)
    g_block = out_grad.reshape(block_rows, kv_local, groups, HD)
    k_block = ext_keys.reshape(span_rows, kv_local, HD)
    v_block = ext_values.reshape(span_rows, kv_local, HD)
    pair_mask = build_mask(query_pos, key_pos, query_seg, key_seg)
    q_grad, k_grad, v_grad = block_grads(q_block, k_block, v_block, g_block, pair_mask, score_scale)
    key_acc = key_acc.at[0:span_rows].add(k_grad)
    value_acc = value_acc.at[0:span_rows].add(v_grad)
    query_parts = q_grad.reshape(block_rows, query_cols)
    key_acc = key_acc.reshape(WINDOW + row_count, key_cols)
    value_acc = value_acc.reshape(WINDOW + row_count, key_cols)

    def halo_piece(distance):
        offset = (halo_depth - distance) * halo_rows
        return jnp.stack(
            [key_acc[offset : offset + halo_rows], value_acc[offset : offset + halo_rows]]
        )

    carried = halo_piece(halo_depth)
    for distance in range(halo_depth - 1, -1, -1):
        carried = shifted(carried.astype(jnp.bfloat16), "seq", -1).astype(carried.dtype)
        if distance > 0:
            carried = carried + halo_piece(distance)
    tail_start = row_count - halo_rows
    key_total = key_acc[WINDOW:].at[tail_start:].add(carried[0])
    value_total = value_acc[WINDOW:].at[tail_start:].add(carried[1])
    key_grad = key_total.astype(jnp.bfloat16)
    value_grad = value_total.astype(jnp.bfloat16)
    head_term = (
        transposed(query_parts, w_query)
        + transposed(key_grad, w_key)
        + transposed(value_grad, w_value)
    )
    input_grad = lax.psum_scatter(
        head_term.astype(jnp.bfloat16), "head", scatter_dimension=1, tiled=True
    )
    all_grads = jnp.concatenate([query_parts, key_grad, value_grad], axis=1)
    summed = lax.psum_scatter(
        input_product(layer_input, all_grads).astype(jnp.bfloat16),
        "seq",
        scatter_dimension=0,
        tiled=True,
    )
    wq_grad = summed[:, :query_cols]
    wk_grad = summed[:, query_cols : query_cols + key_cols]
    wv_grad = summed[:, query_cols + key_cols :]
    return (input_grad, wq_grad, wk_grad, wv_grad)


def solution(mesh):
    return jax.shard_map(
        on_device,
        mesh=mesh,
        in_specs=(
            P("seq", None),
            P("seq", "head"),
            P("seq", "head"),
            P("seq", "head"),
            P("seq", "head"),
            P(None, "head"),
            P(None, "head"),
            P(None, "head"),
            P(),
        ),
        out_specs=(P("seq", "head"), P("seq", "head"), P("seq", "head"), P("seq", "head")),
        check_vma=False,
    )
```

profile of v0, /device:TPU:0, one launch (start us, length us, event | category | flops | bytes accessed | tf_op | source)
XLA Modules:
  0.0 467.3 jit_solution(3555738074250478057)
XLA Ops:
  7.2 1.3 copy.68
  8.6 1.3 copy.69
  9.8 0.1 pad_maximum_fusion
  9.9 3.3 collective-permute-start
  13.3 0.2 reduce-window.9
  13.7 1.0 collective-permute-done
  14.7 14.9 %collective-permute-start.1 = (bf16[2,512,512]{1,2,0:T(8,128)(2,1)}, bf16[2,512,512]{1,2,0:T(8,128)(2,1)}, u32[]{:S(2)}, u32[]{:S(2)}) collective-permute-start(bf16[2,512,512]{1,2,0:T(8,128)(2,1)} %collective-permute-done), channel_id=1, source_target_pairs={{0,4},{4,8},{8,12},{12,16},{16,20},{20,24},{24,28},{1,5},{5,9},{9,... | collective-permute-start | bytes 3145736 | tf_op jit(solution)/shard_map/ppermute | solution.py:15
  29.6 1.0 copy.73
  30.6 1.0 copy.78
  31.6 0.7 reshape.218
  32.3 2.5 copy.87
  34.8 0.5 copy.117
  35.4 2.5 fusion.15
  37.9 1.3 fusion.40
  39.2 1.0 copy.77
  40.2 1.0 copy.72
  41.2 1.3 fusion.39
  42.6 1.0 copy.76
  43.6 0.3 copy.71
  43.9 16.9 %fusion.41 = (f32[4,2,512]{2,1,0:T(2,128)S(1)}, f32[4,2,512,1536]{2,3,1,0:T(8,128)}) fusion(pred[512,1536]{0,1:T(8,128)(4,1)S(1)} %copy-done.7, bf16[512,4,2,128]{0,3,2,1:T(8,128)(2,1)S(1)} %bitcast.114, bf16[512,4,128]{2,0,1:T(8,128)(2,1)} %copy.73, bf16[512,4,128]{2,0,1:T(8,128)(2,1)S(1)} %copy-done.9, bf16[512,4,128]{2,0,1:T(8,128)(2,1)S(1)} %copy.71), kind=kOutput, calls=%fused_computation.68 | convolution fusion | flops 1646790144 | bytes 28590080 | tf_op jit(solution)/shard_map/sub | solution.py:40
  60.8 14.3 %fusion.8 = bf16[4,2,512,1536]{2,3,1,0:T(8,128)(2,1)} fusion(f32[4,2,512,1536]{2,3,1,0:T(8,128)} %get-tuple-element.113, f32[4,2,512]{2,1,0:T(2,128)S(1)} %get-tuple-element.112), kind=kLoop, calls=%fused_computation.14 | loop fusion | flops 12582912 | bytes 37765120 | tf_op jit(solution)/shard_map/convert_element_type | solution.py:42
  75.1 8.9 %convolution_bitcast_fusion = f32[1536,4,128]{0,2,1:T(8,128)S(1)} fusion(bf16[4,2,512,1536]{2,3,1,0:T(8,128)(2,1)} %fusion.8, bf16[512,4,2,128]{0,3,2,1:T(8,128)(2,1)} %copy.87), kind=kOutput, calls=%fused_computation.16 | convolution fusion | flops 1610612736 | bytes 16777216 | tf_op jit(solution)/shard_map/kgql,qkgd->lkd/dot_general | solution.py:54
  84.0 8.3 %convolution_bitcast_fusion.2 = f32[4,2,512,128]{2,3,1,0:T(8,128)} fusion(bf16[4,2,512,1536]{2,3,1,0:T(8,128)(2,1)} %fusion.8, bf16[512,4,128]{2,0,1:T(8,128)(2,1)} %copy.78, bf16[512,4,128]{2,0,1:T(8,128)(2,1)} %copy.77, bf16[512,4,128]{2,0,1:T(8,128)(2,1)} %copy.76), kind=kOutput, calls=%fused_computation.33 | convolution fusion | flops 1615331328 | bytes 16252928 | tf_op jit(solution)/shard_map/kgql,lkd->qkgd/dot_general | solution.py:43
  92.3 4.1 copy.100
  96.4 5.4 %multiply_reduce_fusion = f32[4,2,512]{1,0,2:T(4,128)} fusion(f32[4,2,512,128]{3,1,0,2:T(2,128)} %copy.100, bf16[512,4,2,128]{3,2,1,0:T(2,128)(2,1)} %copy-done.2), kind=kLoop, calls=%fused_computation.31 | loop fusion | flops 1568768 | bytes 3162112
  101.8 1.6 copy.101
  103.4 15.5 %fusion.2 = bf16[4,2,512,1536]{2,3,1,0:T(8,128)(2,1)} fusion(bf16[512,4,2,128]{0,3,2,1:T(8,128)(2,1)} %copy.87, f32[4,2,512]{2,1,0:T(2,128)S(1)} %copy.101, f32[4,2,512,1536]{2,3,1,0:T(8,128)} %get-tuple-element.113, f32[4,2,512]{2,1,0:T(2,128)S(1)} %get-tuple-element.112, bf16[512,4,128]{2,0,1:T(8,128)(2,1)} %copy.78, bf16[512,4,128]{2,0,1:T(8,128)(2,1)} %copy.77, ...), kind=kOutput, calls=%fused_computation.3 | convolution fusion | flops 1640497152 | bytes 40402944 | tf_op jit(solution)/shard_map/qkgd,lkd->kgql/dot_general | solution.py:45
  118.9 10.6 %fusion.12 = f32[1536,4,128]{0,2,1:T(8,128)} fusion(bf16[4,2,512,1536]{2,3,1,0:T(8,128)(2,1)} %fusion.2, bf16[512,4,2,128]{0,3,2,1:T(8,128)(2,1)} %bitcast.115), kind=kOutput, calls=%fused_computation.19 | convolution fusion | flops 1611399168 | bytes 16777216 | tf_op jit(solution)/shard_map/kgql,qkgd->lkd/dot_general | solution.py:51
  129.5 1.4 slice.170
  131.1 1.6 collective-permute-start.2
  132.8 0.5 fusion.36
  133.3 3.9 collective-permute-done.2
  137.1 0.3 fusion.16
  137.5 1.3 collective-permute-start.3
  138.8 3.0 multiply_convert_fusion
  141.8 12.5 %collective-permute-done.3 = bf16[2,512,512]{1,2,0:T(8,128)(2,1)S(1)} collective-permute-done((bf16[2,512,512]{1,2,0:T(8,128)(2,1)S(1)}, bf16[2,512,512]{1,2,0:T(8,128)(2,1)S(1)}, u32[]{:S(2)}, u32[]{:S(2)}) %collective-permute-start.3) | collective-permute-done | bytes 1048608 | tf_op jit(solution)/shard_map/ppermute | solution.py:15
  154.3 0.3 convert_element_type.52
  154.6 0.6 fusion.23
  155.2 20.0 %fusion.4 = bf16[5376,2048]{0,1:T(8,128)(2,1)} fusion(bf16[512,5376]{1,0:T(8,128)(2,1)} %param.25, bf16[512,512]{0,1:T(8,128)(2,1)S(1)} %get-tuple-element.106, bf16[512,512]{0,1:T(8,128)(2,1)S(1)} %get-tuple-element.107, bf16[512,1024]{0,1:T(8,128)(2,1)S(1)} %bitcast.125), kind=kOutput, calls=%fused_computation.8 | convolution fusion | flops 11291590656 | bytes 29622272 | tf_op jit(solution)/shard_map/dot_general | solution.py:61
  175.1 28.4 %copy.112 = bf16[5376,2048]{1,0:T(8,128)(2,1)} copy(bf16[5376,2048]{0,1:T(8,128)(2,1)} %fusion.4) | data formatting | bytes 44040192
  203.5 0.3 reduce-scatter.5.cloned.1.call-start
  203.8 12.7 %fusion.42 = f32[512,5376]{0,1:T(8,128)} fusion(bf16[5376,1024]{1,0:T(8,128)(2,1)} %param.30, bf16[512,1024]{0,1:T(8,128)(2,1)S(1)} %bitcast.126), kind=kOutput, calls=%fused_computation.69 | convolution fusion | flops 5637144576 | bytes 23068672 | tf_op jit(solution)/shard_map/dot_general | solution.py:67
  216.5 8.6 %fusion.43 = f32[512,5376]{0,1:T(8,128)} fusion(bf16[5376,512]{1,0:T(8,128)(2,1)} %param.31, bf16[512,512]{0,1:T(8,128)(2,1)S(1)} %get-tuple-element.107), kind=kOutput, calls=%fused_computation.70 | convolution fusion | flops 2818572288 | bytes 17039360 | tf_op jit(solution)/shard_map/dot_general | solution.py:67
  225.1 19.2 %add_convert_fusion = bf16[512,5376]{0,1:T(8,128)(2,1)} fusion(f32[512,5376]{0,1:T(8,128)} %fusion.42, f32[512,5376]{0,1:T(8,128)} %fusion.43, bf16[5376,512]{1,0:T(8,128)(2,1)} %param.32, bf16[512,512]{0,1:T(8,128)(2,1)S(1)} %get-tuple-element.106), kind=kOutput, calls=%fused_computation.13 | convolution fusion | flops 2826829824 | bytes 33554432 | tf_op jit(solution)/shard_map/dot_general | solution.py:67
  244.4 114.7 %reduce-scatter.7.cloned.1.call-done = bf16[672,2048]{1,0:T(8,128)(2,1)} async-done(((bf16[5376,2048]{1,0:T(8,128)(2,1)}), bf16[672,2048]{1,0:T(8,128)(2,1)}) %reduce-scatter.7.cloned.1.call-update) | async-done | bytes 2752528
  359.1 2.7 slice.154
  361.7 1.2 fusion.38
  362.9 97.1 %reduce-scatter.5.cloned.1.call-done = bf16[512,1344]{0,1:T(8,128)(2,1)} async-done(((bf16[512,5376]{0,1:T(8,128)(2,1)}), bf16[512,1344]{0,1:T(8,128)(2,1)}) %reduce-scatter.5.cloned.1.call-update) | async-done | bytes 1376272 | tf_op jit(solution)/shard_map/reduce_scatter | solution.py:131
  (40 shorter events, 0.5 us)
Async XLA Ops:
  7.2 6.1 %copy-start.12 = (s32[8]{0:T(128)S(1)}, s32[8]{0:T(128)}, u32[]{:S(2)}) copy-start(s32[8]{0:T(128)} %param.33) | copy-start | bytes 100
  7.2 24.4 %copy-start.5 = (bf16[512,1024]{1,0:T(8,128)(2,1)S(1)}, bf16[512,1024]{1,0:T(8,128)(2,1)}, u32[]{:S(2)}) copy-start(bf16[512,1024]{1,0:T(8,128)(2,1)} %param.29) | copy-start | bytes 3145732
  7.2 351.9 %reduce-scatter.7.cloned.1.call-start = ((), (), s32[]{:S(2)}) async-start(), calls=%async_computation.3 | async-start | bytes 24772608
  9.9 4.8 %collective-permute-start = (bf16[2,512,512]{1,2,0:T(8,128)(2,1)S(1)}, bf16[2,512,512]{1,2,0:T(8,128)(2,1)}, u32[]{:S(2)}, u32[]{:S(2)}) collective-permute-start(bf16[2,512,512]{1,2,0:T(8,128)(2,1)S(1)} %pad_maximum_fusion), channel_id=1, source_target_pairs={{0,4},{4,8},{8,12},{12,16},{16,20},{20,24},{24,28},{1,5},{5,9},{9,... | collective-permute-start | bytes 3145736 | tf_op jit(solution)/shard_map/ppermute | solution.py:15
  14.7 26.5 %collective-permute-start.1 = (bf16[2,512,512]{1,2,0:T(8,128)(2,1)}, bf16[2,512,512]{1,2,0:T(8,128)(2,1)}, u32[]{:S(2)}, u32[]{:S(2)}) collective-permute-start(bf16[2,512,512]{1,2,0:T(8,128)(2,1)} %collective-permute-done), channel_id=1, source_target_pairs={{0,4},{4,8},{8,12},{12,16},{16,20},{20,24},{24,28},{1,5},{5,9},{9,... | collective-permute-start | bytes 3145736 | tf_op jit(solution)/shard_map/ppermute | solution.py:15
  29.6 5.3 %copy-start.6 = (bf16[512,1024]{1,0:T(8,128)(2,1)S(1)}, bf16[512,1024]{1,0:T(8,128)(2,1)}, u32[]{:S(2)}) copy-start(bf16[512,1024]{1,0:T(8,128)(2,1)} %param.26) | copy-start | bytes 3145732
  32.3 6.9 %copy-start.2 = (bf16[512,4,2,128]{3,2,1,0:T(2,128)(2,1)}, bf16[512,4,2,128]{3,2,1,0:T(2,128)(2,1)S(1)}, u32[]{:S(2)}) copy-start(bf16[512,4,2,128]{3,2,1,0:T(2,128)(2,1)S(1)} %reshape.218) | copy-start | bytes 3145732
  35.4 8.5 %copy-start.3 = (bf16[512,1024]{0,1:T(8,128)(2,1)}, bf16[512,1024]{0,1:T(8,128)(2,1)S(1)}, u32[]{:S(2)}) copy-start(bf16[512,1024]{0,1:T(8,128)(2,1)S(1)} %copy.117) | copy-start | bytes 3145732
  40.2 3.6 copy-start.7
  41.2 2.6 copy-start.9
  43.9 16.9 %copy-start.11 = (bf16[512,4,128]{2,0,1:T(8,128)(2,1)}, bf16[512,4,128]{2,0,1:T(8,128)(2,1)S(1)}, u32[]{:S(2)}) copy-start(bf16[512,4,128]{2,0,1:T(8,128)(2,1)S(1)} %copy.71) | copy-start | bytes 1572868
  129.5 3.3 copy-start.1
  131.0 7.8 %copy-start.8 = (bf16[512,4,128]{2,0,1:T(8,128)(2,1)S(1)}, bf16[512,4,128]{2,0,1:T(8,128)(2,1)}, u32[]{:S(2)}) copy-start(bf16[512,4,128]{2,0,1:T(8,128)(2,1)} %copy.73) | copy-start | bytes 1572868
  131.0 7.8 %copy-start.10 = (bf16[512,4,128]{2,0,1:T(8,128)(2,1)S(1)}, bf16[512,4,128]{2,0,1:T(8,128)(2,1)}, u32[]{:S(2)}) copy-start(bf16[512,4,128]{2,0,1:T(8,128)(2,1)} %copy.72) | copy-start | bytes 1572868
  131.1 6.0 %collective-permute-start.2 = (bf16[2,512,512]{1,2,0:T(8,128)(2,1)S(1)}, bf16[2,512,512]{1,2,0:T(8,128)(2,1)S(1)}, u32[]{:S(2)}, u32[]{:S(2)}) collective-permute-start(bf16[2,512,512]{1,2,0:T(8,128)(2,1)S(1)} %pad_maximum_fusion.1), channel_id=1, source_target_pairs={{4,0},{8,4},{12,8},{16,12},{20,16},{24,20},{28,24},{5,1},{9,5},{13... | collective-permute-start | bytes 3145736 | tf_op jit(solution)/shard_map/ppermute | solution.py:15
  132.8 6.0 %copy-start = (bf16[4,2,512,1536]{2,3,1,0:T(8,128)(2,1)S(1)}, bf16[4,2,512,1536]{2,3,1,0:T(8,128)(2,1)}, u32[]{:S(2)}) copy-start(bf16[4,2,512,1536]{2,3,1,0:T(8,128)(2,1)} %fusion.2) | copy-start | bytes 37748740
  137.5 16.9 %collective-permute-start.3 = (bf16[2,512,512]{1,2,0:T(8,128)(2,1)S(1)}, bf16[2,512,512]{1,2,0:T(8,128)(2,1)S(1)}, u32[]{:S(2)}, u32[]{:S(2)}) collective-permute-start(bf16[2,512,512]{1,2,0:T(8,128)(2,1)S(1)} %fusion.16), channel_id=1, source_target_pairs={{4,0},{8,4},{12,8},{16,12},{20,16},{24,20},{28,24},{5,1},{9,5},{13... | collective-permute-start | bytes 3145736 | tf_op jit(solution)/shard_map/ppermute | solution.py:15
  203.5 256.4 %reduce-scatter.5.cloned.1.call-start = ((), (), s32[]{:S(2)}) async-start(), calls=%async_computation.2 | async-start | bytes 6881280 | tf_op jit(solution)/shard_map/reduce_scatter | solution.py:131
  359.1 2.7 copy-start.4
Sparse Core Ops, SparseCore 0:
  203.7 155.3 reduce-scatter.6
  361.9 97.9 reduce-scatter.4
where the time goes:
time: 476 us; the launch traced here: 467 us
  waiting for transfers between devices  229 us (48%)
  matrix products  124 us (26%)
  local copies, waits for them, and re-layouts  54.2 us (11%)
  other arithmetic  24 us (5%)
  starting transfers between devices  21.4 us (4%)
  between operations  14.8 us (3%)
    unnamed x3, waiting for transfers between devices  115 us
    reduce_scatter x1, waiting for transfers between devices, on_device(): lax.psum_scatter(head_term.astype(jnp.bfloat16), 'head', scatter_dimensio...  97.1 us
    dot_general x3, matrix products, transposed(): lax.dot_general(left, right, (((1,), (1,)), ((), ())), preferred_element_...  40.5 us
    unnamed x30, local copies, waits for them, and re-layouts  35.1 us
    ppermute x4, starting transfers between devices, shifted(): return lax.ppermute(block, axis, route)  21.1 us
    dot_general x1, matrix products, input_product(): lax.dot_general(layer_input, grads, (((0,), (0,)), ((), ())), preferred_e...  20 us
    ppermute x4, waiting for transfers between devices, shifted(): return lax.ppermute(block, axis, route)  17.4 us
    sub x1, matrix products, block_grads(): weights_exp = jnp.where(pair_mask, jnp.exp(scores - row_max), 0.0)  16.9 us
  transfers between devices with their start and end apart: 6, of which 5 were waited for; matrix products, arithmetic and copies ran while one was open for 13% of the time, Pallas kernels for 0%

commit v1 on v0

v1 whole, which is shorter than its diff:
```python
import functools
import math

import jax
import jax.numpy as jnp
from jax import lax
from jax.experimental import pallas as pl
from jax.experimental.pallas import tpu as pltpu
from jax.sharding import PartitionSpec as P

D = 5376
H = 32
HD = 128
WINDOW = 1024
TILE = 256
SCALE = (D // H) ** (-0.5)
FAR = -1e30
VMEM_BYTES = 56 * 1024 * 1024

NT = (((1,), (1,)), ((), ()))
TN = (((0,), (0,)), ((), ()))


def dot(left, right, dims=(((1,), (0,)), ((), ()))):
    return lax.dot_general(left, right, dims, preferred_element_type=jnp.float32)


def attention_kernel(groups, depth, lowest_ref, q_ref, g_ref, *refs):
    pieces = refs[: depth + 1]
    dq_ref = refs[depth + 1]
    halo_refs = refs[depth + 2 : 2 * depth + 2]
    own_ref = refs[2 * depth + 2]
    score_scr, pgrad_scr, dk_scr, dv_scr = refs[2 * depth + 3 :]
    rows = q_ref.shape[0]
    per_piece = rows // TILE
    behind = WINDOW // TILE
    lanes = groups * TILE

    def key_tile(e, which):
        start = (e % per_piece) * TILE
        return pieces[e // per_piece][which, start : start + TILE, :]

    key_iota = lax.broadcasted_iota(jnp.int32, (TILE, 1), 0)
    query_iota = lax.broadcasted_iota(jnp.int32, (1, TILE), 1)
    query_iota = jnp.concatenate([query_iota] * groups, axis=1)
    for t in range(per_piece):
        here = slice(t * TILE, (t + 1) * TILE)
        score_ref = score_scr.at[t % 2]
        pgrad_ref = pgrad_scr.at[t % 2]
        q2 = jnp.concatenate([q_ref[here, j * HD : (j + 1) * HD] for j in range(groups)], axis=0)
        g2 = jnp.concatenate([g_ref[here, j * HD : (j + 1) * HD] for j in range(groups)], axis=0)
        lowest = jnp.concatenate([lowest_ref[:, here]] * groups, axis=1)
        top = jnp.full((1, lanes), FAR, jnp.float32)
        for b in range(behind + 1):
            s = dot(key_tile(t + b, 0), q2, NT)
            allowed = key_iota + (t + b) * TILE >= lowest
            if b == behind:
                allowed = allowed & (key_iota <= query_iota)
            s = jnp.where(allowed, s, FAR)
            score_ref[b * TILE : (b + 1) * TILE, :] = s
            top = jnp.maximum(top, jnp.max(s, axis=0, keepdims=True))
        factor = SCALE * math.log2(math.e)
        total = jnp.zeros((1, lanes), jnp.float32)
        delta = jnp.zeros((1, lanes), jnp.float32)
        for b in range(behind + 1):
            at = slice(b * TILE, (b + 1) * TILE)
            weight = jnp.exp2((score_ref[at, :] - top) * factor)
            pgrad = dot(key_tile(t + b, 1), g2, NT)
            score_ref[at, :] = weight
            pgrad_ref[at, :] = pgrad
            total = total + jnp.sum(weight, axis=0, keepdims=True)
            delta = delta + jnp.sum(weight * pgrad, axis=0, keepdims=True)
        inverse = 1.0 / total
        delta = delta * inverse
        dq = jnp.zeros((HD, lanes), jnp.float32)
        for b in range(behind + 1):
            at = slice(b * TILE, (b + 1) * TILE)
            e = t + b
            to = slice(e * TILE, (e + 1) * TILE)
            prob = score_ref[at, :] * inverse
            sgrad = (prob * (pgrad_ref[at, :] - delta)).astype(jnp.bfloat16)
            dv = dot(prob.astype(jnp.bfloat16), g2)
            dk = dot(sgrad, q2)
            if t == 0 or b == behind:
                dv_scr[to, :] = dv
                dk_scr[to, :] = dk
            else:
                dv_scr[to, :] += dv
                dk_scr[to, :] += dk
            dq = dq + dot(key_tile(e, 0), sgrad, TN)
        dq = (dq * SCALE).T.astype(jnp.bfloat16)
        for j in range(groups):
            dq_ref[here, j * HD : (j + 1) * HD] = dq[j * TILE : (j + 1) * TILE, :]
    for d in range(depth):
        at = slice(d * rows, (d + 1) * rows)
        halo_refs[d][0] = (dk_scr[at, :] * SCALE).astype(jnp.bfloat16)
        halo_refs[d][1] = dv_scr[at, :].astype(jnp.bfloat16)
    own_ref[0] = dk_scr[depth * rows :, :] * SCALE
    own_ref[1] = dv_scr[depth * rows :, :]


def attention(lowest, query, out_grad, pieces, first, groups):
    rows = query.shape[0]
    depth = len(pieces) - 1
    heads = pieces[0].shape[2] // HD
    wide = groups * HD
    query_spec = pl.BlockSpec((rows, wide), lambda h: (0, h + first))
    pair_spec = pl.BlockSpec((2, rows, HD), lambda h: (0, 0, h))
    span = WINDOW + TILE
    pair = jax.ShapeDtypeStruct((2, rows, heads * HD), jnp.bfloat16)
    pairs_seen = heads * groups * rows * span
    return pl.pallas_call(
        functools.partial(attention_kernel, groups, depth),
        grid=(heads,),
        in_specs=[pl.BlockSpec((1, rows), lambda h: (0, 0)), query_spec, query_spec]
        + [pair_spec] * (depth + 1),
        out_specs=[pl.BlockSpec((rows, wide), lambda h: (0, h))] + [pair_spec] * (depth + 1),
        out_shape=[jax.ShapeDtypeStruct((rows, heads * wide), jnp.bfloat16)]
        + [pair] * depth
        + [jax.ShapeDtypeStruct(pair.shape, jnp.float32)],
        scratch_shapes=[
            pltpu.VMEM((2, span, groups * TILE), jnp.float32),
            pltpu.VMEM((2, span, groups * TILE), jnp.float32),
            pltpu.VMEM((WINDOW + rows, HD), jnp.float32),
            pltpu.VMEM((WINDOW + rows, HD), jnp.float32),
        ],
        compiler_params=pltpu.CompilerParams(vmem_limit_bytes=VMEM_BYTES),
        cost_estimate=pl.CostEstimate(
            flops=10 * pairs_seen * HD * 2,
            bytes_accessed=2 * rows * heads * HD * 20,
            transcendentals=pairs_seen,
        ),
        name="attention_grads",
    )(lowest, query, out_grad, *pieces)


def term_kernel(dq_ref, dk_ref, dv_ref, wq_ref, wk_ref, wv_ref, out_ref):
    out_ref[0] = (
        dot(dq_ref[...], wq_ref[...], NT)
        + dot(dk_ref[...], wk_ref[...], NT)
        + dot(dv_ref[...], wv_ref[...], NT)
    ).astype(jnp.bfloat16)


def input_term(dq, dk, dv, w_query, w_key, w_value, parts):
    rows = dq.shape[0]
    width = w_query.shape[0] // parts
    grads = [pl.BlockSpec(a.shape, lambda p: (0, 0)) for a in (dq, dk, dv)]
    weights = [pl.BlockSpec((width, w.shape[1]), lambda p: (p, 0)) for w in (w_query, w_key, w_value)]
    depth = dq.shape[1] + dk.shape[1] + dv.shape[1]
    return pl.pallas_call(
        term_kernel,
        grid=(parts,),
        in_specs=grads + weights,
        out_specs=pl.BlockSpec((1, rows, width), lambda p: (p, 0, 0)),
        out_shape=jax.ShapeDtypeStruct((parts, rows, width), jnp.bfloat16),
        compiler_params=pltpu.CompilerParams(vmem_limit_bytes=VMEM_BYTES),
        cost_estimate=pl.CostEstimate(
            flops=2 * rows * width * parts * depth,
            bytes_accessed=2 * (width * parts * (depth + rows) + rows * depth),
            transcendentals=0,
        ),
        name="input_term",
    )(dq, dk, dv, w_query, w_key, w_value)


def swapped(block, bit):
    size = lax.axis_size("seq")
    return lax.ppermute(block, "seq", [(i, i ^ bit) for i in range(size)])


def shifted(block, distance):
    size = lax.axis_size("seq")
    return lax.ppermute(
        block, "seq", [(i, i + distance) for i in range(size) if 0 <= i + distance < size]
    )


def earlier_pieces(own, odd):
    two_back = shifted(own, 2)
    one_back = swapped(jnp.where(odd, two_back, own), 1)
    return two_back, one_back


def returned(two_back, one_back, own, odd):
    beside = swapped(one_back, 1)
    both = two_back.astype(jnp.float32) + jnp.where(odd, beside.astype(jnp.float32), 0.0)
    later = shifted(both.astype(jnp.bfloat16), -2)
    total = own + later.astype(jnp.float32) + jnp.where(odd, 0.0, beside.astype(jnp.float32))
    return total.astype(jnp.bfloat16)


def scattered_product(rows_by_offset, grads, bits):
    size = len(rows_by_offset)
    arrived = {o: [] for o in range(size)}

    def summed(offset):
        value = dot(rows_by_offset[offset], grads)
        for other in arrived[offset]:
            value = value + other.astype(jnp.float32)
        return value.astype(jnp.bfloat16)

    alive = list(range(size))
    for bit in bits:
        leaving = [o for o in alive if o & bit]
        alive = [o for o in alive if not o & bit]
        for o in leaving:
            arrived[o ^ bit].append(swapped(summed(o), bit))
    return summed(0)


def on_device(layer_input, query, keys, values, out_grad, w_query, w_key, w_value, proof_lengths):
    rows = query.shape[0]
    key_cols = keys.shape[1]
    kv_local = key_cols // HD
    groups = query.shape[1] // key_cols
    seq_size = lax.axis_size("seq")
    head_size = lax.axis_size("head")
    me = lax.axis_index("seq")
    odd = me % 2 == 1
    first_row = me * rows

    positions = first_row + jnp.arange(rows, dtype=jnp.int32)
    starts = jnp.cumsum(proof_lengths) - proof_lengths
    begun = starts[:, None] <= positions[None, :]
    proof_start = jnp.max(jnp.where(begun, starts[:, None], 0), axis=0)
    lowest = jnp.maximum(proof_start, positions - (WINDOW - 1)) - first_row + WINDOW
    lowest = lowest.astype(jnp.int32)[None, :]

    sets = 2 if kv_local % 2 == 0 else 1
    per_set = kv_local // sets
    cols = per_set * HD
    dqs, dks, dvs = [], [], []
    stacked = []
    for c in range(sets):
        at = slice(c * cols, (c + 1) * cols)
        own = jnp.stack([keys[:, at], values[:, at]])
        stacked.append((earlier_pieces(own, odd), own))
    for c in range(sets):
        (two_back, one_back), own = stacked[c]
        dq, halo_two, halo_one, own_grad = attention(
            lowest, query, out_grad, [two_back, one_back, own], c * per_set, groups
        )
        total = returned(halo_two, halo_one, own_grad, odd)
        dqs.append(dq)
        dks.append(total[0])
        dvs.append(total[1])
    dq = jnp.concatenate(dqs, axis=1)
    dk = jnp.concatenate(dks, axis=1)
    dv = jnp.concatenate(dvs, axis=1)

    term = input_term(dq, dk, dv, w_query, w_key, w_value, head_size)
    input_grad = lax.psum_scatter(term, "head", scatter_dimension=0, tiled=False)

    block = layer_input.shape[1] // seq_size
    by_block = layer_input.T.reshape(seq_size, block, rows)
    order = me ^ jnp.arange(seq_size, dtype=jnp.int32)
    by_offset = [
        lax.dynamic_index_in_dim(by_block, order[o], 0, keepdims=False) for o in range(seq_size)
    ]
    bits = [1 << j for j in range(1, seq_size.bit_length() - 1)]
    forward = [1] + bits
    backward = [1] + bits[::-1]
    half = dq.shape[1] // 2
    wq_grad = jnp.concatenate(
        [
            scattered_product(by_offset, dq[:, :half], forward),
            scattered_product(by_offset, dq[:, half:], backward),
        ],
        axis=1,
    )
    wk_grad = scattered_product(by_offset, dk, forward)
    wv_grad = scattered_product(by_offset, dv, backward)
    return (input_grad, wq_grad, wk_grad, wv_grad)


def solution(mesh):
    return jax.shard_map(
        on_device,
        mesh=mesh,
        in_specs=(
            P("seq", None),
            P("seq", "head"),
            P("seq", "head"),
            P("seq", "head"),
            P("seq", "head"),
            P(None, "head"),
            P(None, "head"),
            P(None, "head"),
            P(),
        ),
        out_specs=(P("seq", "head"), P("seq", "head"), P("seq", "head"), P("seq", "head")),
        check_vma=False,
    )
```

time: 476 us -> 260 us (0.55); the launches traced: 467 us -> 259 us
  waiting for transfers between devices: 229 us -> 113 us
  matrix products: 124 us -> 20.7 us
  Pallas kernels: 0 us -> 43.3 us
  local copies, waits for them, and re-layouts: 54.2 us -> 14.3 us
  other arithmetic: 24 us -> 8.96 us
  between operations: 14.8 us -> 29.6 us
  starting transfers between devices: 21.4 us -> 30 us
    unnamed x3 -> x1, waiting for transfers between devices: 115 us -> 0.02 us
    reduce_scatter x1, waiting for transfers between devices: 97.1 us -> 0.01 us  [on_device(): lax.psum_scatter(term, 'head', scatter_dimension=0, tiled=False)]
    ppermute x4 -> x36, waiting for transfers between devices: 17.4 us -> 113 us  [the longest x32 71 us: swapped(): return lax.ppermute(block, 'seq', [(i, i ^ bit) for i in range(size)])]
    dot_general x9 -> x32, matrix products: 107 us -> 20.7 us  [dot(): lax.dot_general(left, right, dims, preferred_element_type=jnp.float32)]
    pallas_call x0 -> x3, Pallas kernels: none -> 43.3 us  [the longest x2 24.7 us: attention(): pl.pallas_call(functools.partial(attention_kernel, groups, depth), grid=(...]
    unnamed x30, local copies, waits for them, and re-layouts: 35.1 us -> 12.4 us
    sub x1 -> x0, matrix products: 16.9 us -> none  [block_grads(): weights_exp = jnp.where(pair_mask, jnp.exp(scores - row_max), 0.0)]
    convert_element_type x4 -> x8, other arithmetic: 15.5 us -> 3.81 us  [the longest x4 3.07 us: summed(): return value.astype(jnp.bfloat16)]
  transfers between devices with their start and end apart: 6 -> 37, of which waited for: 5 -> 13; matrix products, arithmetic and copies ran while one was open for 13% -> 14% of each run, Pallas kernels for 0% -> 10%
where the time goes in v1:
time: 260 us; the launch traced here: 259 us
  waiting for transfers between devices  113 us (43%)
  Pallas kernels  43.3 us (17%)
  starting transfers between devices  30 us (12%)
  between operations  29.6 us (11%)
  matrix products  20.7 us (8%)
  local copies, waits for them, and re-layouts  14.3 us (6%)
  other arithmetic  8.96 us (3%)
    ppermute x32, waiting for transfers between devices, swapped(): return lax.ppermute(block, 'seq', [(i, i ^ bit) for i in range(size)])  71 us
    ppermute x4, waiting for transfers between devices, shifted(): lax.ppermute(block, 'seq', [(i, i + distance) for i in range(size) if 0 <...  41.6 us
    pallas_call x2, Pallas kernels, attention(): pl.pallas_call(functools.partial(attention_kernel, groups, depth), grid=(...  24.7 us
    dot_general x32, matrix products, dot(): lax.dot_general(left, right, dims, preferred_element_type=jnp.float32)  20.7 us
    ppermute x32, starting transfers between devices, swapped(): return lax.ppermute(block, 'seq', [(i, i ^ bit) for i in range(size)])  18.7 us
    pallas_call x1, Pallas kernels, input_term(): pl.pallas_call(term_kernel, grid=(parts,), in_specs=grads + weights, out_...  18.6 us
    unnamed x30, local copies, waits for them, and re-layouts  12.4 us
    ppermute x4, starting transfers between devices, shifted(): lax.ppermute(block, 'seq', [(i, i + distance) for i in range(size) if 0 <...  11.2 us
  transfers between devices with their start and end apart: 37, of which 13 were waited for; matrix products, arithmetic and copies ran while one was open for 14% of the time, Pallas kernels for 10%

profile of v1, /device:TPU:0, one launch (start us, length us, event | category | flops | bytes accessed | tf_op | source)
XLA Modules:
  0.0 259.4 jit_solution(2643244234092547651)
XLA Ops:
  7.2 1.3 slice_bitcast_fusion.6
  8.6 4.9 %collective-permute-start = (bf16[2,512,256]{2,1,0:T(8,128)(2,1)S(1)}, bf16[2,512,256]{2,1,0:T(8,128)(2,1)S(1)}, u32[]{:S(2)}, u32[]{:S(2)}) collective-permute-start(bf16[2,512,256]{2,1,0:T(8,128)(2,1)S(1)} %pad_maximum_fusion.2.refs_2_), channel_id=1, source_target_pairs={{0,8},{4,12},{8,16},{12,20},{16,24},{20,28},{1,9},{5,13},{9,17},{1... | collective-permute-start | bytes 1572872 | tf_op jit(solution)/shard_map/ppermute | solution.py:174
  13.5 3.4 %collective-permute-start.2 = (bf16[2,512,256]{2,1,0:T(8,128)(2,1)S(1)}, bf16[2,512,256]{2,1,0:T(8,128)(2,1)S(1)}, u32[]{:S(2)}, u32[]{:S(2)}) collective-permute-start(bf16[2,512,256]{2,1,0:T(8,128)(2,1)S(1)} %pad_maximum_fusion.3.refs_2_), channel_id=1, source_target_pairs={{0,8},{4,12},{8,16},{12,20},{16,24},{20,28},{1,9},{5,13},{9,17},{1... | collective-permute-start | bytes 1572872 | tf_op jit(solution)/shard_map/ppermute | solution.py:174
  17.1 8.6 %collective-permute-done.refs_0_ = bf16[2,512,256]{2,1,0:T(8,128)(2,1)S(1)} collective-permute-done((bf16[2,512,256]{2,1,0:T(8,128)(2,1)S(1)}, bf16[2,512,256]{2,1,0:T(8,128)(2,1)S(1)}, u32[]{:S(2)}, u32[]{:S(2)}) %collective-permute-start) | collective-permute-done | bytes 524320 | tf_op jit(solution)/shard_map/ppermute | solution.py:174
  26.0 0.6 subtract_add_fusion.lowest_ref
  26.5 9.3 %collective-permute-done.2.refs_0_ = bf16[2,512,256]{2,1,0:T(8,128)(2,1)S(1)} collective-permute-done((bf16[2,512,256]{2,1,0:T(8,128)(2,1)S(1)}, bf16[2,512,256]{2,1,0:T(8,128)(2,1)S(1)}, u32[]{:S(2)}, u32[]{:S(2)}) %collective-permute-start.2) | collective-permute-done | bytes 524320 | tf_op jit(solution)/shard_map/ppermute | solution.py:174
  36.0 0.8 copy-done.12
  36.8 12.4 %attention_grads.2 = (bf16[512,512]{1,0:T(8,128)(2,1)}, bf16[2,512,256]{2,1,0:T(8,128)(2,1)}, bf16[2,512,256]{2,1,0:T(8,128)(2,1)}, f32[2,512,256]{2,1,0:T(8,128)}) custom-call(s32[1,512]{1,0:T(1,128)} %subtract_add_fusion.lowest_ref, bf16[512,1024]{1,0:T(8,128)(2,1)} %q_ref.3, bf16[512,1024]{1,0:T(8,128)(2,1)} %g_ref.3, bf16[2,512,256]{2,1,0:T(8,128)(2,1)} %copy-done.8, ...), custom_call_target="tpu_custom_call" | custom-call | flops 6710886400 | bytes 5242880 | tf_op jit(solution)/shard_map/attention_grads/pallas_call | solution.py:112
  49.7 0.8 copy-done.11
  50.5 12.3 %attention_grads.3 = (bf16[512,512]{1,0:T(8,128)(2,1)}, bf16[2,512,256]{2,1,0:T(8,128)(2,1)}, bf16[2,512,256]{2,1,0:T(8,128)(2,1)}, f32[2,512,256]{2,1,0:T(8,128)}) custom-call(s32[1,512]{1,0:T(1,128)} %subtract_add_fusion.lowest_ref, bf16[512,1024]{1,0:T(8,128)(2,1)} %q_ref.3, bf16[512,1024]{1,0:T(8,128)(2,1)} %g_ref.3, bf16[2,512,256]{2,1,0:T(8,128)(2,1)} %copy-done.6, ...), custom_call_target="tpu_custom_call" | custom-call | flops 6710886400 | bytes 5242880 | tf_op jit(solution)/shard_map/attention_grads/pallas_call | solution.py:112
  63.1 1.6 collective-permute-start.5
  64.8 1.1 pad_maximum_fusion.1.dq_ref
  66.1 1.3 collective-permute-start.7
  67.4 13.0 %collective-permute-done.5 = bf16[2,512,256]{2,1,0:T(8,128)(2,1)S(1)} collective-permute-done((bf16[2,512,256]{2,1,0:T(8,128)(2,1)S(1)}, bf16[2,512,256]{2,1,0:T(8,128)(2,1)S(1)}, u32[]{:S(2)}, u32[]{:S(2)}) %collective-permute-start.5) | collective-permute-done | bytes 524320 | tf_op jit(solution)/shard_map/ppermute | solution.py:174
  80.7 10.7 %collective-permute-done.7 = bf16[2,512,256]{2,1,0:T(8,128)(2,1)S(1)} collective-permute-done((bf16[2,512,256]{2,1,0:T(8,128)(2,1)S(1)}, bf16[2,512,256]{2,1,0:T(8,128)(2,1)S(1)}, u32[]{:S(2)}, u32[]{:S(2)}) %collective-permute-start.7) | collective-permute-done | bytes 524320 | tf_op jit(solution)/shard_map/ppermute | solution.py:174
  91.7 0.8 pad_maximum_fusion.5.dv_ref
  92.5 0.8 pad_maximum_fusion.4.dk_ref
  93.4 18.6 %input_term.1 = bf16[4,512,1344]{2,1,0:T(8,128)(2,1)} custom-call(bf16[512,1024]{1,0:T(8,128)(2,1)} %pad_maximum_fusion.1.dq_ref, bf16[512,512]{1,0:T(8,128)(2,1)} %pad_maximum_fusion.4.dk_ref, bf16[512,512]{1,0:T(8,128)(2,1)} %pad_maximum_fusion.5.dv_ref, bf16[5376,1024]{1,0:T(8,128)(2,1)} %wq_ref.1, bf16[5376,512]{1,0:T(8,128)(2,1)} %wk_ref.1, ...), custom_call_target="tpu_custom_call" | custom-call | flops 11274289152 | bytes 29622272 | tf_op jit(solution)/shard_map/input_term/pallas_call | solution.py:151
  112.0 0.6 fusion.134
  122.6 8.2 %copy.16 = bf16[512,5376]{0,1:T(8,128)(2,1)} copy(bf16[512,5376]{1,0:T(8,128)(2,1)} %param.9) | data formatting | bytes 11010048 | tf_op args[0]
  135.8 1.8 convolution_convert_fusion.12
  137.7 1.6 convolution_convert_fusion.13
  139.3 0.6 collective-permute-start.11
  139.9 1.6 convolution_convert_fusion.14
  146.6 2.8 %collective-permute-start.13 = (bf16[672,512]{1,0:T(8,128)(2,1)S(1)}, bf16[672,512]{1,0:T(8,128)(2,1)S(1)}, u32[]{:S(2)}, u32[]{:S(2)}) collective-permute-start(bf16[672,512]{1,0:T(8,128)(2,1)S(1)} %fusion.7), channel_id=1, source_target_pairs={{0,8},{4,12},{8,0},{12,4},{16,24},{20,28},{24,16},{28,20},{1,9},{5... | collective-permute-start | bytes 2064392 | tf_op jit(solution)/shard_map/ppermute | solution.py:169
  157.5 7.8 %collective-permute-done.13 = bf16[672,512]{1,0:T(8,128)(2,1)S(1)} collective-permute-done((bf16[672,512]{1,0:T(8,128)(2,1)S(1)}, bf16[672,512]{1,0:T(8,128)(2,1)S(1)}, u32[]{:S(2)}, u32[]{:S(2)}) %collective-permute-start.13) | collective-permute-done | bytes 688160 | tf_op jit(solution)/shard_map/ppermute | solution.py:169
  165.3 2.1 collective-permute-done.20
  167.4 0.6 fusion.12
  168.0 0.6 fusion.10
  170.1 1.7 collective-permute-start.14
  173.2 13.3 %collective-permute-done.10 = bf16[672,512]{1,0:T(8,128)(2,1)S(1)} collective-permute-done((bf16[672,512]{1,0:T(8,128)(2,1)S(1)}, bf16[672,512]{1,0:T(8,128)(2,1)S(1)}, u32[]{:S(2)}, u32[]{:S(2)}) %collective-permute-start.10) | collective-permute-done | bytes 688160 | tf_op jit(solution)/shard_map/ppermute | solution.py:169
  187.4 1.8 collective-permute-start.17
  189.2 13.9 %collective-permute-done.34 = bf16[672,512]{1,0:T(8,128)(2,1)S(1)} collective-permute-done((bf16[672,512]{1,0:T(8,128)(2,1)S(1)}, bf16[672,512]{1,0:T(8,128)(2,1)S(1)}, u32[]{:S(2)}, u32[]{:S(2)}) %collective-permute-start.34) | collective-permute-done | bytes 688160 | tf_op jit(solution)/shard_map/ppermute | solution.py:169
  203.1 1.7 collective-permute-start.21
  204.8 0.9 fusion.13
  206.3 1.8 collective-permute-start.35
  208.4 9.4 %collective-permute-done.17 = bf16[672,512]{1,0:T(8,128)(2,1)S(1)} collective-permute-done((bf16[672,512]{1,0:T(8,128)(2,1)S(1)}, bf16[672,512]{1,0:T(8,128)(2,1)S(1)}, u32[]{:S(2)}, u32[]{:S(2)}) %collective-permute-start.17) | collective-permute-done | bytes 688160 | tf_op jit(solution)/shard_map/ppermute | solution.py:169
  217.9 1.7 collective-permute-start.24
  219.6 1.9 collective-permute-done.21
  221.5 1.7 collective-permute-start.28
  223.2 0.7 fusion.11
  223.9 1.2 pad_maximum_fusion
  225.1 7.5 %collective-permute-done.31 = bf16[672,512]{1,0:T(8,128)(2,1)S(1)} collective-permute-done((bf16[672,512]{1,0:T(8,128)(2,1)S(1)}, bf16[672,512]{1,0:T(8,128)(2,1)S(1)}, u32[]{:S(2)}, u32[]{:S(2)}) %collective-permute-start.31) | collective-permute-done | bytes 688160 | tf_op jit(solution)/shard_map/ppermute | solution.py:169
  232.6 3.6 %collective-permute-done.35 = bf16[672,512]{1,0:T(8,128)(2,1)S(1)} collective-permute-done((bf16[672,512]{1,0:T(8,128)(2,1)S(1)}, bf16[672,512]{1,0:T(8,128)(2,1)S(1)}, u32[]{:S(2)}, u32[]{:S(2)}) %collective-permute-start.35) | collective-permute-done | bytes 688160 | tf_op jit(solution)/shard_map/ppermute | solution.py:169
  236.2 1.2 add_convert_fusion
  237.5 11.4 %collective-permute-done.24 = bf16[672,512]{1,0:T(8,128)(2,1)S(1)} collective-permute-done((bf16[672,512]{1,0:T(8,128)(2,1)S(1)}, bf16[672,512]{1,0:T(8,128)(2,1)S(1)}, u32[]{:S(2)}, u32[]{:S(2)}) %collective-permute-start.24) | collective-permute-done | bytes 688160 | tf_op jit(solution)/shard_map/ppermute | solution.py:169
  248.9 1.2 add_convert_fusion.4
  250.1 2.5 copy.17
  (118 shorter events, 20.0 us)
Async XLA Ops:
  7.2 243.0 %reduce-scatter.2.cloned.1.call-start = ((), (), s32[]{:S(2)}) async-start(), calls=%async_computation.1 | async-start | bytes 7208960 | tf_op jit(solution)/shard_map/reduce_scatter | solution.py:253
  8.5 8.5 %copy-start.13 = (s32[8]{0:T(128)S(1)}, s32[8]{0:T(128)}, u32[]{:S(2)}) copy-start(s32[8]{0:T(128)} %param.17) | copy-start | bytes 100
  8.5 27.3 %copy-start.7 = (bf16[2,512,256]{2,1,0:T(8,128)(2,1)}, bf16[2,512,256]{2,1,0:T(8,128)(2,1)S(1)}, u32[]{:S(2)}) copy-start(bf16[2,512,256]{2,1,0:T(8,128)(2,1)S(1)} %pad_maximum_fusion.2.refs_2_) | copy-start | bytes 1572868
  8.6 17.2 %collective-permute-start = (bf16[2,512,256]{2,1,0:T(8,128)(2,1)S(1)}, bf16[2,512,256]{2,1,0:T(8,128)(2,1)S(1)}, u32[]{:S(2)}, u32[]{:S(2)}) collective-permute-start(bf16[2,512,256]{2,1,0:T(8,128)(2,1)S(1)} %pad_maximum_fusion.2.refs_2_), channel_id=1, source_target_pairs={{0,8},{4,12},{8,16},{12,20},{16,24},{20,28},{1,9},{5,13},{9,17},{1... | collective-permute-start | bytes 1572872 | tf_op jit(solution)/shard_map/ppermute | solution.py:174
  13.5 22.4 %copy-start.5 = (bf16[2,512,256]{2,1,0:T(8,128)(2,1)}, bf16[2,512,256]{2,1,0:T(8,128)(2,1)S(1)}, u32[]{:S(2)}) copy-start(bf16[2,512,256]{2,1,0:T(8,128)(2,1)S(1)} %pad_maximum_fusion.3.refs_2_) | copy-start | bytes 1572868
  13.5 22.3 %collective-permute-start.2 = (bf16[2,512,256]{2,1,0:T(8,128)(2,1)S(1)}, bf16[2,512,256]{2,1,0:T(8,128)(2,1)S(1)}, u32[]{:S(2)}, u32[]{:S(2)}) collective-permute-start(bf16[2,512,256]{2,1,0:T(8,128)(2,1)S(1)} %pad_maximum_fusion.3.refs_2_), channel_id=1, source_target_pairs={{0,8},{4,12},{8,16},{12,20},{16,24},{20,28},{1,9},{5,13},{9,17},{1... | collective-permute-start | bytes 1572872 | tf_op jit(solution)/shard_map/ppermute | solution.py:174
  25.7 10.2 %copy-start.8 = (bf16[2,512,256]{2,1,0:T(8,128)(2,1)}, bf16[2,512,256]{2,1,0:T(8,128)(2,1)S(1)}, u32[]{:S(2)}) copy-start(bf16[2,512,256]{2,1,0:T(8,128)(2,1)S(1)} %collective-permute-done.refs_0_) | copy-start | bytes 1572868
  25.8 10.2 %collective-permute-start.1 = (bf16[2,512,256]{2,1,0:T(8,128)(2,1)S(1)}, bf16[2,512,256]{2,1,0:T(8,128)(2,1)S(1)}, u32[]{:S(2)}, u32[]{:S(2)}) collective-permute-start(bf16[2,512,256]{2,1,0:T(8,128)(2,1)S(1)} %broadcast_select_fusion.1), channel_id=1, source_target_pairs={{0,4},{4,0},{8,12},{12,8},{16,20},{20,16},{24,28},{28,24},{1,5},{5... | collective-permute-start | bytes 1572872 | tf_op jit(solution)/shard_map/ppermute | solution.py:169
  35.8 13.4 %copy-start.6 = (bf16[2,512,256]{2,1,0:T(8,128)(2,1)}, bf16[2,512,256]{2,1,0:T(8,128)(2,1)S(1)}, u32[]{:S(2)}) copy-start(bf16[2,512,256]{2,1,0:T(8,128)(2,1)S(1)} %collective-permute-done.2.refs_0_) | copy-start | bytes 1572868
  35.9 13.8 %collective-permute-start.3 = (bf16[2,512,256]{2,1,0:T(8,128)(2,1)S(1)}, bf16[2,512,256]{2,1,0:T(8,128)(2,1)S(1)}, u32[]{:S(2)}, u32[]{:S(2)}) collective-permute-start(bf16[2,512,256]{2,1,0:T(8,128)(2,1)S(1)} %broadcast_select_fusion), channel_id=1, source_target_pairs={{0,4},{4,0},{8,12},{12,8},{16,20},{20,16},{24,28},{28,24},{1,5},{5... | collective-permute-start | bytes 1572872 | tf_op jit(solution)/shard_map/ppermute | solution.py:169
  49.2 13.8 %copy-start.9 = (bf16[2,512,256]{2,1,0:T(8,128)(2,1)S(1)}, bf16[2,512,256]{2,1,0:T(8,128)(2,1)}, u32[]{:S(2)}) copy-start(bf16[2,512,256]{2,1,0:T(8,128)(2,1)} %get-tuple-element.15) | copy-start | bytes 1572868
  49.2 13.8 %collective-permute-start.4 = (bf16[2,512,256]{2,1,0:T(8,128)(2,1)}, bf16[2,512,256]{2,1,0:T(8,128)(2,1)S(1)}, u32[]{:S(2)}, u32[]{:S(2)}) collective-permute-start(bf16[2,512,256]{2,1,0:T(8,128)(2,1)} %get-tuple-element.16), channel_id=1, source_target_pairs={{0,4},{4,0},{8,12},{12,8},{16,20},{20,16},{24,28},{28,24},{1,5},{5... | collective-permute-start | bytes 1572872 | tf_op jit(solution)/shard_map/ppermute | solution.py:169
  62.8 1.9 copy-start.1
  62.9 3.1 %collective-permute-start.6 = (bf16[2,512,256]{2,1,0:T(8,128)(2,1)}, bf16[2,512,256]{2,1,0:T(8,128)(2,1)S(1)}, u32[]{:S(2)}, u32[]{:S(2)}) collective-permute-start(bf16[2,512,256]{2,1,0:T(8,128)(2,1)} %get-tuple-element.19), channel_id=1, source_target_pairs={{0,4},{4,0},{8,12},{12,8},{16,20},{20,16},{24,28},{28,24},{1,5},{5... | collective-permute-start | bytes 1572872 | tf_op jit(solution)/shard_map/ppermute | solution.py:169
  63.1 2.8 %copy-start.10 = (bf16[2,512,256]{2,1,0:T(8,128)(2,1)S(1)}, bf16[2,512,256]{2,1,0:T(8,128)(2,1)}, u32[]{:S(2)}) copy-start(bf16[2,512,256]{2,1,0:T(8,128)(2,1)} %get-tuple-element.18) | copy-start | bytes 1572868
  63.1 17.3 %collective-permute-start.5 = (bf16[2,512,256]{2,1,0:T(8,128)(2,1)S(1)}, bf16[2,512,256]{2,1,0:T(8,128)(2,1)S(1)}, u32[]{:S(2)}, u32[]{:S(2)}) collective-permute-start(bf16[2,512,256]{2,1,0:T(8,128)(2,1)S(1)} %fusion.15), channel_id=1, source_target_pairs={{8,0},{12,4},{16,8},{20,12},{24,16},{28,20},{9,1},{13,5},{17,9},{2... | collective-permute-start | bytes 1572872 | tf_op jit(solution)/shard_map/ppermute | solution.py:174
  64.8 15.7 %copy-start.3 = (f32[2,512,256]{2,1,0:T(8,128)S(1)}, f32[2,512,256]{2,1,0:T(8,128)}, u32[]{:S(2)}) copy-start(f32[2,512,256]{2,1,0:T(8,128)} %get-tuple-element.14) | copy-start | bytes 3145732
  66.1 25.4 %collective-permute-start.7 = (bf16[2,512,256]{2,1,0:T(8,128)(2,1)S(1)}, bf16[2,512,256]{2,1,0:T(8,128)(2,1)S(1)}, u32[]{:S(2)}, u32[]{:S(2)}) collective-permute-start(bf16[2,512,256]{2,1,0:T(8,128)(2,1)S(1)} %fusion.19), channel_id=1, source_target_pairs={{8,0},{12,4},{16,8},{20,12},{24,16},{28,20},{9,1},{13,5},{17,9},{2... | collective-permute-start | bytes 1572872 | tf_op jit(solution)/shard_map/ppermute | solution.py:174
  80.4 11.0 %copy-start.4 = (f32[2,512,256]{2,1,0:T(8,128)S(1)}, f32[2,512,256]{2,1,0:T(8,128)}, u32[]{:S(2)}) copy-start(f32[2,512,256]{2,1,0:T(8,128)} %get-tuple-element.17) | copy-start | bytes 3145732
  135.8 5.8 %copy-start = (bf16[512,5376]{0,1:T(8,128)(2,1)S(1)}, bf16[512,5376]{0,1:T(8,128)(2,1)}, u32[]{:S(2)}) copy-start(bf16[512,5376]{0,1:T(8,128)(2,1)} %copy.16) | copy-start | bytes 16515076
  137.6 7.3 %collective-permute-start.12 = (bf16[672,512]{1,0:T(8,128)(2,1)S(1)}, bf16[672,512]{1,0:T(8,128)(2,1)S(1)}, u32[]{:S(2)}, u32[]{:S(2)}) collective-permute-start(bf16[672,512]{1,0:T(8,128)(2,1)S(1)} %convolution_convert_fusion.12), channel_id=1, source_target_pairs={{0,4},{4,0},{8,12},{12,8},{16,20},{20,16},{24,28},{28,24},{1,5},{5... | collective-permute-start | bytes 2064392 | tf_op jit(solution)/shard_map/ppermute | solution.py:169
  139.3 17.1 %collective-permute-start.11 = (bf16[672,512]{1,0:T(8,128)(2,1)S(1)}, bf16[672,512]{1,0:T(8,128)(2,1)S(1)}, u32[]{:S(2)}, u32[]{:S(2)}) collective-permute-start(bf16[672,512]{1,0:T(8,128)(2,1)S(1)} %convolution_convert_fusion.13), channel_id=1, source_target_pairs={{0,4},{4,0},{8,12},{12,8},{16,20},{20,16},{24,28},{28,24},{1,5},{5... | collective-permute-start | bytes 2064392 | tf_op jit(solution)/shard_map/ppermute | solution.py:169
  141.5 5.1 %collective-permute-start.9 = (bf16[672,512]{1,0:T(8,128)(2,1)S(1)}, bf16[672,512]{1,0:T(8,128)(2,1)S(1)}, u32[]{:S(2)}, u32[]{:S(2)}) collective-permute-start(bf16[672,512]{1,0:T(8,128)(2,1)S(1)} %convolution_convert_fusion.14), channel_id=1, source_target_pairs={{0,4},{4,0},{8,12},{12,8},{16,20},{20,16},{24,28},{28,24},{1,5},{5... | collective-permute-start | bytes 2064392 | tf_op jit(solution)/shard_map/ppermute | solution.py:169
  142.1 26.5 %collective-permute-start.8 = (bf16[672,512]{1,0:T(8,128)(2,1)S(1)}, bf16[672,512]{1,0:T(8,128)(2,1)S(1)}, u32[]{:S(2)}, u32[]{:S(2)}) collective-permute-start(bf16[672,512]{1,0:T(8,128)(2,1)S(1)} %convolution_convert_fusion.15), channel_id=1, source_target_pairs={{0,4},{4,0},{8,12},{12,8},{16,20},{20,16},{24,28},{28,24},{1,5},{5... | collective-permute-start | bytes 2064392 | tf_op jit(solution)/shard_map/ppermute | solution.py:169
  143.2 2.8 %collective-permute-start.19 = (bf16[672,512]{1,0:T(8,128)(2,1)S(1)}, bf16[672,512]{1,0:T(8,128)(2,1)S(1)}, u32[]{:S(2)}, u32[]{:S(2)}) collective-permute-start(bf16[672,512]{1,0:T(8,128)(2,1)S(1)} %convolution_convert_fusion.8), channel_id=1, source_target_pairs={{0,4},{4,0},{8,12},{12,8},{16,20},{20,16},{24,28},{28,24},{1,5},{5... | collective-permute-start | bytes 2064392 | tf_op jit(solution)/shard_map/ppermute | solution.py:169
  144.9 5.0 %collective-permute-start.16 = (bf16[672,512]{1,0:T(8,128)(2,1)S(1)}, bf16[672,512]{1,0:T(8,128)(2,1)S(1)}, u32[]{:S(2)}, u32[]{:S(2)}) collective-permute-start(bf16[672,512]{1,0:T(8,128)(2,1)S(1)} %convolution_convert_fusion.10), channel_id=1, source_target_pairs={{0,4},{4,0},{8,12},{12,8},{16,20},{20,16},{24,28},{28,24},{1,5},{5... | collective-permute-start | bytes 2064392 | tf_op jit(solution)/shard_map/ppermute | solution.py:169
  145.9 11.1 %collective-permute-start.18 = (bf16[672,512]{1,0:T(8,128)(2,1)S(1)}, bf16[672,512]{1,0:T(8,128)(2,1)S(1)}, u32[]{:S(2)}, u32[]{:S(2)}) collective-permute-start(bf16[672,512]{1,0:T(8,128)(2,1)S(1)} %convolution_convert_fusion.9), channel_id=1, source_target_pairs={{0,4},{4,0},{8,12},{12,8},{16,20},{20,16},{24,28},{28,24},{1,5},{5... | collective-permute-start | bytes 2064392 | tf_op jit(solution)/shard_map/ppermute | solution.py:169
  146.6 18.8 %collective-permute-start.13 = (bf16[672,512]{1,0:T(8,128)(2,1)S(1)}, bf16[672,512]{1,0:T(8,128)(2,1)S(1)}, u32[]{:S(2)}, u32[]{:S(2)}) collective-permute-start(bf16[672,512]{1,0:T(8,128)(2,1)S(1)} %fusion.7), channel_id=1, source_target_pairs={{0,8},{4,12},{8,0},{12,4},{16,24},{20,28},{24,16},{28,20},{1,9},{5... | collective-permute-start | bytes 2064392 | tf_op jit(solution)/shard_map/ppermute | solution.py:169
  149.9 17.6 %collective-permute-start.20 = (bf16[672,512]{1,0:T(8,128)(2,1)S(1)}, bf16[672,512]{1,0:T(8,128)(2,1)S(1)}, u32[]{:S(2)}, u32[]{:S(2)}) collective-permute-start(bf16[672,512]{1,0:T(8,128)(2,1)S(1)} %fusion.9), channel_id=1, source_target_pairs={{0,16},{4,20},{8,24},{12,28},{16,0},{20,4},{24,8},{28,12},{1,17},{... | collective-permute-start | bytes 2064392 | tf_op jit(solution)/shard_map/ppermute | solution.py:169
  156.4 12.6 %collective-permute-start.33 = (bf16[672,512]{1,0:T(8,128)(2,1)S(1)}, bf16[672,512]{1,0:T(8,128)(2,1)S(1)}, u32[]{:S(2)}, u32[]{:S(2)}) collective-permute-start(bf16[672,512]{1,0:T(8,128)(2,1)S(1)} %convolution_convert_fusion), channel_id=1, source_target_pairs={{0,4},{4,0},{8,12},{12,8},{16,20},{20,16},{24,28},{28,24},{1,5},{5... | collective-permute-start | bytes 2064392 | tf_op jit(solution)/shard_map/ppermute | solution.py:169
  157.1 12.7 %collective-permute-start.15 = (bf16[672,512]{1,0:T(8,128)(2,1)S(1)}, bf16[672,512]{1,0:T(8,128)(2,1)S(1)}, u32[]{:S(2)}, u32[]{:S(2)}) collective-permute-start(bf16[672,512]{1,0:T(8,128)(2,1)S(1)} %convolution_convert_fusion.11), channel_id=1, source_target_pairs={{0,4},{4,0},{8,12},{12,8},{16,20},{20,16},{24,28},{28,24},{1,5},{5... | collective-permute-start | bytes 2064392 | tf_op jit(solution)/shard_map/ppermute | solution.py:169
  165.3 4.8 %collective-permute-start.30 = (bf16[672,512]{1,0:T(8,128)(2,1)S(1)}, bf16[672,512]{1,0:T(8,128)(2,1)S(1)}, u32[]{:S(2)}, u32[]{:S(2)}) collective-permute-start(bf16[672,512]{1,0:T(8,128)(2,1)S(1)} %convolution_convert_fusion.2), channel_id=1, source_target_pairs={{0,4},{4,0},{8,12},{12,8},{16,20},{20,16},{24,28},{28,24},{1,5},{5... | collective-permute-start | bytes 2064392 | tf_op jit(solution)/shard_map/ppermute | solution.py:169
  167.4 4.4 %collective-permute-start.26 = (bf16[672,512]{1,0:T(8,128)(2,1)S(1)}, bf16[672,512]{1,0:T(8,128)(2,1)S(1)}, u32[]{:S(2)}, u32[]{:S(2)}) collective-permute-start(bf16[672,512]{1,0:T(8,128)(2,1)S(1)} %convolution_convert_fusion.4), channel_id=1, source_target_pairs={{0,4},{4,0},{8,12},{12,8},{16,20},{20,16},{24,28},{28,24},{1,5},{5... | collective-permute-start | bytes 2064392 | tf_op jit(solution)/shard_map/ppermute | solution.py:169
  168.6 17.9 %collective-permute-start.10 = (bf16[672,512]{1,0:T(8,128)(2,1)S(1)}, bf16[672,512]{1,0:T(8,128)(2,1)S(1)}, u32[]{:S(2)}, u32[]{:S(2)}) collective-permute-start(bf16[672,512]{1,0:T(8,128)(2,1)S(1)} %fusion.6), channel_id=1, source_target_pairs={{0,8},{4,12},{8,0},{12,4},{16,24},{20,28},{24,16},{28,20},{1,9},{5... | collective-permute-start | bytes 2064392 | tf_op jit(solution)/shard_map/ppermute | solution.py:169
  169.0 17.5 %collective-permute-start.23 = (bf16[672,512]{1,0:T(8,128)(2,1)S(1)}, bf16[672,512]{1,0:T(8,128)(2,1)S(1)}, u32[]{:S(2)}, u32[]{:S(2)}) collective-permute-start(bf16[672,512]{1,0:T(8,128)(2,1)S(1)} %convolution_convert_fusion.6), channel_id=1, source_target_pairs={{0,4},{4,0},{8,12},{12,8},{16,20},{20,16},{24,28},{28,24},{1,5},{5... | collective-permute-start | bytes 2064392 | tf_op jit(solution)/shard_map/ppermute | solution.py:169
  169.8 17.6 %collective-permute-start.32 = (bf16[672,512]{1,0:T(8,128)(2,1)S(1)}, bf16[672,512]{1,0:T(8,128)(2,1)S(1)}, u32[]{:S(2)}, u32[]{:S(2)}) collective-permute-start(bf16[672,512]{1,0:T(8,128)(2,1)S(1)} %convolution_convert_fusion.1), channel_id=1, source_target_pairs={{0,4},{4,0},{8,12},{12,8},{16,20},{20,16},{24,28},{28,24},{1,5},{5... | collective-permute-start | bytes 2064392 | tf_op jit(solution)/shard_map/ppermute | solution.py:169
  170.1 19.1 %collective-permute-start.14 = (bf16[672,512]{1,0:T(8,128)(2,1)S(1)}, bf16[672,512]{1,0:T(8,128)(2,1)S(1)}, u32[]{:S(2)}, u32[]{:S(2)}) collective-permute-start(bf16[672,512]{1,0:T(8,128)(2,1)S(1)} %fusion.12), channel_id=1, source_target_pairs={{0,16},{4,20},{8,24},{12,28},{16,0},{20,4},{24,8},{28,12},{1,17},{... | collective-permute-start | bytes 2064392 | tf_op jit(solution)/shard_map/ppermute | solution.py:169
  171.8 31.3 %collective-permute-start.34 = (bf16[672,512]{1,0:T(8,128)(2,1)S(1)}, bf16[672,512]{1,0:T(8,128)(2,1)S(1)}, u32[]{:S(2)}, u32[]{:S(2)}) collective-permute-start(bf16[672,512]{1,0:T(8,128)(2,1)S(1)} %add_convert_fusion.2), channel_id=1, source_target_pairs={{0,16},{4,20},{8,24},{12,28},{16,0},{20,4},{24,8},{28,12},{1,17},{... | collective-permute-start | bytes 2064392 | tf_op jit(solution)/shard_map/ppermute | solution.py:169
  186.5 19.5 %collective-permute-start.25 = (bf16[672,512]{1,0:T(8,128)(2,1)S(1)}, bf16[672,512]{1,0:T(8,128)(2,1)S(1)}, u32[]{:S(2)}, u32[]{:S(2)}) collective-permute-start(bf16[672,512]{1,0:T(8,128)(2,1)S(1)} %convolution_convert_fusion.5), channel_id=1, source_target_pairs={{0,4},{4,0},{8,12},{12,8},{16,20},{20,16},{24,28},{28,24},{1,5},{5... | collective-permute-start | bytes 2064392 | tf_op jit(solution)/shard_map/ppermute | solution.py:169
  186.5 19.8 %collective-permute-start.27 = (bf16[672,512]{1,0:T(8,128)(2,1)S(1)}, bf16[672,512]{1,0:T(8,128)(2,1)S(1)}, u32[]{:S(2)}, u32[]{:S(2)}) collective-permute-start(bf16[672,512]{1,0:T(8,128)(2,1)S(1)} %add_convert_fusion.6), channel_id=1, source_target_pairs={{0,8},{4,12},{8,0},{12,4},{16,24},{20,28},{24,16},{28,20},{1,9},{5... | collective-permute-start | bytes 2064392 | tf_op jit(solution)/shard_map/ppermute | solution.py:169
  187.4 30.5 %collective-permute-start.17 = (bf16[672,512]{1,0:T(8,128)(2,1)S(1)}, bf16[672,512]{1,0:T(8,128)(2,1)S(1)}, u32[]{:S(2)}, u32[]{:S(2)}) collective-permute-start(bf16[672,512]{1,0:T(8,128)(2,1)S(1)} %fusion.8), channel_id=1, source_target_pairs={{0,16},{4,20},{8,24},{12,28},{16,0},{20,4},{24,8},{28,12},{1,17},{... | collective-permute-start | bytes 2064392 | tf_op jit(solution)/shard_map/ppermute | solution.py:169
  189.2 28.7 %collective-permute-start.29 = (bf16[672,512]{1,0:T(8,128)(2,1)S(1)}, bf16[672,512]{1,0:T(8,128)(2,1)S(1)}, u32[]{:S(2)}, u32[]{:S(2)}) collective-permute-start(bf16[672,512]{1,0:T(8,128)(2,1)S(1)} %convolution_convert_fusion.3), channel_id=1, source_target_pairs={{0,4},{4,0},{8,12},{12,8},{16,20},{20,16},{24,28},{28,24},{1,5},{5... | collective-permute-start | bytes 2064392 | tf_op jit(solution)/shard_map/ppermute | solution.py:169
  203.1 18.4 %collective-permute-start.21 = (bf16[672,512]{1,0:T(8,128)(2,1)S(1)}, bf16[672,512]{1,0:T(8,128)(2,1)S(1)}, u32[]{:S(2)}, u32[]{:S(2)}) collective-permute-start(bf16[672,512]{1,0:T(8,128)(2,1)S(1)} %fusion.10), channel_id=1, source_target_pairs={{0,8},{4,12},{8,0},{12,4},{16,24},{20,28},{24,16},{28,20},{1,9},{5... | collective-permute-start | bytes 2064392 | tf_op jit(solution)/shard_map/ppermute | solution.py:169
  206.0 26.6 %collective-permute-start.31 = (bf16[672,512]{1,0:T(8,128)(2,1)S(1)}, bf16[672,512]{1,0:T(8,128)(2,1)S(1)}, u32[]{:S(2)}, u32[]{:S(2)}) collective-permute-start(bf16[672,512]{1,0:T(8,128)(2,1)S(1)} %add_convert_fusion.3), channel_id=1, source_target_pairs={{0,16},{4,20},{8,24},{12,28},{16,0},{20,4},{24,8},{28,12},{1,17},{... | collective-permute-start | bytes 2064392 | tf_op jit(solution)/shard_map/ppermute | solution.py:169
  206.3 29.9 %collective-permute-start.35 = (bf16[672,512]{1,0:T(8,128)(2,1)S(1)}, bf16[672,512]{1,0:T(8,128)(2,1)S(1)}, u32[]{:S(2)}, u32[]{:S(2)}) collective-permute-start(bf16[672,512]{1,0:T(8,128)(2,1)S(1)} %add_convert_fusion.1), channel_id=1, source_target_pairs={{0,8},{4,12},{8,0},{12,4},{16,24},{20,28},{24,16},{28,20},{1,9},{5... | collective-permute-start | bytes 2064392 | tf_op jit(solution)/shard_map/ppermute | solution.py:169
  217.9 19.6 %collective-permute-start.22 = (bf16[672,512]{1,0:T(8,128)(2,1)S(1)}, bf16[672,512]{1,0:T(8,128)(2,1)S(1)}, u32[]{:S(2)}, u32[]{:S(2)}) collective-permute-start(bf16[672,512]{1,0:T(8,128)(2,1)S(1)} %convolution_convert_fusion.7), channel_id=1, source_target_pairs={{0,4},{4,0},{8,12},{12,8},{16,20},{20,16},{24,28},{28,24},{1,5},{5... | collective-permute-start | bytes 2064392 | tf_op jit(solution)/shard_map/ppermute | solution.py:169
  217.9 31.0 %collective-permute-start.24 = (bf16[672,512]{1,0:T(8,128)(2,1)S(1)}, bf16[672,512]{1,0:T(8,128)(2,1)S(1)}, u32[]{:S(2)}, u32[]{:S(2)}) collective-permute-start(bf16[672,512]{1,0:T(8,128)(2,1)S(1)} %add_convert_fusion.7), channel_id=1, source_target_pairs={{0,8},{4,12},{8,0},{12,4},{16,24},{20,28},{24,16},{28,20},{1,9},{5... | collective-permute-start | bytes 2064392 | tf_op jit(solution)/shard_map/ppermute | solution.py:169
  221.5 27.4 %collective-permute-start.28 = (bf16[672,512]{1,0:T(8,128)(2,1)S(1)}, bf16[672,512]{1,0:T(8,128)(2,1)S(1)}, u32[]{:S(2)}, u32[]{:S(2)}) collective-permute-start(bf16[672,512]{1,0:T(8,128)(2,1)S(1)} %add_convert_fusion.5), channel_id=1, source_target_pairs={{0,16},{4,20},{8,24},{12,28},{16,0},{20,4},{24,8},{28,12},{1,17},{... | collective-permute-start | bytes 2064392 | tf_op jit(solution)/shard_map/ppermute | solution.py:169
  (3 other events, 3.5 us)
Sparse Core Ops, SparseCore 0:
  112.1 103.7 reduce-scatter.1

commit v2 on v1

--- a/solution.py
+++ b/solution.py
@@ -15,6 +15,7 @@
 TILE = 256
 SCALE = (D // H) ** (-0.5)
 FAR = -1e30
+TOKEN_PARTS = 1
 VMEM_BYTES = 56 * 1024 * 1024
 
 NT = (((1,), (1,)), ((), ()))
@@ -108,7 +109,6 @@
     pair_spec = pl.BlockSpec((2, rows, HD), lambda h: (0, 0, h))
     span = WINDOW + TILE
     pair = jax.ShapeDtypeStruct((2, rows, heads * HD), jnp.bfloat16)
-    pairs_seen = heads * groups * rows * span
     return pl.pallas_call(
         functools.partial(attention_kernel, groups, depth),
         grid=(heads,),
@@ -125,41 +125,126 @@
             pltpu.VMEM((WINDOW + rows, HD), jnp.float32),
         ],
         compiler_params=pltpu.CompilerParams(vmem_limit_bytes=VMEM_BYTES),
-        cost_estimate=pl.CostEstimate(
-            flops=10 * pairs_seen * HD * 2,
-            bytes_accessed=2 * rows * heads * HD * 20,
-            transcendentals=pairs_seen,
-        ),
         name="attention_grads",
     )(lowest, query, out_grad, *pieces)
 
 
+def arrange_kernel(order_ref, x_ref, first_ref, second_ref, scratch):
+    width = first_ref.shape[1]
+    step = pl.program_id(0)
+    half = pl.num_programs(0) // 2
+
+    @pl.when(step == 0)
+    def _():
+        tile = 768 if x_ref.shape[1] % 768 == 0 else 128
+        for i in range(x_ref.shape[1] // tile):
+            at = slice(i * tile, (i + 1) * tile)
+            scratch[at, :] = x_ref[:, at].T
+
+    start = pl.multiple_of(order_ref[step] * width, 16)
+
+    @pl.when(step < half)
+    def _():
+        first_ref[0] = scratch[pl.ds(start, width), :]
+
+    @pl.when(step >= half)
+    def _():
+        second_ref[0] = scratch[pl.ds(start, width), :]
+
+
+def arranged(array, order, count):
+    rows, cols = array.shape
+    width, half = cols // count, count // 2
+    out = jax.ShapeDtypeStruct((half, width, rows), array.dtype)
+    return pl.pallas_call(
+        arrange_kernel,
+        grid_spec=pltpu.PrefetchScalarGridSpec(
+            num_scalar_prefetch=1,
+            grid=(count,),
+            in_specs=[pl.BlockSpec((rows, cols), lambda i, order_ref: (0, 0))],
+            out_specs=[
+                pl.BlockSpec((1, width, rows), lambda i, order_ref: (jnp.minimum(i, half - 1), 0, 0)),
+                pl.BlockSpec((1, width, rows), lambda i, order_ref: (jnp.maximum(i - half, 0), 0, 0)),
+            ],
+            scratch_shapes=[pltpu.VMEM((cols, rows), array.dtype)],
+        ),
+        out_shape=[out, out],
+        compiler_params=pltpu.CompilerParams(vmem_limit_bytes=VMEM_BYTES),
+        name="arranged_input",
+    )(order, array)
+
+
+def listed(values, index):
+    total = jnp.int32(values[0])
+    for i, value in enumerate(values[1:], 1):
+        total = jnp.where(index == i, jnp.int32(value), total)
+    return total
+
+
+def paired_kernel(count, joined, *refs):
+    outs = refs[2 * (2 + count) :]
+    for side in range(2):
+        x_ref, g_ref, *arrived = refs[side * (2 + count) : (side + 1) * (2 + count)]
+        value = dot(x_ref[0], g_ref[...])
+        for ref in arrived:
+            value = value + ref[0].astype(jnp.float32)
+        value = value.astype(jnp.bfloat16)
+        if joined:
+            cols = value.shape[1]
+            outs[0][:, side * cols : (side + 1) * cols] = value
+        else:
+            outs[side][0] = value
+
+
+def paired_products(sides, joined=False):
+    specs, operands = [], []
+    for inputs, grads, arrived, at in sides:
+        for array, where in zip([inputs, *arrived], at):
+            spec = pl.BlockSpec((1,) + array.shape[1:], lambda i, where=where: (listed(where, i), 0, 0))
+            specs.append(spec)
+            operands.append(array)
+        place = len(specs) - len(arrived)
+        specs.insert(place, pl.BlockSpec(grads.shape, lambda i: (0, 0)))
+        operands.insert(place, grads)
+    inputs, grads, arrived, at = sides[0]
+    count, width, cols = len(at[0]), inputs.shape[1], grads.shape[1]
+    if joined:
+        out_specs = pl.BlockSpec((width, 2 * cols), lambda i: (0, 0))
+        out_shape = jax.ShapeDtypeStruct((width, 2 * cols), jnp.bfloat16)
+    else:
+        out_specs = [pl.BlockSpec((1, width, cols), lambda i: (i, 0, 0))] * 2
+        out_shape = [jax.ShapeDtypeStruct((count, width, cols), jnp.bfloat16)] * 2
+    return pl.pallas_call(
+        functools.partial(paired_kernel, len(arrived), joined),
+        grid=(count,),
+        in_specs=specs,
+        out_specs=out_specs,
+        out_shape=out_shape,
+        compiler_params=pltpu.CompilerParams(vmem_limit_bytes=VMEM_BYTES),
+        name="projection_products",
+    )(*operands)
+
+
 def term_kernel(dq_ref, dk_ref, dv_ref, wq_ref, wk_ref, wv_ref, out_ref):
     out_ref[0] = (
-        dot(dq_ref[...], wq_ref[...], NT)
-        + dot(dk_ref[...], wk_ref[...], NT)
-        + dot(dv_ref[...], wv_ref[...], NT)
+        dot(wq_ref[...], dq_ref[...], NT)
+        + dot(wk_ref[...], dk_ref[...], NT)
+        + dot(wv_ref[...], dv_ref[...], NT)
     ).astype(jnp.bfloat16)
 
 
-def input_term(dq, dk, dv, w_query, w_key, w_value, parts):
-    rows = dq.shape[0]
+def input_term(dq, dk, dv, w_query, w_key, w_value, parts, piece, pieces):
+    rows = dq.shape[0] // pieces
     width = w_query.shape[0] // parts
-    grads = [pl.BlockSpec(a.shape, lambda p: (0, 0)) for a in (dq, dk, dv)]
+    grads = [pl.BlockSpec((rows, a.shape[1]), lambda p: (piece, 0)) for a in (dq, dk, dv)]
     weights = [pl.BlockSpec((width, w.shape[1]), lambda p: (p, 0)) for w in (w_query, w_key, w_value)]
-    depth = dq.shape[1] + dk.shape[1] + dv.shape[1]
     return pl.pallas_call(
         term_kernel,
         grid=(parts,),
         in_specs=grads + weights,
-        out_specs=pl.BlockSpec((1, rows, width), lambda p: (p, 0, 0)),
-        out_shape=jax.ShapeDtypeStruct((parts, rows, width), jnp.bfloat16),
+        out_specs=pl.BlockSpec((1, width, rows), lambda p: (p, 0, 0)),
+        out_shape=jax.ShapeDtypeStruct((parts, width, rows), jnp.bfloat16),
         compiler_params=pltpu.CompilerParams(vmem_limit_bytes=VMEM_BYTES),
-        cost_estimate=pl.CostEstimate(
-            flops=2 * rows * width * parts * depth,
-            bytes_accessed=2 * (width * parts * (depth + rows) + rows * depth),
-            transcendentals=0,
-        ),
         name="input_term",
     )(dq, dk, dv, w_query, w_key, w_value)
 
@@ -176,37 +261,63 @@
     )
 
 
-def earlier_pieces(own, odd):
-    two_back = shifted(own, 2)
-    one_back = swapped(jnp.where(odd, two_back, own), 1)
-    return two_back, one_back
-
-
-def returned(two_back, one_back, own, odd):
-    beside = swapped(one_back, 1)
-    both = two_back.astype(jnp.float32) + jnp.where(odd, beside.astype(jnp.float32), 0.0)
-    later = shifted(both.astype(jnp.bfloat16), -2)
-    total = own + later.astype(jnp.float32) + jnp.where(odd, 0.0, beside.astype(jnp.float32))
-    return total.astype(jnp.bfloat16)
-
-
-def scattered_product(rows_by_offset, grads, bits):
-    size = len(rows_by_offset)
-    arrived = {o: [] for o in range(size)}
-
-    def summed(offset):
-        value = dot(rows_by_offset[offset], grads)
-        for other in arrived[offset]:
-            value = value + other.astype(jnp.float32)
-        return value.astype(jnp.bfloat16)
-
-    alive = list(range(size))
-    for bit in bits:
-        leaving = [o for o in alive if o & bit]
-        alive = [o for o in alive if not o & bit]
-        for o in leaving:
-            arrived[o ^ bit].append(swapped(summed(o), bit))
-    return summed(0)
+def gray(index):
+    return index ^ (index >> 1)
+
+
+class Order:
+    def __init__(self):
+        self.last = ()
+
+    def after(self, *values):
+        values, _ = lax.optimization_barrier((values, self.last))
+        return values if len(values) > 1 else values[0]
+
+    def did(self, value):
+        self.last = value
+        return value
+
+
+class Scattered:
+    def __init__(self, inputs, offsets, grads, beside, bits):
+        self.inputs, self.offsets, self.grads = inputs, offsets, list(grads)
+        self.bits = [list(bits), list(bits[::-1])]
+        self.alive = [list(offsets)] * 2
+        self.arrived = [[(list(offsets), b)] for b in beside]
+
+    def summed(self, order, leaving, joined=False):
+        arrived = order.after(*[[array for _, array in held] for held in self.arrived])
+        sides = []
+        for i in range(2):
+            at = [[held.index(o) for o in leaving[i]] for held, _ in self.arrived[i]]
+            at.insert(0, [self.offsets.index(o) for o in leaving[i]])
+            sides.append((self.inputs, self.grads[i], arrived[i], at))
+        return order.did(paired_products(sides, joined))
+
+    def step(self, order):
+        bits = [b.pop(0) for b in self.bits]
+        leaving = [[o for o in alive if o & bit] for alive, bit in zip(self.alive, bits)]
+        self.alive = [[o for o in alive if not o & bit] for alive, bit in zip(self.alive, bits)]
+        blocks = self.summed(order, leaving)
+        for i in range(2):
+            self.arrived[i].append(([o ^ bits[i] for o in leaving[i]], swapped(blocks[i], bits[i])))
+
+    def result(self, order, joined=False):
+        out = self.summed(order, [[0], [0]], joined)
+        return out if joined else [o[0] for o in out]
+
+
+def beside_products(odds, first, second):
+    at = [list(range(odds.shape[0]))]
+    blocks = paired_products([(odds, first, [], at), (odds, second, [], at)])
+    return [swapped(block, 1) for block in blocks]
+
+
+def kept_together(always, work, *operands):
+    def nothing(*operands):
+        return jax.tree.map(lambda a: jnp.zeros(a.shape, a.dtype), jax.eval_shape(work, *operands))
+
+    return lax.cond(always, work, nothing, *operands)
 
 
 def on_device(layer_input, query, keys, values, out_grad, w_query, w_key, w_value, proof_lengths):
@@ -227,51 +338,79 @@
     lowest = jnp.maximum(proof_start, positions - (WINDOW - 1)) - first_row + WINDOW
     lowest = lowest.astype(jnp.int32)[None, :]
 
+    order = Order()
     sets = 2 if kv_local % 2 == 0 else 1
     per_set = kv_local // sets
     cols = per_set * HD
-    dqs, dks, dvs = [], [], []
-    stacked = []
+
+    def pair(c):
+        at = slice(c * cols, (c + 1) * cols)
+        return jnp.stack([keys[:, at], values[:, at]])
+
+    own = order.did(pair(0))
+    two_back = shifted(own, 2)
+    steps = seq_size.bit_length() - 1
+    even = [2 * gray(i) for i in range(1, seq_size // 2)] + [0]
+    offsets = [o ^ 1 for o in even] + even
+    layer_input = order.after(layer_input)
+    odds, evens = order.did(arranged(layer_input, me ^ jnp.array(offsets, jnp.int32), seq_size))
+    pieces = []
+    for c in range(1, sets):
+        keys, values = order.after(keys, values)
+        other = order.did(pair(c))
+        pieces.append([shifted(other, 2), shifted(other, 1), other])
+    two_back = order.after(two_back)
+    passed = order.did(jnp.where(odd, two_back, own))
+    pieces.insert(0, [two_back, swapped(passed, 1), own])
+    dqs, halos = [], []
     for c in range(sets):
-        at = slice(c * cols, (c + 1) * cols)
-        own = jnp.stack([keys[:, at], values[:, at]])
-        stacked.append((earlier_pieces(own, odd), own))
-    for c in range(sets):
-        (two_back, one_back), own = stacked[c]
-        dq, halo_two, halo_one, own_grad = attention(
-            lowest, query, out_grad, [two_back, one_back, own], c * per_set, groups
+        seen = order.after(*pieces[c])
+        dq, halo_two, halo_one, own_grad = order.did(
+            attention(lowest, query, out_grad, seen, c * per_set, groups)
         )
-        total = returned(halo_two, halo_one, own_grad, odd)
         dqs.append(dq)
-        dks.append(total[0])
-        dvs.append(total[1])
+        halos.append((own_grad, shifted(halo_one, -1), shifted(halo_two, -2)))
     dq = jnp.concatenate(dqs, axis=1)
-    dk = jnp.concatenate(dks, axis=1)
-    dv = jnp.concatenate(dvs, axis=1)
-
-    term = input_term(dq, dk, dv, w_query, w_key, w_value, head_size)
-    input_grad = lax.psum_scatter(term, "head", scatter_dimension=0, tiled=False)
-
-    block = layer_input.shape[1] // seq_size
-    by_block = layer_input.T.reshape(seq_size, block, rows)
-    order = me ^ jnp.arange(seq_size, dtype=jnp.int32)
-    by_offset = [
-        lax.dynamic_index_in_dim(by_block, order[o], 0, keepdims=False) for o in range(seq_size)
-    ]
-    bits = [1 << j for j in range(1, seq_size.bit_length() - 1)]
-    forward = [1] + bits
-    backward = [1] + bits[::-1]
     half = dq.shape[1] // 2
-    wq_grad = jnp.concatenate(
-        [
-            scattered_product(by_offset, dq[:, :half], forward),
-            scattered_product(by_offset, dq[:, half:], backward),
-        ],
-        axis=1,
-    )
-    wk_grad = scattered_product(by_offset, dk, forward)
-    wv_grad = scattered_product(by_offset, dv, backward)
-    return (input_grad, wq_grad, wk_grad, wv_grad)
+    if sets != 2:
+        dqs = [dq[:, :half], dq[:, half:]]
+
+    always = proof_lengths[0] > 0
+    bits = [1 << j for j in range(1, steps)]
+    totals = []
+    for c, parts in enumerate(halos):
+        if c == sets - 1:
+            args = order.after(odds, *dqs)
+            beside = order.did(kept_together(always, beside_products, *args))
+        parts = order.after(*parts)
+        total = sum(part.astype(jnp.float32) for part in parts).astype(jnp.bfloat16)
+        totals.append(order.did(total))
+    dk = jnp.concatenate([t[0] for t in totals], axis=1)
+    dv = jnp.concatenate([t[1] for t in totals], axis=1)
+    input_grads = []
+    for i in range(TOKEN_PARTS):
+        grads = order.after(dq, dk, dv)
+        term = order.did(input_term(*grads, w_query, w_key, w_value, head_size, i, TOKEN_PARTS))
+        input_grads.append(lax.psum_scatter(term, "head", scatter_dimension=0, tiled=False))
+    input_grad = jnp.concatenate(input_grads, axis=1).T
+
+    def projections(odds, evens, dqs, beside, dk, dv):
+        order = Order()
+        query_sum = Scattered(evens, even, dqs, beside, bits)
+        query_sum.step(order)
+        args = order.after(odds, dk, dv)
+        beside = order.did(kept_together(always, beside_products, *args))
+        other_sum = Scattered(evens, even, [dk, dv], beside, bits)
+        other_sum.step(order)
+        while query_sum.bits[0]:
+            query_sum.step(order)
+            other_sum.step(order)
+        wq_grad = query_sum.result(order, True)
+        return (wq_grad, *other_sum.result(order))
+
+    parts = order.after(odds, evens, dqs, beside, dk, dv)
+    grads = kept_together(always, projections, *parts)
+    return (input_grad, *grads)
 
 
 def solution(mesh):

time: 260 us -> 219 us (0.84)
  Pallas kernels: 43.3 us -> 86 us
  waiting for transfers between devices: 113 us -> 71.9 us
  matrix products: 20.7 us -> 0 us
  between operations: 29.6 us -> 14.2 us
  local copies, waits for them, and re-layouts: 14.3 us -> 6.66 us
    pallas_call x0 -> x9, Pallas kernels: none -> 44.1 us  [the longest x8 36.3 us: paired_products(): pl.pallas_call(functools.partial(paired_kernel, len(arrived), joined), gr...]
    ppermute x4 -> x7, waiting for transfers between devices: 41.6 us -> 3.17 us  [shifted(): lax.ppermute(block, 'seq', [(i, i + distance) for i in range(size) if 0 <...]
    dot_general x32 -> x0, matrix products: 20.7 us -> none  [dot(): lax.dot_general(left, right, dims, preferred_element_type=jnp.float32)]
    unnamed x30 -> x18, local copies, waits for them, and re-layouts: 12.4 us -> 1.62 us
    ppermute x4 -> x7, starting transfers between devices: 11.2 us -> 16.8 us  [shifted(): lax.ppermute(block, 'seq', [(i, i + distance) for i in range(size) if 0 <...]
    ppermute x32 -> x13, starting transfers between devices: 18.7 us -> 14.1 us  [swapped(): return lax.ppermute(block, 'seq', [(i, i ^ bit) for i in range(size)])]
    concatenate x3 -> x2, other arithmetic: 2.91 us -> 0.07 us  [the longest x1 0.04 us: on_device(): dk = jnp.concatenate([t[0] for t in totals], axis=1)]
    cond x0 -> x14, local copies, waits for them, and re-layouts: none -> 2.84 us
  transfers between devices with their start and end apart: 37 -> 21, of which waited for: 13 -> 12; matrix products, arithmetic and copies ran while one was open for 14% -> 3% of each run, Pallas kernels for 10% -> 32%
where the time goes in v2:
time: 219 us
  Pallas kernels  86 us (39%)
  waiting for transfers between devices  71.9 us (33%)
  starting transfers between devices  30.9 us (14%)
  between operations  14.2 us (6%)
  other arithmetic  8.82 us (4%)
  local copies, waits for them, and re-layouts  6.66 us (3%)
    ppermute x13, waiting for transfers between devices, swapped(): return lax.ppermute(block, 'seq', [(i, i ^ bit) for i in range(size)])  68.7 us
    pallas_call x8, Pallas kernels, paired_products(): pl.pallas_call(functools.partial(paired_kernel, len(arrived), joined), gr...  36.3 us
    pallas_call x2, Pallas kernels, attention(): pl.pallas_call(functools.partial(attention_kernel, groups, depth), grid=(...  25.1 us
    ppermute x7, starting transfers between devices, shifted(): lax.ppermute(block, 'seq', [(i, i + distance) for i in range(size) if 0 <...  16.8 us
    pallas_call x1, Pallas kernels, input_term(): pl.pallas_call(term_kernel, grid=(parts,), in_specs=grads + weights, out_...  16.7 us
    ppermute x13, starting transfers between devices, swapped(): return lax.ppermute(block, 'seq', [(i, i ^ bit) for i in range(size)])  14.1 us
    pallas_call x1, Pallas kernels, arranged(): pl.pallas_call(arrange_kernel, grid_spec=pltpu.PrefetchScalarGridSpec(num...  7.87 us
  transfers between devices with their start and end apart: 21, of which 12 were waited for; matrix products, arithmetic and copies ran while one was open for 3% of the time, Pallas kernels for 32%

profile of v2, /device:TPU:0, one launch (start us, length us, event | category | flops | bytes accessed | tf_op | source)
XLA Modules:
  0.0 218.5 jit_solution(62543909574452933)
XLA Ops:
  7.2 1.1 slice_bitcast_fusion.6
  9.1 5.7 %collective-permute-start.12 = (bf16[2,512,256]{2,1,0:T(8,128)(2,1)}, bf16[2,512,256]{2,1,0:T(8,128)(2,1)}, u32[]{:S(2)}, u32[]{:S(2)}) collective-permute-start(bf16[2,512,256]{2,1,0:T(8,128)(2,1)} %pad_maximum_fusion.1.refs_2_), channel_id=1, source_target_pairs={{0,8},{4,12},{8,16},{12,20},{16,24},{20,28},{1,9},{5,13},{9,17},{1... | collective-permute-start | bytes 1572872 | tf_op jit(solution)/shard_map/ppermute | solution.py:259
  14.8 1.2 broadcast_xor_fusion.order_ref
  16.0 7.9 %arranged_input.1 = (bf16[4,672,512]{2,1,0:T(8,128)(2,1)}, bf16[4,672,512]{2,1,0:T(8,128)(2,1)S(1)}) custom-call(s32[8]{0:T(128)} %broadcast_xor_fusion.order_ref, bf16[512,5376]{1,0:T(8,128)(2,1)} %x_ref), custom_call_target="tpu_custom_call" | custom-call | tf_op jit(solution)/shard_map/arranged_input/pallas_call | solution.py:159
  24.7 3.4 %collective-permute-start.14 = (bf16[2,512,256]{2,1,0:T(8,128)(2,1)}, bf16[2,512,256]{2,1,0:T(8,128)(2,1)}, u32[]{:S(2)}, u32[]{:S(2)}) collective-permute-start(bf16[2,512,256]{2,1,0:T(8,128)(2,1)} %pad_maximum_fusion.2.refs_2_), channel_id=1, source_target_pairs={{0,8},{4,12},{8,16},{12,20},{16,24},{20,28},{1,9},{5,13},{9,17},{1... | collective-permute-start | bytes 1572872 | tf_op jit(solution)/shard_map/ppermute | solution.py:259
  28.1 2.1 collective-permute-start.15
  30.5 1.7 collective-permute-start.13
  34.6 12.5 %attention_grads.2 = (bf16[512,512]{1,0:T(8,128)(2,1)S(1)}, bf16[2,512,256]{2,1,0:T(8,128)(2,1)}, bf16[2,512,256]{2,1,0:T(8,128)(2,1)}, f32[2,512,256]{2,1,0:T(8,128)}) custom-call(s32[1,512]{1,0:T(1,128)} %subtract_add_fusion.lowest_ref, bf16[512,1024]{1,0:T(8,128)(2,1)} %q_ref.3, bf16[512,1024]{1,0:T(8,128)(2,1)} %g_ref.3, ...), custom_call_target="tpu_custom_call" | custom-call | tf_op jit(solution)/shard_map/attention_grads/pallas_call | solution.py:112
  47.1 1.3 collective-permute-start.16
  48.4 1.5 collective-permute-start.17
  49.9 12.6 %attention_grads.3 = (bf16[512,512]{1,0:T(8,128)(2,1)S(1)}, bf16[2,512,256]{2,1,0:T(8,128)(2,1)}, bf16[2,512,256]{2,1,0:T(8,128)(2,1)}, f32[2,512,256]{2,1,0:T(8,128)}) custom-call(s32[1,512]{1,0:T(1,128)} %subtract_add_fusion.lowest_ref, bf16[512,1024]{1,0:T(8,128)(2,1)} %q_ref.3, bf16[512,1024]{1,0:T(8,128)(2,1)} %g_ref.3, ...), custom_call_target="tpu_custom_call" | custom-call | tf_op jit(solution)/shard_map/attention_grads/pallas_call | solution.py:112
  62.5 1.6 collective-permute-start.18
  64.1 1.3 collective-permute-start.19
  65.4 1.1 pad_maximum_fusion.dq_ref
  66.5 3.2 %collective-permute-done.17 = bf16[2,512,256]{2,1,0:T(8,128)(2,1)} collective-permute-done((bf16[2,512,256]{2,1,0:T(8,128)(2,1)}, bf16[2,512,256]{2,1,0:T(8,128)(2,1)}, u32[]{:S(2)}, u32[]{:S(2)}) %collective-permute-start.17) | collective-permute-done | bytes 524320 | tf_op jit(solution)/shard_map/ppermute | solution.py:259
  69.7 2.1 add_convert_fusion.1
  71.9 14.0 %conditional.3 = (bf16[4,672,512]{2,1,0:T(8,128)(2,1)}, bf16[4,672,512]{2,1,0:T(8,128)(2,1)}) conditional(s32[]{:T(128)} %convert_element_type.28, () %tuple.55, (bf16[4,672,512]{2,1,0:T(8,128)(2,1)S(1)}, bf16[512,512]{1,0:T(8,128)(2,1)S(1)}, bf16[512,512]{1,0:T(8,128)(2,1)S(1)}) %tuple.75), branch_computations={%region_2.3_spmd, %region_3.4_spmd} | conditional | bytes 22020192 | solution.py:320
  71.9 4.6 %projection_products.8 = (bf16[4,672,512]{2,1,0:T(8,128)(2,1)}, bf16[4,672,512]{2,1,0:T(8,128)(2,1)}) custom-call(bf16[4,672,512]{2,1,0:T(8,128)(2,1)S(1)} %get-tuple-element.30.refs_0_.refs_2_, bf16[512,512]{1,0:T(8,128)(2,1)S(1)} %get-tuple-element.31.refs_1_, bf16[4,672,512]{2,1,0:T(8,128)(2,1)S(1)} %get-tuple-element.30.refs_0_.refs_2_, ...), custom_call_target="tpu_custom_call" | custom-call | tf_op jit(solution)/shard_map/cond/branch_1_fun/projection_products/pallas_call | solution.py:217
  77.0 4.9 %collective-permute-done = bf16[4,672,512]{2,1,0:T(8,128)(2,1)} collective-permute-done((bf16[4,672,512]{2,1,0:T(8,128)(2,1)}, bf16[4,672,512]{2,1,0:T(8,128)(2,1)}, u32[]{:S(2)}, u32[]{:S(2)}) %collective-permute-start) | collective-permute-done | bytes 2752544 | tf_op jit(solution)/shard_map/cond/branch_1_fun/ppermute | solution.py:254
  82.0 3.9 %collective-permute-done.1 = bf16[4,672,512]{2,1,0:T(8,128)(2,1)} collective-permute-done((bf16[4,672,512]{2,1,0:T(8,128)(2,1)}, bf16[4,672,512]{2,1,0:T(8,128)(2,1)}, u32[]{:S(2)}, u32[]{:S(2)}) %collective-permute-start.1) | collective-permute-done | bytes 2752544 | tf_op jit(solution)/shard_map/cond/branch_1_fun/ppermute | solution.py:254
  85.9 1.1 slice_bitcast_fusion.1
  87.0 1.7 add_convert_fusion
  89.6 16.7 %input_term.1 = bf16[4,1344,512]{2,1,0:T(8,128)(2,1)} custom-call(bf16[512,1024]{1,0:T(8,128)(2,1)} %pad_maximum_fusion.dq_ref, bf16[512,512]{1,0:T(8,128)(2,1)S(1)} %pad_maximum_fusion.3.dk_ref, bf16[512,512]{1,0:T(8,128)(2,1)S(1)} %pad_maximum_fusion.4.dv_ref, bf16[5376,1024]{1,0:T(8,128)(2,1)} %wq_ref.1, bf16[5376,512]{1,0:T(8,128)(2,1)} %wk_ref.1, ...), custom_call_target="tpu_custom_call" | custom-call | tf_op jit(solution)/shard_map/input_term/pallas_call | solution.py:241
  106.3 105.4 %conditional.4 = (bf16[672,1024]{1,0:T(8,128)(2,1)}, bf16[672,512]{1,0:T(8,128)(2,1)}, bf16[672,512]{1,0:T(8,128)(2,1)}) conditional(s32[]{:T(128)} %convert_element_type.28, () %tuple.60, (bf16[4,672,512]{2,1,0:T(8,128)(2,1)}, bf16[4,672,512]{2,1,0:T(8,128)(2,1)}, bf16[4,672,512]{2,1,0:T(8,128)(2,1)S(1)}, bf16[512,512]{1,0:T(8,128)(2,1)}, ...), branch_computations={%region_5.6_spmd, %region_6.9_spmd} | conditional | flops 1 | bytes 77857424 | solution.py:320
  106.3 4.3 %projection_products.10 = (bf16[2,672,512]{2,1,0:T(8,128)(2,1)}, bf16[2,672,512]{2,1,0:T(8,128)(2,1)}) custom-call(bf16[4,672,512]{2,1,0:T(8,128)(2,1)S(1)} %get-tuple-element.40.refs_0_.refs_3_.refs_4_.refs_5_, bf16[512,512]{1,0:T(8,128)(2,1)} %get-tuple-element.41.refs_1_, bf16[4,672,512]{2,1,0:T(8,128)(2,1)} %get-tuple-element.74.refs_2_, ...), custom_call_target="tpu_custom_call" | custom-call | tf_op jit(solution)/shard_map/cond/branch_1_fun/projection_products/pallas_call | solution.py:217
  110.6 2.6 %collective-permute-start.4 = (bf16[2,672,512]{2,1,0:T(8,128)(2,1)}, bf16[2,672,512]{2,1,0:T(8,128)(2,1)}, u32[]{:S(2)}, u32[]{:S(2)}) collective-permute-start(bf16[2,672,512]{2,1,0:T(8,128)(2,1)} %get-tuple-element.47), channel_id=1, source_target_pairs={{0,8},{4,12},{8,0},{12,4},{16,24},{20,28},{24,16},{28,20},{1,9},{5... | collective-permute-start | bytes 4128776 | tf_op jit(solution)/shard_map/cond/branch_1_fun/ppermute | solution.py:254
  113.2 3.0 %collective-permute-start.5 = (bf16[2,672,512]{2,1,0:T(8,128)(2,1)}, bf16[2,672,512]{2,1,0:T(8,128)(2,1)}, u32[]{:S(2)}, u32[]{:S(2)}) collective-permute-start(bf16[2,672,512]{2,1,0:T(8,128)(2,1)} %get-tuple-element.48), channel_id=1, source_target_pairs={{0,16},{4,20},{8,24},{12,28},{16,0},{20,4},{24,8},{28,12},{1,17},{... | collective-permute-start | bytes 4128776 | tf_op jit(solution)/shard_map/cond/branch_1_fun/ppermute | solution.py:254
  116.3 16.7 %conditional = (bf16[4,672,512]{2,1,0:T(8,128)(2,1)}, bf16[4,672,512]{2,1,0:T(8,128)(2,1)}) conditional(s32[]{:T(128)} %convert_element_type.7, () %tuple.24, (bf16[4,672,512]{2,1,0:T(8,128)(2,1)}, bf16[512,512]{1,0:T(8,128)(2,1)S(1)}, bf16[512,512]{1,0:T(8,128)(2,1)}) %tuple.26), branch_computations={%region_7.7_spmd, %region_8.8_spmd} | conditional | bytes 22020192 | solution.py:320
  116.3 7.3 %projection_products.9 = (bf16[4,672,512]{2,1,0:T(8,128)(2,1)}, bf16[4,672,512]{2,1,0:T(8,128)(2,1)}) custom-call(bf16[4,672,512]{2,1,0:T(8,128)(2,1)} %get-tuple-element.35.refs_0_.refs_2_, bf16[512,512]{1,0:T(8,128)(2,1)S(1)} %get-tuple-element.36.refs_1_, bf16[4,672,512]{2,1,0:T(8,128)(2,1)} %get-tuple-element.35.refs_0_.refs_2_, ...), custom_call_target="tpu_custom_call" | custom-call | tf_op jit(solution)/shard_map/cond/branch_1_fun/cond/branch_1_fun/projection_products/pallas_call | solution.py:217
  124.1 4.9 %collective-permute-done.2 = bf16[4,672,512]{2,1,0:T(8,128)(2,1)} collective-permute-done((bf16[4,672,512]{2,1,0:T(8,128)(2,1)}, bf16[4,672,512]{2,1,0:T(8,128)(2,1)}, u32[]{:S(2)}, u32[]{:S(2)}) %collective-permute-start.2) | collective-permute-done | bytes 2752544 | tf_op jit(solution)/shard_map/cond/branch_1_fun/cond/branch_1_fun/ppermute | solution.py:254
  129.0 3.9 %collective-permute-done.3 = bf16[4,672,512]{2,1,0:T(8,128)(2,1)} collective-permute-done((bf16[4,672,512]{2,1,0:T(8,128)(2,1)}, bf16[4,672,512]{2,1,0:T(8,128)(2,1)}, u32[]{:S(2)}, u32[]{:S(2)}) %collective-permute-start.3) | collective-permute-done | bytes 2752544 | tf_op jit(solution)/shard_map/cond/branch_1_fun/cond/branch_1_fun/ppermute | solution.py:254
  133.0 4.2 %projection_products.11 = (bf16[2,672,512]{2,1,0:T(8,128)(2,1)}, bf16[2,672,512]{2,1,0:T(8,128)(2,1)}) custom-call(bf16[4,672,512]{2,1,0:T(8,128)(2,1)S(1)} %get-tuple-element.40.refs_0_.refs_3_.refs_4_.refs_5_, bf16[512,512]{1,0:T(8,128)(2,1)S(1)} %get-tuple-element.54.refs_1_, bf16[4,672,512]{2,1,0:T(8,128)(2,1)} %get-tuple-element.80.refs_2_, ...), custom_call_target="tpu_custom_call" | custom-call | tf_op jit(solution)/shard_map/cond/branch_1_fun/projection_products/pallas_call | solution.py:217
  137.7 7.0 %collective-permute-done.4.refs_3_ = bf16[2,672,512]{2,1,0:T(8,128)(2,1)} collective-permute-done((bf16[2,672,512]{2,1,0:T(8,128)(2,1)}, bf16[2,672,512]{2,1,0:T(8,128)(2,1)}, u32[]{:S(2)}, u32[]{:S(2)}) %collective-permute-start.4) | collective-permute-done | bytes 1376288 | tf_op jit(solution)/shard_map/cond/branch_1_fun/ppermute | solution.py:254
  144.6 3.0 %collective-permute-done.5.refs_7_.refs_8_ = bf16[2,672,512]{2,1,0:T(8,128)(2,1)} collective-permute-done((bf16[2,672,512]{2,1,0:T(8,128)(2,1)}, bf16[2,672,512]{2,1,0:T(8,128)(2,1)}, u32[]{:S(2)}, u32[]{:S(2)}) %collective-permute-start.5) | collective-permute-done | bytes 1376288 | tf_op jit(solution)/shard_map/cond/branch_1_fun/ppermute | solution.py:254
  147.6 3.6 %projection_products.12 = (bf16[1,672,512]{2,1,0:T(8,128)(2,1)}, bf16[1,672,512]{2,1,0:T(8,128)(2,1)}) custom-call(bf16[4,672,512]{2,1,0:T(8,128)(2,1)S(1)} %get-tuple-element.40.refs_0_.refs_3_.refs_4_.refs_5_, bf16[512,512]{1,0:T(8,128)(2,1)S(1)} %copy-done.4, bf16[4,672,512]{2,1,0:T(8,128)(2,1)} %get-tuple-element.74.refs_2_, ...), custom_call_target="tpu_custom_call" | custom-call | tf_op jit(solution)/shard_map/cond/branch_1_fun/projection_products/pallas_call | solution.py:217
  151.2 2.1 collective-permute-start.6
  153.3 20.7 %collective-permute-done.8.refs_3_ = bf16[2,672,512]{2,1,0:T(8,128)(2,1)S(1)} collective-permute-done((bf16[2,672,512]{2,1,0:T(8,128)(2,1)}, bf16[2,672,512]{2,1,0:T(8,128)(2,1)S(1)}, u32[]{:S(2)}, u32[]{:S(2)}) %collective-permute-start.8) | collective-permute-done | bytes 1376288 | tf_op jit(solution)/shard_map/cond/branch_1_fun/ppermute | solution.py:254
  174.0 3.0 %collective-permute-done.9.refs_7_.refs_8_ = bf16[2,672,512]{2,1,0:T(8,128)(2,1)S(1)} collective-permute-done((bf16[2,672,512]{2,1,0:T(8,128)(2,1)}, bf16[2,672,512]{2,1,0:T(8,128)(2,1)S(1)}, u32[]{:S(2)}, u32[]{:S(2)}) %collective-permute-start.9) | collective-permute-done | bytes 1376288 | tf_op jit(solution)/shard_map/cond/branch_1_fun/ppermute | solution.py:254
  177.0 1.1 copy-done.8
  178.1 3.7 %projection_products.13 = (bf16[1,672,512]{2,1,0:T(8,128)(2,1)}, bf16[1,672,512]{2,1,0:T(8,128)(2,1)}) custom-call(bf16[4,672,512]{2,1,0:T(8,128)(2,1)S(1)} %get-tuple-element.40.refs_0_.refs_3_.refs_4_.refs_5_, bf16[512,512]{1,0:T(8,128)(2,1)S(1)} %get-tuple-element.54.refs_1_, bf16[4,672,512]{2,1,0:T(8,128)(2,1)} %get-tuple-element.80.refs_2_, ...), custom_call_target="tpu_custom_call" | custom-call | tf_op jit(solution)/shard_map/cond/branch_1_fun/projection_products/pallas_call | solution.py:217
  181.8 2.1 collective-permute-start.10
  183.8 1.1 collective-permute-start.11
  184.9 6.9 %collective-permute-done.6.refs_4_ = bf16[1,672,512]{2,1,0:T(8,128)(2,1)} collective-permute-done((bf16[1,672,512]{2,1,0:T(8,128)(2,1)}, bf16[1,672,512]{2,1,0:T(8,128)(2,1)}, u32[]{:S(2)}, u32[]{:S(2)}) %collective-permute-start.6) | collective-permute-done | bytes 688160 | tf_op jit(solution)/shard_map/cond/branch_1_fun/ppermute | solution.py:254
  191.8 4.3 %projection_products.14 = bf16[672,1024]{1,0:T(8,128)(2,1)} custom-call(bf16[4,672,512]{2,1,0:T(8,128)(2,1)S(1)} %get-tuple-element.40.refs_0_.refs_3_.refs_4_.refs_5_, bf16[512,512]{1,0:T(8,128)(2,1)S(1)} %copy-done.4, bf16[4,672,512]{2,1,0:T(8,128)(2,1)} %get-tuple-element.74.refs_2_, bf16[2,672,512]{2,1,0:T(8,128)(2,1)} %collective-permute-done.4.refs_3_, ...), custom_call_target="tpu_custom_call" | custom-call | tf_op jit(solution)/shard_map/cond/branch_1_fun/projection_products/pallas_call | solution.py:217
  196.2 9.6 %collective-permute-done.10.refs_4_ = bf16[1,672,512]{2,1,0:T(8,128)(2,1)S(1)} collective-permute-done((bf16[1,672,512]{2,1,0:T(8,128)(2,1)}, bf16[1,672,512]{2,1,0:T(8,128)(2,1)S(1)}, u32[]{:S(2)}, u32[]{:S(2)}) %collective-permute-start.10) | collective-permute-done | bytes 688160 | tf_op jit(solution)/shard_map/cond/branch_1_fun/ppermute | solution.py:254
  205.8 0.9 copy-done.10
  206.6 0.9 copy-done.11
  207.5 4.2 %projection_products.15 = (bf16[1,672,512]{2,1,0:T(8,128)(2,1)}, bf16[1,672,512]{2,1,0:T(8,128)(2,1)}) custom-call(bf16[4,672,512]{2,1,0:T(8,128)(2,1)S(1)} %get-tuple-element.40.refs_0_.refs_3_.refs_4_.refs_5_, bf16[512,512]{1,0:T(8,128)(2,1)S(1)} %get-tuple-element.54.refs_1_, bf16[4,672,512]{2,1,0:T(8,128)(2,1)} %get-tuple-element.80.refs_2_, ...), custom_call_target="tpu_custom_call" | custom-call | tf_op jit(solution)/shard_map/cond/branch_1_fun/projection_products/pallas_call | solution.py:217
  (61 shorter events, 6.9 us)
Async XLA Ops:
  7.2 204.5 %reduce-scatter.2.cloned.1.call-start = ((), (), s32[]{:S(2)}) async-start(), calls=%async_computation.1 | async-start | bytes 6881280 | tf_op jit(solution)/shard_map/reduce_scatter | solution.py:394
  9.1 21.3 %collective-permute-start.12 = (bf16[2,512,256]{2,1,0:T(8,128)(2,1)}, bf16[2,512,256]{2,1,0:T(8,128)(2,1)}, u32[]{:S(2)}, u32[]{:S(2)}) collective-permute-start(bf16[2,512,256]{2,1,0:T(8,128)(2,1)} %pad_maximum_fusion.1.refs_2_), channel_id=1, source_target_pairs={{0,8},{4,12},{8,16},{12,20},{16,24},{20,28},{1,9},{5,13},{9,17},{1... | collective-permute-start | bytes 1572872 | tf_op jit(solution)/shard_map/ppermute | solution.py:259
  15.9 7.9 %copy-start.13 = (bf16[512,512]{1,0:T(8,128)(2,1)S(1)}, bf16[512,512]{1,0:T(8,128)(2,1)}, u32[]{:S(2)}) copy-start(bf16[512,512]{1,0:T(8,128)(2,1)} %param.19) | copy-start | bytes 1572868
  16.0 7.9 %copy-start.14 = (bf16[512,512]{1,0:T(8,128)(2,1)S(1)}, bf16[512,512]{1,0:T(8,128)(2,1)}, u32[]{:S(2)}) copy-start(bf16[512,512]{1,0:T(8,128)(2,1)} %param.18) | copy-start | bytes 1572868
  16.0 14.3 %copy-start.15 = (s32[8]{0:T(128)S(1)}, s32[8]{0:T(128)}, u32[]{:S(2)}) copy-start(s32[8]{0:T(128)} %param.24) | copy-start | bytes 100
  24.7 25.2 %collective-permute-start.14 = (bf16[2,512,256]{2,1,0:T(8,128)(2,1)}, bf16[2,512,256]{2,1,0:T(8,128)(2,1)}, u32[]{:S(2)}, u32[]{:S(2)}) collective-permute-start(bf16[2,512,256]{2,1,0:T(8,128)(2,1)} %pad_maximum_fusion.2.refs_2_), channel_id=1, source_target_pairs={{0,8},{4,12},{8,16},{12,20},{16,24},{20,28},{1,9},{5,13},{9,17},{1... | collective-permute-start | bytes 1572872 | tf_op jit(solution)/shard_map/ppermute | solution.py:259
  28.1 21.8 %collective-permute-start.15 = (bf16[2,512,256]{2,1,0:T(8,128)(2,1)}, bf16[2,512,256]{2,1,0:T(8,128)(2,1)}, u32[]{:S(2)}, u32[]{:S(2)}) collective-permute-start(bf16[2,512,256]{2,1,0:T(8,128)(2,1)} %pad_maximum_fusion.2.refs_2_), channel_id=1, source_target_pairs={{0,4},{4,8},{8,12},{12,16},{16,20},{20,24},{24,28},{1,5},{5,9},{9,... | collective-permute-start | bytes 1572872 | tf_op jit(solution)/shard_map/ppermute | solution.py:259
  30.5 3.3 %collective-permute-start.13 = (bf16[2,512,256]{2,1,0:T(8,128)(2,1)S(1)}, bf16[2,512,256]{2,1,0:T(8,128)(2,1)S(1)}, u32[]{:S(2)}, u32[]{:S(2)}) collective-permute-start(bf16[2,512,256]{2,1,0:T(8,128)(2,1)S(1)} %broadcast_select_fusion), channel_id=1, source_target_pairs={{0,4},{4,0},{8,12},{12,8},{16,20},{20,16},{24,28},{28,24},{1,5},{5... | collective-permute-start | bytes 1572872 | tf_op jit(solution)/shard_map/ppermute | solution.py:254
  33.8 0.8 copy-start.12
  47.1 24.8 %copy-start.3 = (bf16[512,512]{1,0:T(8,128)(2,1)}, bf16[512,512]{1,0:T(8,128)(2,1)S(1)}, u32[]{:S(2)}) copy-start(bf16[512,512]{1,0:T(8,128)(2,1)S(1)} %get-tuple-element.174) | copy-start | bytes 1572868
  47.1 19.4 %collective-permute-start.16 = (bf16[2,512,256]{2,1,0:T(8,128)(2,1)}, bf16[2,512,256]{2,1,0:T(8,128)(2,1)}, u32[]{:S(2)}, u32[]{:S(2)}) collective-permute-start(bf16[2,512,256]{2,1,0:T(8,128)(2,1)} %get-tuple-element.148), channel_id=1, source_target_pairs={{4,0},{8,4},{12,8},{16,12},{20,16},{24,20},{28,24},{5,1},{9,5},{13... | collective-permute-start | bytes 1572872 | tf_op jit(solution)/shard_map/ppermute | solution.py:259
  48.4 21.3 %collective-permute-start.17 = (bf16[2,512,256]{2,1,0:T(8,128)(2,1)}, bf16[2,512,256]{2,1,0:T(8,128)(2,1)}, u32[]{:S(2)}, u32[]{:S(2)}) collective-permute-start(bf16[2,512,256]{2,1,0:T(8,128)(2,1)} %get-tuple-element.147), channel_id=1, source_target_pairs={{8,0},{12,4},{16,8},{20,12},{24,16},{28,20},{9,1},{13,5},{17,9},{2... | collective-permute-start | bytes 1572872 | tf_op jit(solution)/shard_map/ppermute | solution.py:259
  49.9 19.8 %copy-start.9 = (f32[2,512,256]{2,1,0:T(8,128)S(1)}, f32[2,512,256]{2,1,0:T(8,128)}, u32[]{:S(2)}) copy-start(f32[2,512,256]{2,1,0:T(8,128)} %get-tuple-element.157) | copy-start | bytes 3145732
  62.5 9.3 %copy-start.5 = (bf16[512,512]{1,0:T(8,128)(2,1)}, bf16[512,512]{1,0:T(8,128)(2,1)S(1)}, u32[]{:S(2)}) copy-start(bf16[512,512]{1,0:T(8,128)(2,1)S(1)} %get-tuple-element.175) | copy-start | bytes 1572868
  62.5 9.3 %copy-start = (bf16[4,672,512]{2,1,0:T(8,128)(2,1)S(1)}, bf16[4,672,512]{2,1,0:T(8,128)(2,1)}, u32[]{:S(2)}) copy-start(bf16[4,672,512]{2,1,0:T(8,128)(2,1)} %get-tuple-element.176) | copy-start | bytes 8257540
  62.5 24.4 %collective-permute-start.18 = (bf16[2,512,256]{2,1,0:T(8,128)(2,1)}, bf16[2,512,256]{2,1,0:T(8,128)(2,1)}, u32[]{:S(2)}, u32[]{:S(2)}) collective-permute-start(bf16[2,512,256]{2,1,0:T(8,128)(2,1)} %get-tuple-element.155), channel_id=1, source_target_pairs={{4,0},{8,4},{12,8},{16,12},{20,16},{24,20},{28,24},{5,1},{9,5},{13... | collective-permute-start | bytes 1572872 | tf_op jit(solution)/shard_map/ppermute | solution.py:259
  64.1 22.9 %collective-permute-start.19 = (bf16[2,512,256]{2,1,0:T(8,128)(2,1)}, bf16[2,512,256]{2,1,0:T(8,128)(2,1)}, u32[]{:S(2)}, u32[]{:S(2)}) collective-permute-start(bf16[2,512,256]{2,1,0:T(8,128)(2,1)} %get-tuple-element.154), channel_id=1, source_target_pairs={{8,0},{12,4},{16,8},{20,12},{24,16},{28,20},{9,1},{13,5},{17,9},{2... | collective-permute-start | bytes 1572872 | tf_op jit(solution)/shard_map/ppermute | solution.py:259
  76.5 5.4 %collective-permute-start = (bf16[4,672,512]{2,1,0:T(8,128)(2,1)}, bf16[4,672,512]{2,1,0:T(8,128)(2,1)}, u32[]{:S(2)}, u32[]{:S(2)}) collective-permute-start(bf16[4,672,512]{2,1,0:T(8,128)(2,1)} %get-tuple-element.33), channel_id=1, source_target_pairs={{0,4},{4,0},{8,12},{12,8},{16,20},{20,16},{24,28},{28,24},{1,5},{5... | collective-permute-start | bytes 8257544 | tf_op jit(solution)/shard_map/cond/branch_1_fun/ppermute | solution.py:254
  76.5 9.4 %collective-permute-start.1 = (bf16[4,672,512]{2,1,0:T(8,128)(2,1)}, bf16[4,672,512]{2,1,0:T(8,128)(2,1)}, u32[]{:S(2)}, u32[]{:S(2)}) collective-permute-start(bf16[4,672,512]{2,1,0:T(8,128)(2,1)} %get-tuple-element.34), channel_id=1, source_target_pairs={{0,4},{4,0},{8,12},{12,8},{16,20},{20,16},{24,28},{28,24},{1,5},{5... | collective-permute-start | bytes 8257544 | tf_op jit(solution)/shard_map/cond/branch_1_fun/ppermute | solution.py:254
  88.8 0.8 copy-start.1
  110.6 34.0 %collective-permute-start.4 = (bf16[2,672,512]{2,1,0:T(8,128)(2,1)}, bf16[2,672,512]{2,1,0:T(8,128)(2,1)}, u32[]{:S(2)}, u32[]{:S(2)}) collective-permute-start(bf16[2,672,512]{2,1,0:T(8,128)(2,1)} %get-tuple-element.47), channel_id=1, source_target_pairs={{0,8},{4,12},{8,0},{12,4},{16,24},{20,28},{24,16},{28,20},{1,9},{5... | collective-permute-start | bytes 4128776 | tf_op jit(solution)/shard_map/cond/branch_1_fun/ppermute | solution.py:254
  113.2 34.4 %collective-permute-start.5 = (bf16[2,672,512]{2,1,0:T(8,128)(2,1)}, bf16[2,672,512]{2,1,0:T(8,128)(2,1)}, u32[]{:S(2)}, u32[]{:S(2)}) collective-permute-start(bf16[2,672,512]{2,1,0:T(8,128)(2,1)} %get-tuple-element.48), channel_id=1, source_target_pairs={{0,16},{4,20},{8,24},{12,28},{16,0},{20,4},{24,8},{28,12},{1,17},{... | collective-permute-start | bytes 4128776 | tf_op jit(solution)/shard_map/cond/branch_1_fun/ppermute | solution.py:254
  123.6 5.4 %collective-permute-start.2 = (bf16[4,672,512]{2,1,0:T(8,128)(2,1)}, bf16[4,672,512]{2,1,0:T(8,128)(2,1)}, u32[]{:S(2)}, u32[]{:S(2)}) collective-permute-start(bf16[4,672,512]{2,1,0:T(8,128)(2,1)} %get-tuple-element.38), channel_id=1, source_target_pairs={{0,4},{4,0},{8,12},{12,8},{16,20},{20,16},{24,28},{28,24},{1,5},{5... | collective-permute-start | bytes 8257544 | tf_op jit(solution)/shard_map/cond/branch_1_fun/cond/branch_1_fun/ppermute | solution.py:254
  123.6 9.4 %collective-permute-start.3 = (bf16[4,672,512]{2,1,0:T(8,128)(2,1)}, bf16[4,672,512]{2,1,0:T(8,128)(2,1)}, u32[]{:S(2)}, u32[]{:S(2)}) collective-permute-start(bf16[4,672,512]{2,1,0:T(8,128)(2,1)} %get-tuple-element.39), channel_id=1, source_target_pairs={{0,4},{4,0},{8,12},{12,8},{16,20},{20,16},{24,28},{28,24},{1,5},{5... | collective-permute-start | bytes 8257544 | tf_op jit(solution)/shard_map/cond/branch_1_fun/cond/branch_1_fun/ppermute | solution.py:254
  133.0 14.6 %copy-start.4 = (bf16[512,512]{1,0:T(8,128)(2,1)S(1)}, bf16[512,512]{1,0:T(8,128)(2,1)}, u32[]{:S(2)}) copy-start(bf16[512,512]{1,0:T(8,128)(2,1)} %get-tuple-element.41.refs_1_) | copy-start | bytes 1572868 | tf_op jit(solution)/shard_map/cond
  133.0 14.6 %copy-start.6 = (bf16[512,512]{1,0:T(8,128)(2,1)S(1)}, bf16[512,512]{1,0:T(8,128)(2,1)}, u32[]{:S(2)}) copy-start(bf16[512,512]{1,0:T(8,128)(2,1)} %get-tuple-element.45.refs_4_.refs_5_.refs_6_) | copy-start | bytes 1572868 | tf_op jit(solution)/shard_map/cond
  137.2 36.8 %collective-permute-start.8 = (bf16[2,672,512]{2,1,0:T(8,128)(2,1)}, bf16[2,672,512]{2,1,0:T(8,128)(2,1)S(1)}, u32[]{:S(2)}, u32[]{:S(2)}) collective-permute-start(bf16[2,672,512]{2,1,0:T(8,128)(2,1)} %get-tuple-element.60), channel_id=1, source_target_pairs={{0,8},{4,12},{8,0},{12,4},{16,24},{20,28},{24,16},{28,20},{1,9},{5... | collective-permute-start | bytes 4128776 | tf_op jit(solution)/shard_map/cond/branch_1_fun/ppermute | solution.py:254
  137.2 40.9 %copy-start.2 = (bf16[512,512]{1,0:T(8,128)(2,1)S(1)}, bf16[512,512]{1,0:T(8,128)(2,1)}, u32[]{:S(2)}) copy-start(bf16[512,512]{1,0:T(8,128)(2,1)} %get-tuple-element.55.refs_4_.refs_5_.refs_6_) | copy-start | bytes 1572868 | tf_op jit(solution)/shard_map/cond
  137.2 39.8 %collective-permute-start.9 = (bf16[2,672,512]{2,1,0:T(8,128)(2,1)}, bf16[2,672,512]{2,1,0:T(8,128)(2,1)S(1)}, u32[]{:S(2)}, u32[]{:S(2)}) collective-permute-start(bf16[2,672,512]{2,1,0:T(8,128)(2,1)} %get-tuple-element.61), channel_id=1, source_target_pairs={{0,16},{4,20},{8,24},{12,28},{16,0},{20,4},{24,8},{28,12},{1,17},{... | collective-permute-start | bytes 4128776 | tf_op jit(solution)/shard_map/cond/branch_1_fun/ppermute | solution.py:254
  151.2 40.6 %collective-permute-start.6 = (bf16[1,672,512]{2,1,0:T(8,128)(2,1)}, bf16[1,672,512]{2,1,0:T(8,128)(2,1)}, u32[]{:S(2)}, u32[]{:S(2)}) collective-permute-start(bf16[1,672,512]{2,1,0:T(8,128)(2,1)} %get-tuple-element.66), channel_id=1, source_target_pairs={{0,16},{4,20},{8,24},{12,28},{16,0},{20,4},{24,8},{28,12},{1,17},{... | collective-permute-start | bytes 2064392 | tf_op jit(solution)/shard_map/cond/branch_1_fun/ppermute | solution.py:254
  153.3 38.5 %collective-permute-start.7 = (bf16[1,672,512]{2,1,0:T(8,128)(2,1)}, bf16[1,672,512]{2,1,0:T(8,128)(2,1)}, u32[]{:S(2)}, u32[]{:S(2)}) collective-permute-start(bf16[1,672,512]{2,1,0:T(8,128)(2,1)} %get-tuple-element.67), channel_id=1, source_target_pairs={{0,8},{4,12},{8,0},{12,4},{16,24},{20,28},{24,16},{28,20},{1,9},{5... | collective-permute-start | bytes 2064392 | tf_op jit(solution)/shard_map/cond/branch_1_fun/ppermute | solution.py:254
  174.0 3.0 %copy-start.7 = (bf16[2,672,512]{2,1,0:T(8,128)(2,1)}, bf16[2,672,512]{2,1,0:T(8,128)(2,1)S(1)}, u32[]{:S(2)}) copy-start(bf16[2,672,512]{2,1,0:T(8,128)(2,1)S(1)} %collective-permute-done.8.refs_3_) | copy-start | bytes 4128772 | tf_op jit(solution)/shard_map/cond
  177.0 1.1 copy-start.8
  181.8 24.0 %collective-permute-start.10 = (bf16[1,672,512]{2,1,0:T(8,128)(2,1)}, bf16[1,672,512]{2,1,0:T(8,128)(2,1)S(1)}, u32[]{:S(2)}, u32[]{:S(2)}) collective-permute-start(bf16[1,672,512]{2,1,0:T(8,128)(2,1)} %get-tuple-element.72), channel_id=1, source_target_pairs={{0,16},{4,20},{8,24},{12,28},{16,0},{20,4},{24,8},{28,12},{1,17},{... | collective-permute-start | bytes 2064392 | tf_op jit(solution)/shard_map/cond/branch_1_fun/ppermute | solution.py:254
  183.8 21.9 %collective-permute-start.11 = (bf16[1,672,512]{2,1,0:T(8,128)(2,1)}, bf16[1,672,512]{2,1,0:T(8,128)(2,1)S(1)}, u32[]{:S(2)}, u32[]{:S(2)}) collective-permute-start(bf16[1,672,512]{2,1,0:T(8,128)(2,1)} %get-tuple-element.73), channel_id=1, source_target_pairs={{0,8},{4,12},{8,0},{12,4},{16,24},{20,28},{24,16},{28,20},{1,9},{5... | collective-permute-start | bytes 2064392 | tf_op jit(solution)/shard_map/cond/branch_1_fun/ppermute | solution.py:254
  205.8 0.9 copy-start.10
  206.6 0.9 copy-start.11
Sparse Core Ops, SparseCore 0:
  106.4 101.8 reduce-scatter.1

commit v3 on v2

--- a/solution.py
+++ b/solution.py
@@ -15,7 +15,6 @@
 TILE = 256
 SCALE = (D // H) ** (-0.5)
 FAR = -1e30
-TOKEN_PARTS = 1
 VMEM_BYTES = 56 * 1024 * 1024
 
 NT = (((1,), (1,)), ((), ()))
@@ -225,28 +224,50 @@
     )(*operands)
 
 
-def term_kernel(dq_ref, dk_ref, dv_ref, wq_ref, wk_ref, wv_ref, out_ref):
-    out_ref[0] = (
-        dot(wq_ref[...], dq_ref[...], NT)
-        + dot(wk_ref[...], dk_ref[...], NT)
-        + dot(wv_ref[...], dv_ref[...], NT)
-    ).astype(jnp.bfloat16)
-
-
-def input_term(dq, dk, dv, w_query, w_key, w_value, parts, piece, pieces):
-    rows = dq.shape[0] // pieces
+def term_kernel(sets, *refs):
+    dq_refs, refs = refs[:sets], refs[sets:]
+    parts, refs = refs[: 3 * sets], refs[3 * sets :]
+    wq_ref, wk_ref, wv_ref, out_ref, dk_ref, dv_ref = refs
+
+    @pl.when(pl.program_id(0) == 0)
+    def _():
+        for c in range(sets):
+            own_ref, one_ref, two_ref = parts[3 * c : 3 * c + 3]
+            cols = own_ref.shape[2]
+            at = slice(c * cols, (c + 1) * cols)
+            for which, total_ref in enumerate((dk_ref, dv_ref)):
+                total = own_ref[which] + one_ref[which].astype(jnp.float32)
+                total = total + two_ref[which].astype(jnp.float32)
+                total_ref[:, at] = total.astype(jnp.bfloat16)
+
+    value = dot(wk_ref[...], dk_ref[...], NT) + dot(wv_ref[...], dv_ref[...], NT)
+    for c, dq_ref in enumerate(dq_refs):
+        cols = dq_ref.shape[1]
+        value = value + dot(wq_ref[:, c * cols : (c + 1) * cols], dq_ref[...], NT)
+    out_ref[0] = value.astype(jnp.bfloat16)
+
+
+def input_term(dqs, halos, w_query, w_key, w_value, parts):
+    sets, rows = len(dqs), dqs[0].shape[0]
     width = w_query.shape[0] // parts
-    grads = [pl.BlockSpec((rows, a.shape[1]), lambda p: (piece, 0)) for a in (dq, dk, dv)]
-    weights = [pl.BlockSpec((width, w.shape[1]), lambda p: (p, 0)) for w in (w_query, w_key, w_value)]
+    whole = [*dqs, *(part for halo in halos for part in halo)]
+    weights = (w_query, w_key, w_value)
+    key_cols = w_key.shape[1]
+
+    def constant(array):
+        return pl.BlockSpec(array.shape, lambda p: (0,) * array.ndim)
+
+    total = jax.ShapeDtypeStruct((rows, key_cols), jnp.bfloat16)
     return pl.pallas_call(
-        term_kernel,
+        functools.partial(term_kernel, sets),
         grid=(parts,),
-        in_specs=grads + weights,
-        out_specs=pl.BlockSpec((1, width, rows), lambda p: (p, 0, 0)),
-        out_shape=jax.ShapeDtypeStruct((parts, width, rows), jnp.bfloat16),
+        in_specs=[constant(a) for a in whole]
+        + [pl.BlockSpec((width, w.shape[1]), lambda p: (p, 0)) for w in weights],
+        out_specs=[pl.BlockSpec((1, width, rows), lambda p: (p, 0, 0)), constant(total), constant(total)],
+        out_shape=[jax.ShapeDtypeStruct((parts, width, rows), jnp.bfloat16), total, total],
         compiler_params=pltpu.CompilerParams(vmem_limit_bytes=VMEM_BYTES),
         name="input_term",
-    )(dq, dk, dv, w_query, w_key, w_value)
+    )(*whole, *weights)
 
 
 def swapped(block, bit):
@@ -279,31 +300,33 @@
 
 
 class Scattered:
-    def __init__(self, inputs, offsets, grads, beside, bits):
-        self.inputs, self.offsets, self.grads = inputs, offsets, list(grads)
+    def __init__(self, offsets, bits):
+        self.offsets = offsets
         self.bits = [list(bits), list(bits[::-1])]
         self.alive = [list(offsets)] * 2
-        self.arrived = [[(list(offsets), b)] for b in beside]
-
-    def summed(self, order, leaving, joined=False):
-        arrived = order.after(*[[array for _, array in held] for held in self.arrived])
+        self.held = [[list(offsets)], [list(offsets)]]
+
+    def summed(self, leaving, inputs, grads, arrived, joined=False):
         sides = []
         for i in range(2):
-            at = [[held.index(o) for o in leaving[i]] for held, _ in self.arrived[i]]
+            at = [[held.index(o) for o in leaving[i]] for held in self.held[i]]
             at.insert(0, [self.offsets.index(o) for o in leaving[i]])
-            sides.append((self.inputs, self.grads[i], arrived[i], at))
-        return order.did(paired_products(sides, joined))
-
-    def step(self, order):
+            sides.append((inputs, grads[i], [a[i] for a in arrived], at))
+        return paired_products(sides, joined)
+
+    def leaving(self, inputs, grads, arrived):
+        leaving = [[o for o in self.alive[i] if o & self.bits[i][0]] for i in range(2)]
+        return self.summed(leaving, inputs, grads, arrived)
+
+    def step(self, blocks):
         bits = [b.pop(0) for b in self.bits]
-        leaving = [[o for o in alive if o & bit] for alive, bit in zip(self.alive, bits)]
-        self.alive = [[o for o in alive if not o & bit] for alive, bit in zip(self.alive, bits)]
-        blocks = self.summed(order, leaving)
         for i in range(2):
-            self.arrived[i].append(([o ^ bits[i] for o in leaving[i]], swapped(blocks[i], bits[i])))
-
-    def result(self, order, joined=False):
-        out = self.summed(order, [[0], [0]], joined)
+            self.held[i].append([o ^ bits[i] for o in self.alive[i] if o & bits[i]])
+            self.alive[i] = [o for o in self.alive[i] if not o & bits[i]]
+        return [swapped(block, bit) for block, bit in zip(blocks, bits)]
+
+    def result(self, inputs, grads, arrived, joined=False):
+        out = self.summed([[0], [0]], inputs, grads, arrived, joined)
         return out if joined else [o[0] for o in out]
 
 
@@ -314,10 +337,17 @@
 
 
 def kept_together(always, work, *operands):
+    shapes = []
+
+    def traced(*operands):
+        out = work(*operands)
+        shapes.append(jax.tree.map(lambda a: jax.ShapeDtypeStruct(a.shape, a.dtype), out))
+        return out
+
     def nothing(*operands):
-        return jax.tree.map(lambda a: jnp.zeros(a.shape, a.dtype), jax.eval_shape(work, *operands))
-
-    return lax.cond(always, work, nothing, *operands)
+        return jax.tree.map(lambda a: jnp.zeros(a.shape, a.dtype), shapes[0])
+
+    return lax.cond(always, traced, nothing, *operands)
 
 
 def on_device(layer_input, query, keys, values, out_grad, w_query, w_key, w_value, proof_lengths):
@@ -369,48 +399,62 @@
             attention(lowest, query, out_grad, seen, c * per_set, groups)
         )
         dqs.append(dq)
-        halos.append((own_grad, shifted(halo_one, -1), shifted(halo_two, -2)))
-    dq = jnp.concatenate(dqs, axis=1)
-    half = dq.shape[1] // 2
-    if sets != 2:
-        dqs = [dq[:, :half], dq[:, half:]]
+        if c < sets - 1:
+            halos.append((own_grad, shifted(halo_one, -1), shifted(halo_two, -2)))
+    if sets == 2:
+        halves = dqs
+    else:
+        half = dqs[0].shape[1] // 2
+        halves = [dqs[0][:, :half], dqs[0][:, half:]]
 
     always = proof_lengths[0] > 0
     bits = [1 << j for j in range(1, steps)]
-    totals = []
-    for c, parts in enumerate(halos):
-        if c == sets - 1:
-            args = order.after(odds, *dqs)
-            beside = order.did(kept_together(always, beside_products, *args))
-        parts = order.after(*parts)
-        total = sum(part.astype(jnp.float32) for part in parts).astype(jnp.bfloat16)
-        totals.append(order.did(total))
-    dk = jnp.concatenate([t[0] for t in totals], axis=1)
-    dv = jnp.concatenate([t[1] for t in totals], axis=1)
-    input_grads = []
-    for i in range(TOKEN_PARTS):
-        grads = order.after(dq, dk, dv)
-        term = order.did(input_term(*grads, w_query, w_key, w_value, head_size, i, TOKEN_PARTS))
-        input_grads.append(lax.psum_scatter(term, "head", scatter_dimension=0, tiled=False))
-    input_grad = jnp.concatenate(input_grads, axis=1).T
-
-    def projections(odds, evens, dqs, beside, dk, dv):
+    query_sum, other_sum = Scattered(even, bits), Scattered(even, bits)
+
+    def first_products(odds, evens, *dqs):
+        beside = beside_products(odds, *dqs)
+        return beside, query_sum.leaving(evens, dqs, [beside])
+
+    def last_halo(halo_one, halo_two, *args):
         order = Order()
-        query_sum = Scattered(evens, even, dqs, beside, bits)
-        query_sum.step(order)
+        arrived = shifted(halo_one, -1), shifted(halo_two, -2)
+        products = order.did(kept_together(always, first_products, *args))
+        return order.after(*arrived), products
+
+    *args, early = order.after(halo_one, halo_two, odds, evens, *halves, [two for _, _, two in halos])
+    halos = [(own, one, two) for (own, one, _), two in zip(halos, early)]
+    arrived, (beside, blocks) = order.did(kept_together(always, last_halo, *args))
+    halos.append((own_grad, *arrived))
+    dqs, halos = order.after(dqs, halos)
+    term, dk, dv = order.did(input_term(dqs, halos, w_query, w_key, w_value, head_size))
+
+    def projections(odds, evens, dqs, beside, blocks, dk, dv):
+        order = Order()
+        arrived = [beside, query_sum.step(blocks)]
         args = order.after(odds, dk, dv)
         beside = order.did(kept_together(always, beside_products, *args))
-        other_sum = Scattered(evens, even, [dk, dv], beside, bits)
-        other_sum.step(order)
+        others = order.did(other_sum.leaving(evens, [dk, dv], [beside]))
+        other_arrived = [beside, other_sum.step(others)]
         while query_sum.bits[0]:
-            query_sum.step(order)
-            other_sum.step(order)
-        wq_grad = query_sum.result(order, True)
-        return (wq_grad, *other_sum.result(order))
-
-    parts = order.after(odds, evens, dqs, beside, dk, dv)
-    grads = kept_together(always, projections, *parts)
-    return (input_grad, *grads)
+            held = order.after(arrived)
+            blocks = order.did(query_sum.leaving(evens, dqs, held))
+            arrived = arrived + [query_sum.step(blocks)]
+            held = order.after(other_arrived)
+            blocks = order.did(other_sum.leaving(evens, [dk, dv], held))
+            other_arrived = other_arrived + [other_sum.step(blocks)]
+        held = order.after(arrived)
+        wq_grad = order.did(query_sum.result(evens, dqs, held, True))
+        held = order.after(other_arrived)
+        return (wq_grad, *other_sum.result(evens, [dk, dv], held))
+
+    def finish(term, *args):
+        grads = kept_together(always, projections, *args)
+        total = lax.psum_scatter(term, "head", scatter_dimension=0, tiled=False)
+        return (total, *grads)
+
+    args = order.after(odds, evens, halves, beside, blocks, dk, dv)
+    input_grad, *grads = finish(term, *args)
+    return (input_grad.T, *grads)
 
 
 def solution(mesh):

time: 219 us -> 217 us (level)
  other arithmetic: 8.82 us -> 3.83 us
  Pallas kernels: 86 us -> 89.5 us
    convert_element_type x2 -> x0, other arithmetic: 3.83 us -> none  [on_device(): sum((part.astype(jnp.float32) for part in parts)).astype(jnp.bfloat16)]
    pallas_call x8, Pallas kernels: 36.3 us -> 38.5 us  [paired_products(): pl.pallas_call(functools.partial(paired_kernel, len(arrived), joined), gr...]
  transfers between devices with their start and end apart: 21 -> 21, of which waited for: 12 -> 13; matrix products, arithmetic and copies ran while one was open for 3% -> 1% of each run, Pallas kernels for 32% -> 33%
where the time goes in v3:
time: 217 us; the launch traced here: 216 us
  Pallas kernels  89.5 us (41%)
  waiting for transfers between devices  70.7 us (33%)
  starting transfers between devices  32.1 us (15%)
  between operations  14.2 us (7%)
  local copies, waits for them, and re-layouts  5.58 us (3%)
  other arithmetic  3.83 us (2%)
    ppermute x13, waiting for transfers between devices, swapped(): return lax.ppermute(block, 'seq', [(i, i ^ bit) for i in range(size)])  68.2 us
    pallas_call x8, Pallas kernels, paired_products(): pl.pallas_call(functools.partial(paired_kernel, len(arrived), joined), gr...  38.5 us
    pallas_call x2, Pallas kernels, attention(): pl.pallas_call(functools.partial(attention_kernel, groups, depth), grid=(...  24.9 us
    pallas_call x1, Pallas kernels, input_term(): pl.pallas_call(functools.partial(term_kernel, sets), grid=(parts,), in_sp...  18.2 us
    ppermute x7, starting transfers between devices, shifted(): lax.ppermute(block, 'seq', [(i, i + distance) for i in range(size) if 0 <...  16.5 us
    ppermute x13, starting transfers between devices, swapped(): return lax.ppermute(block, 'seq', [(i, i ^ bit) for i in range(size)])  15.6 us
    pallas_call x1, Pallas kernels, arranged(): pl.pallas_call(arrange_kernel, grid_spec=pltpu.PrefetchScalarGridSpec(num...  7.87 us
  transfers between devices with their start and end apart: 21, of which 13 were waited for; matrix products, arithmetic and copies ran while one was open for 1% of the time, Pallas kernels for 33%

profile of v3, /device:TPU:0, one launch (start us, length us, event | category | flops | bytes accessed | tf_op | source)
XLA Modules:
  0.0 215.9 jit_solution(16458357365811113068)
XLA Ops:
  7.2 1.1 slice_bitcast_fusion.2
  9.1 5.7 %collective-permute-start.14 = (bf16[2,512,256]{2,1,0:T(8,128)(2,1)}, bf16[2,512,256]{2,1,0:T(8,128)(2,1)}, u32[]{:S(2)}, u32[]{:S(2)}) collective-permute-start(bf16[2,512,256]{2,1,0:T(8,128)(2,1)} %pad_maximum_fusion.refs_2_), channel_id=1, source_target_pairs={{0,8},{4,12},{8,16},{12,20},{16,24},{20,28},{1,9},{5,13},{9,17},{1... | collective-permute-start | bytes 1572872 | tf_op jit(solution)/shard_map/ppermute | solution.py:280
  14.8 1.2 broadcast_xor_fusion.order_ref
  15.9 7.9 %arranged_input.1 = (bf16[4,672,512]{2,1,0:T(8,128)(2,1)}, bf16[4,672,512]{2,1,0:T(8,128)(2,1)S(1)}) custom-call(s32[8]{0:T(128)} %broadcast_xor_fusion.order_ref, bf16[512,5376]{1,0:T(8,128)(2,1)} %x_ref), custom_call_target="tpu_custom_call" | custom-call | tf_op jit(solution)/shard_map/arranged_input/pallas_call | solution.py:158
  23.9 0.9 pad_maximum_fusion.1.refs_2_
  24.8 3.4 %collective-permute-start.16 = (bf16[2,512,256]{2,1,0:T(8,128)(2,1)}, bf16[2,512,256]{2,1,0:T(8,128)(2,1)}, u32[]{:S(2)}, u32[]{:S(2)}) collective-permute-start(bf16[2,512,256]{2,1,0:T(8,128)(2,1)} %pad_maximum_fusion.1.refs_2_), channel_id=1, source_target_pairs={{0,8},{4,12},{8,16},{12,20},{16,24},{20,28},{1,9},{5,13},{9,17},{1... | collective-permute-start | bytes 1572872 | tf_op jit(solution)/shard_map/ppermute | solution.py:280
  28.2 2.1 collective-permute-start.17
  30.5 1.7 collective-permute-start.15
  33.0 0.8 collective-permute-done.15.refs_1_
  34.6 12.6 %attention_grads.2 = (bf16[512,512]{1,0:T(8,128)(2,1)S(1)}, bf16[2,512,256]{2,1,0:T(8,128)(2,1)}, bf16[2,512,256]{2,1,0:T(8,128)(2,1)}, f32[2,512,256]{2,1,0:T(8,128)}) custom-call(s32[1,512]{1,0:T(1,128)} %subtract_add_fusion.lowest_ref, bf16[512,1024]{1,0:T(8,128)(2,1)} %q_ref.3, bf16[512,1024]{1,0:T(8,128)(2,1)} %g_ref.3, ...), custom_call_target="tpu_custom_call" | custom-call | tf_op jit(solution)/shard_map/attention_grads/pallas_call | solution.py:111
  47.2 1.3 collective-permute-start.19
  48.5 1.5 collective-permute-start.18
  50.0 12.3 %attention_grads.3 = (bf16[512,512]{1,0:T(8,128)(2,1)}, bf16[2,512,256]{2,1,0:T(8,128)(2,1)}, bf16[2,512,256]{2,1,0:T(8,128)(2,1)}, f32[2,512,256]{2,1,0:T(8,128)}) custom-call(s32[1,512]{1,0:T(1,128)} %subtract_add_fusion.lowest_ref, bf16[512,1024]{1,0:T(8,128)(2,1)} %q_ref.3, bf16[512,1024]{1,0:T(8,128)(2,1)} %g_ref.3, ...), custom_call_target="tpu_custom_call" | custom-call | tf_op jit(solution)/shard_map/attention_grads/pallas_call | solution.py:111
  62.4 1.3 collective-permute-done.19.refs_4_
  63.6 23.9 %conditional.4 = (bf16[2,512,256]{2,1,0:T(8,128)(2,1)}, bf16[2,512,256]{2,1,0:T(8,128)(2,1)}, bf16[4,672,512]{2,1,0:T(8,128)(2,1)}, bf16[4,672,512]{2,1,0:T(8,12...) conditional(s32[]{:T(128)} %convert_element_type.10, () %tuple.62, ...), branch_computations={%region_2.3_spmd, %region_3.6_spmd} | conditional | flops 1 | bytes 28311856 | solution.py:350
  63.6 1.3 collective-permute-start.2
  64.9 1.3 collective-permute-start.3
  66.2 21.3 %conditional = (bf16[4,672,512]{2,1,0:T(8,128)(2,1)}, bf16[4,672,512]{2,1,0:T(8,128)(2,1)}, bf16[2,672,512]{2,1,0:T(8,128)(2,1)}, bf16[2,672,512]{2,1,0:T(8,128)(2,1)}) conditional(s32[]{:T(128)} %convert_element_type.3, () %tuple.28, (bf16[4,672,512]{2,1,0:T(8,128)(2,1)}, bf16[512,512]{1,0:T(8,128)(2,1)S(1)}, bf16[512,512]{1,0:T(8,128)(2,1)}, ...), branch_computations={%region_4.4_spmd, %region_5.5_spmd} | conditional | bytes 24117388 | solution.py:350
  66.2 7.1 %projection_products.8 = (bf16[4,672,512]{2,1,0:T(8,128)(2,1)}, bf16[4,672,512]{2,1,0:T(8,128)(2,1)}) custom-call(bf16[4,672,512]{2,1,0:T(8,128)(2,1)} %get-tuple-element.50.refs_0_.refs_2_, bf16[512,512]{1,0:T(8,128)(2,1)S(1)} %get-tuple-element.51.refs_1_, bf16[4,672,512]{2,1,0:T(8,128)(2,1)} %get-tuple-element.50.refs_0_.refs_2_, ...), custom_call_target="tpu_custom_call" | custom-call | tf_op jit(solution)/shard_map/cond/branch_1_fun/cond/branch_1_fun/projection_products/pallas_call | solution.py:216
  73.4 1.1 collective-permute-start
  74.5 5.1 %collective-permute-done.refs_2_ = bf16[4,672,512]{2,1,0:T(8,128)(2,1)} collective-permute-done((bf16[4,672,512]{2,1,0:T(8,128)(2,1)}, bf16[4,672,512]{2,1,0:T(8,128)(2,1)}, u32[]{:S(2)}, u32[]{:S(2)}) %collective-permute-start) | collective-permute-done | bytes 2752544 | tf_op jit(solution)/shard_map/cond/branch_1_fun/cond/branch_1_fun/ppermute | solution.py:275
  79.6 3.9 %collective-permute-done.1.refs_5_ = bf16[4,672,512]{2,1,0:T(8,128)(2,1)} collective-permute-done((bf16[4,672,512]{2,1,0:T(8,128)(2,1)}, bf16[4,672,512]{2,1,0:T(8,128)(2,1)}, u32[]{:S(2)}, u32[]{:S(2)}) %collective-permute-start.1) | collective-permute-done | bytes 2752544 | tf_op jit(solution)/shard_map/cond/branch_1_fun/cond/branch_1_fun/ppermute | solution.py:275
  83.5 4.1 %projection_products.9 = (bf16[2,672,512]{2,1,0:T(8,128)(2,1)}, bf16[2,672,512]{2,1,0:T(8,128)(2,1)}) custom-call(bf16[4,672,512]{2,1,0:T(8,128)(2,1)S(1)} %get-tuple-element.55.refs_0_.refs_3_, bf16[512,512]{1,0:T(8,128)(2,1)S(1)} %get-tuple-element.51.refs_1_, bf16[4,672,512]{2,1,0:T(8,128)(2,1)} %collective-permute-done.refs_2_, ...), custom_call_target="tpu_custom_call" | custom-call | tf_op jit(solution)/shard_map/cond/branch_1_fun/cond/branch_1_fun/projection_products/pallas_call | solution.py:216
  87.6 18.2 %input_term.1 = (bf16[4,1344,512]{2,1,0:T(8,128)(2,1)}, bf16[512,512]{1,0:T(8,128)(2,1)}, bf16[512,512]{1,0:T(8,128)(2,1)}) custom-call(bf16[512,512]{1,0:T(8,128)(2,1)S(1)} %get-tuple-element.230.refs_0_, bf16[512,512]{1,0:T(8,128)(2,1)} %get-tuple-element.231.refs_1_, f32[2,512,256]{2,1,0:T(8,128)} %get-tuple-element.213.refs_2_, ...), custom_call_target="tpu_custom_call" | custom-call | tf_op jit(solution)/shard_map/input_term/pallas_call | solution.py:261
  105.8 102.2 %conditional.5 = (bf16[672,1024]{1,0:T(8,128)(2,1)}, bf16[672,512]{1,0:T(8,128)(2,1)}, bf16[672,512]{1,0:T(8,128)(2,1)}) conditional(s32[]{:T(128)} %convert_element_type.10, () %tuple.65, (bf16[2,672,512]{2,1,0:T(8,128)(2,1)}, bf16[2,672,512]{2,1,0:T(8,128)(2,1)}, pred[]{:T(512)}, bf16[4,672,512]{2,1,0:T(8,128)(2,1)}, bf16[512,512]{1,0:T(8,128)(2,1)}, ...), branch_computations={%region_7.8_spmd, %region_8.11_spmd} | conditional | flops 1 | bytes 80609968 | solution.py:350
  105.8 2.8 %collective-permute-start.6 = (bf16[2,672,512]{2,1,0:T(8,128)(2,1)}, bf16[2,672,512]{2,1,0:T(8,128)(2,1)}, u32[]{:S(2)}, u32[]{:S(2)}) collective-permute-start(bf16[2,672,512]{2,1,0:T(8,128)(2,1)} %get-tuple-element.80), channel_id=1, source_target_pairs={{0,8},{4,12},{8,0},{12,4},{16,24},{20,28},{24,16},{28,20},{1,9},{5... | collective-permute-start | bytes 4128776 | tf_op jit(solution)/shard_map/cond/branch_1_fun/ppermute | solution.py:275
  108.6 4.2 %collective-permute-start.7 = (bf16[2,672,512]{2,1,0:T(8,128)(2,1)}, bf16[2,672,512]{2,1,0:T(8,128)(2,1)}, u32[]{:S(2)}, u32[]{:S(2)}) collective-permute-start(bf16[2,672,512]{2,1,0:T(8,128)(2,1)} %get-tuple-element.81), channel_id=1, source_target_pairs={{0,16},{4,20},{8,24},{12,28},{16,0},{20,4},{24,8},{28,12},{1,17},{... | collective-permute-start | bytes 4128776 | tf_op jit(solution)/shard_map/cond/branch_1_fun/ppermute | solution.py:275
  112.8 16.6 %conditional.1 = (bf16[4,672,512]{2,1,0:T(8,128)(2,1)}, bf16[4,672,512]{2,1,0:T(8,128)(2,1)}) conditional(s32[]{:T(128)} %convert_element_type.8, () %tuple.35, (bf16[4,672,512]{2,1,0:T(8,128)(2,1)}, bf16[512,512]{1,0:T(8,128)(2,1)}, bf16[512,512]{1,0:T(8,128)(2,1)}) %tuple.36), branch_computations={%region_9.9_spmd, %region_10.10_spmd} | conditional | bytes 22020192 | solution.py:350
  112.8 7.2 %projection_products.10 = (bf16[4,672,512]{2,1,0:T(8,128)(2,1)}, bf16[4,672,512]{2,1,0:T(8,128)(2,1)}) custom-call(bf16[4,672,512]{2,1,0:T(8,128)(2,1)} %get-tuple-element.71.refs_0_.refs_2_, bf16[512,512]{1,0:T(8,128)(2,1)} %get-tuple-element.72.refs_1_, bf16[4,672,512]{2,1,0:T(8,128)(2,1)} %get-tuple-element.71.refs_0_.refs_2_, ...), custom_call_target="tpu_custom_call" | custom-call | tf_op jit(solution)/shard_map/cond/branch_1_fun/cond/branch_1_fun/projection_products/pallas_call | solution.py:216
  120.5 4.9 %collective-permute-done.4 = bf16[4,672,512]{2,1,0:T(8,128)(2,1)} collective-permute-done((bf16[4,672,512]{2,1,0:T(8,128)(2,1)}, bf16[4,672,512]{2,1,0:T(8,128)(2,1)}, u32[]{:S(2)}, u32[]{:S(2)}) %collective-permute-start.4) | collective-permute-done | bytes 2752544 | tf_op jit(solution)/shard_map/cond/branch_1_fun/cond/branch_1_fun/ppermute | solution.py:275
  125.4 3.9 %collective-permute-done.5 = bf16[4,672,512]{2,1,0:T(8,128)(2,1)} collective-permute-done((bf16[4,672,512]{2,1,0:T(8,128)(2,1)}, bf16[4,672,512]{2,1,0:T(8,128)(2,1)}, u32[]{:S(2)}, u32[]{:S(2)}) %collective-permute-start.5) | collective-permute-done | bytes 2752544 | tf_op jit(solution)/shard_map/cond/branch_1_fun/cond/branch_1_fun/ppermute | solution.py:275
  129.4 4.4 %projection_products.11 = (bf16[2,672,512]{2,1,0:T(8,128)(2,1)}, bf16[2,672,512]{2,1,0:T(8,128)(2,1)}) custom-call(bf16[4,672,512]{2,1,0:T(8,128)(2,1)S(1)} %get-tuple-element.76.refs_0_.refs_3_.refs_4_.refs_5_, bf16[512,512]{1,0:T(8,128)(2,1)} %get-tuple-element.82.refs_1_, bf16[4,672,512]{2,1,0:T(8,128)(2,1)} %get-tuple-element.109.refs_2_, ...), custom_call_target="tpu_custom_call" | custom-call | tf_op jit(solution)/shard_map/cond/branch_1_fun/projection_products/pallas_call | solution.py:216
  133.8 6.1 %collective-permute-done.6.refs_3_ = bf16[2,672,512]{2,1,0:T(8,128)(2,1)} collective-permute-done((bf16[2,672,512]{2,1,0:T(8,128)(2,1)}, bf16[2,672,512]{2,1,0:T(8,128)(2,1)}, u32[]{:S(2)}, u32[]{:S(2)}) %collective-permute-start.6) | collective-permute-done | bytes 1376288 | tf_op jit(solution)/shard_map/cond/branch_1_fun/ppermute | solution.py:275
  139.9 4.1 %collective-permute-done.7.refs_7_.refs_8_ = bf16[2,672,512]{2,1,0:T(8,128)(2,1)} collective-permute-done((bf16[2,672,512]{2,1,0:T(8,128)(2,1)}, bf16[2,672,512]{2,1,0:T(8,128)(2,1)}, u32[]{:S(2)}, u32[]{:S(2)}) %collective-permute-start.7) | collective-permute-done | bytes 1376288 | tf_op jit(solution)/shard_map/cond/branch_1_fun/ppermute | solution.py:275
  144.1 3.7 %projection_products.12 = (bf16[1,672,512]{2,1,0:T(8,128)(2,1)}, bf16[1,672,512]{2,1,0:T(8,128)(2,1)}) custom-call(bf16[4,672,512]{2,1,0:T(8,128)(2,1)S(1)} %get-tuple-element.76.refs_0_.refs_3_.refs_4_.refs_5_, bf16[512,512]{1,0:T(8,128)(2,1)S(1)} %get-tuple-element.77.refs_1_, bf16[4,672,512]{2,1,0:T(8,128)(2,1)} %get-tuple-element.103.refs_2_, ...), custom_call_target="tpu_custom_call" | custom-call | tf_op jit(solution)/shard_map/cond/branch_1_fun/projection_products/pallas_call | solution.py:216
  147.8 2.1 collective-permute-start.8
  149.9 19.4 %collective-permute-done.10.refs_3_ = bf16[2,672,512]{2,1,0:T(8,128)(2,1)S(1)} collective-permute-done((bf16[2,672,512]{2,1,0:T(8,128)(2,1)}, bf16[2,672,512]{2,1,0:T(8,128)(2,1)S(1)}, u32[]{:S(2)}, u32[]{:S(2)}) %collective-permute-start.10) | collective-permute-done | bytes 1376288 | tf_op jit(solution)/shard_map/cond/branch_1_fun/ppermute | solution.py:275
  169.3 4.1 %collective-permute-done.11.refs_7_.refs_8_ = bf16[2,672,512]{2,1,0:T(8,128)(2,1)S(1)} collective-permute-done((bf16[2,672,512]{2,1,0:T(8,128)(2,1)}, bf16[2,672,512]{2,1,0:T(8,128)(2,1)S(1)}, u32[]{:S(2)}, u32[]{:S(2)}) %collective-permute-start.11) | collective-permute-done | bytes 1376288 | tf_op jit(solution)/shard_map/cond/branch_1_fun/ppermute | solution.py:275
  173.5 1.1 copy-done.5
  174.6 3.7 %projection_products.13 = (bf16[1,672,512]{2,1,0:T(8,128)(2,1)}, bf16[1,672,512]{2,1,0:T(8,128)(2,1)}) custom-call(bf16[4,672,512]{2,1,0:T(8,128)(2,1)S(1)} %get-tuple-element.76.refs_0_.refs_3_.refs_4_.refs_5_, bf16[512,512]{1,0:T(8,128)(2,1)S(1)} %copy-done.2, bf16[4,672,512]{2,1,0:T(8,128)(2,1)} %get-tuple-element.109.refs_2_, ...), custom_call_target="tpu_custom_call" | custom-call | tf_op jit(solution)/shard_map/cond/branch_1_fun/projection_products/pallas_call | solution.py:216
  178.2 2.1 collective-permute-start.12
  180.3 1.0 collective-permute-start.13
  181.3 6.9 %collective-permute-done.8.refs_4_ = bf16[1,672,512]{2,1,0:T(8,128)(2,1)S(1)} collective-permute-done((bf16[1,672,512]{2,1,0:T(8,128)(2,1)}, bf16[1,672,512]{2,1,0:T(8,128)(2,1)S(1)}, u32[]{:S(2)}, u32[]{:S(2)}) %collective-permute-start.8) | collective-permute-done | bytes 688160 | tf_op jit(solution)/shard_map/cond/branch_1_fun/ppermute | solution.py:275
  189.1 4.3 %projection_products.14 = bf16[672,1024]{1,0:T(8,128)(2,1)} custom-call(bf16[4,672,512]{2,1,0:T(8,128)(2,1)S(1)} %get-tuple-element.76.refs_0_.refs_3_.refs_4_.refs_5_, bf16[512,512]{1,0:T(8,128)(2,1)S(1)} %get-tuple-element.77.refs_1_, bf16[4,672,512]{2,1,0:T(8,128)(2,1)} %get-tuple-element.103.refs_2_, ...), custom_call_target="tpu_custom_call" | custom-call | tf_op jit(solution)/shard_map/cond/branch_1_fun/projection_products/pallas_call | solution.py:216
  193.3 8.8 %collective-permute-done.12.refs_4_ = bf16[1,672,512]{2,1,0:T(8,128)(2,1)S(1)} collective-permute-done((bf16[1,672,512]{2,1,0:T(8,128)(2,1)}, bf16[1,672,512]{2,1,0:T(8,128)(2,1)S(1)}, u32[]{:S(2)}, u32[]{:S(2)}) %collective-permute-start.12) | collective-permute-done | bytes 688160 | tf_op jit(solution)/shard_map/cond/branch_1_fun/ppermute | solution.py:275
  203.0 0.9 copy-done.8
  203.9 4.1 %projection_products.15 = (bf16[1,672,512]{2,1,0:T(8,128)(2,1)}, bf16[1,672,512]{2,1,0:T(8,128)(2,1)}) custom-call(bf16[4,672,512]{2,1,0:T(8,128)(2,1)S(1)} %get-tuple-element.76.refs_0_.refs_3_.refs_4_.refs_5_, bf16[512,512]{1,0:T(8,128)(2,1)S(1)} %copy-done.2, bf16[4,672,512]{2,1,0:T(8,128)(2,1)} %get-tuple-element.109.refs_2_, ...), custom_call_target="tpu_custom_call" | custom-call | tf_op jit(solution)/shard_map/cond/branch_1_fun/projection_products/pallas_call | solution.py:216
  207.9 1.1 reduce-scatter.2.cloned.1.call-done
  (49 shorter events, 5.0 us)
Async XLA Ops:
  7.2 201.9 %reduce-scatter.2.cloned.1.call-start = ((), (), s32[]{:S(2)}) async-start(), calls=%async_computation.1 | async-start | bytes 6881280 | tf_op jit(solution)/shard_map/reduce_scatter | solution.py:452
  9.1 21.3 %collective-permute-start.14 = (bf16[2,512,256]{2,1,0:T(8,128)(2,1)}, bf16[2,512,256]{2,1,0:T(8,128)(2,1)}, u32[]{:S(2)}, u32[]{:S(2)}) collective-permute-start(bf16[2,512,256]{2,1,0:T(8,128)(2,1)} %pad_maximum_fusion.refs_2_), channel_id=1, source_target_pairs={{0,8},{4,12},{8,16},{12,20},{16,24},{20,28},{1,9},{5,13},{9,17},{1... | collective-permute-start | bytes 1572872 | tf_op jit(solution)/shard_map/ppermute | solution.py:280
  15.9 7.9 %copy-start.10 = (bf16[512,512]{1,0:T(8,128)(2,1)S(1)}, bf16[512,512]{1,0:T(8,128)(2,1)}, u32[]{:S(2)}) copy-start(bf16[512,512]{1,0:T(8,128)(2,1)} %param.21) | copy-start | bytes 1572868
  15.9 7.9 %copy-start.11 = (bf16[512,512]{1,0:T(8,128)(2,1)S(1)}, bf16[512,512]{1,0:T(8,128)(2,1)}, u32[]{:S(2)}) copy-start(bf16[512,512]{1,0:T(8,128)(2,1)} %param.20) | copy-start | bytes 1572868
  15.9 14.3 %copy-start.12 = (s32[8]{0:T(128)S(1)}, s32[8]{0:T(128)}, u32[]{:S(2)}) copy-start(s32[8]{0:T(128)} %param.26) | copy-start | bytes 100
  24.8 25.3 %collective-permute-start.16 = (bf16[2,512,256]{2,1,0:T(8,128)(2,1)}, bf16[2,512,256]{2,1,0:T(8,128)(2,1)}, u32[]{:S(2)}, u32[]{:S(2)}) collective-permute-start(bf16[2,512,256]{2,1,0:T(8,128)(2,1)} %pad_maximum_fusion.1.refs_2_), channel_id=1, source_target_pairs={{0,8},{4,12},{8,16},{12,20},{16,24},{20,28},{1,9},{5,13},{9,17},{1... | collective-permute-start | bytes 1572872 | tf_op jit(solution)/shard_map/ppermute | solution.py:280
  28.2 21.9 %collective-permute-start.17 = (bf16[2,512,256]{2,1,0:T(8,128)(2,1)}, bf16[2,512,256]{2,1,0:T(8,128)(2,1)}, u32[]{:S(2)}, u32[]{:S(2)}) collective-permute-start(bf16[2,512,256]{2,1,0:T(8,128)(2,1)} %pad_maximum_fusion.1.refs_2_), channel_id=1, source_target_pairs={{0,4},{4,8},{8,12},{12,16},{16,20},{20,24},{24,28},{1,5},{5,9},{9,... | collective-permute-start | bytes 1572872 | tf_op jit(solution)/shard_map/ppermute | solution.py:280
  30.5 3.3 %collective-permute-start.15 = (bf16[2,512,256]{2,1,0:T(8,128)(2,1)S(1)}, bf16[2,512,256]{2,1,0:T(8,128)(2,1)S(1)}, u32[]{:S(2)}, u32[]{:S(2)}) collective-permute-start(bf16[2,512,256]{2,1,0:T(8,128)(2,1)S(1)} %broadcast_select_fusion), channel_id=1, source_target_pairs={{0,4},{4,0},{8,12},{12,8},{16,20},{20,16},{24,28},{28,24},{1,5},{5... | collective-permute-start | bytes 1572872 | tf_op jit(solution)/shard_map/ppermute | solution.py:275
  33.8 0.8 copy-start.9
  47.2 16.4 %collective-permute-start.19 = (bf16[2,512,256]{2,1,0:T(8,128)(2,1)}, bf16[2,512,256]{2,1,0:T(8,128)(2,1)}, u32[]{:S(2)}, u32[]{:S(2)}) collective-permute-start(bf16[2,512,256]{2,1,0:T(8,128)(2,1)} %get-tuple-element.188), channel_id=1, source_target_pairs={{8,0},{12,4},{16,8},{20,12},{24,16},{28,20},{9,1},{13,5},{17,9},{2... | collective-permute-start | bytes 1572872 | tf_op jit(solution)/shard_map/ppermute | solution.py:280
  48.5 39.1 %collective-permute-start.18 = (bf16[2,512,256]{2,1,0:T(8,128)(2,1)}, bf16[2,512,256]{2,1,0:T(8,128)(2,1)}, u32[]{:S(2)}, u32[]{:S(2)}) collective-permute-start(bf16[2,512,256]{2,1,0:T(8,128)(2,1)} %get-tuple-element.189), channel_id=1, source_target_pairs={{4,0},{8,4},{12,8},{16,12},{20,16},{24,20},{28,24},{5,1},{9,5},{13... | collective-permute-start | bytes 1572872 | tf_op jit(solution)/shard_map/ppermute | solution.py:280
  63.6 23.9 %collective-permute-start.2 = (bf16[2,512,256]{2,1,0:T(8,128)(2,1)}, bf16[2,512,256]{2,1,0:T(8,128)(2,1)}, u32[]{:S(2)}, u32[]{:S(2)}) collective-permute-start(bf16[2,512,256]{2,1,0:T(8,128)(2,1)} %get-tuple-element.58), channel_id=1, source_target_pairs={{4,0},{8,4},{12,8},{16,12},{20,16},{24,20},{28,24},{5,1},{9,5},{13... | collective-permute-start | bytes 1572872 | tf_op jit(solution)/shard_map/cond/branch_1_fun/ppermute | solution.py:280
  64.9 22.7 %collective-permute-start.3 = (bf16[2,512,256]{2,1,0:T(8,128)(2,1)}, bf16[2,512,256]{2,1,0:T(8,128)(2,1)}, u32[]{:S(2)}, u32[]{:S(2)}) collective-permute-start(bf16[2,512,256]{2,1,0:T(8,128)(2,1)} %get-tuple-element.59), channel_id=1, source_target_pairs={{8,0},{12,4},{16,8},{20,12},{24,16},{28,20},{9,1},{13,5},{17,9},{2... | collective-permute-start | bytes 1572872 | tf_op jit(solution)/shard_map/cond/branch_1_fun/ppermute | solution.py:280
  66.2 17.3 %copy-start = (bf16[512,512]{1,0:T(8,128)(2,1)S(1)}, bf16[512,512]{1,0:T(8,128)(2,1)}, u32[]{:S(2)}) copy-start(bf16[512,512]{1,0:T(8,128)(2,1)} %get-tuple-element.52.refs_3_.refs_4_) | copy-start | bytes 1572868 | tf_op jit(solution)/shard_map/cond/branch_1_fun/cond
  73.4 6.2 %collective-permute-start = (bf16[4,672,512]{2,1,0:T(8,128)(2,1)}, bf16[4,672,512]{2,1,0:T(8,128)(2,1)}, u32[]{:S(2)}, u32[]{:S(2)}) collective-permute-start(bf16[4,672,512]{2,1,0:T(8,128)(2,1)} %get-tuple-element.53), channel_id=1, source_target_pairs={{0,4},{4,0},{8,12},{12,8},{16,20},{20,16},{24,28},{28,24},{1,5},{5... | collective-permute-start | bytes 8257544 | tf_op jit(solution)/shard_map/cond/branch_1_fun/cond/branch_1_fun/ppermute | solution.py:275
  74.5 9.0 %collective-permute-start.1 = (bf16[4,672,512]{2,1,0:T(8,128)(2,1)}, bf16[4,672,512]{2,1,0:T(8,128)(2,1)}, u32[]{:S(2)}, u32[]{:S(2)}) collective-permute-start(bf16[4,672,512]{2,1,0:T(8,128)(2,1)} %get-tuple-element.54), channel_id=1, source_target_pairs={{0,4},{4,0},{8,12},{12,8},{16,20},{20,16},{24,28},{28,24},{1,5},{5... | collective-permute-start | bytes 8257544 | tf_op jit(solution)/shard_map/cond/branch_1_fun/cond/branch_1_fun/ppermute | solution.py:275
  105.8 34.1 %collective-permute-start.6 = (bf16[2,672,512]{2,1,0:T(8,128)(2,1)}, bf16[2,672,512]{2,1,0:T(8,128)(2,1)}, u32[]{:S(2)}, u32[]{:S(2)}) collective-permute-start(bf16[2,672,512]{2,1,0:T(8,128)(2,1)} %get-tuple-element.80), channel_id=1, source_target_pairs={{0,8},{4,12},{8,0},{12,4},{16,24},{20,28},{24,16},{28,20},{1,9},{5... | collective-permute-start | bytes 4128776 | tf_op jit(solution)/shard_map/cond/branch_1_fun/ppermute | solution.py:275
  108.6 35.5 %collective-permute-start.7 = (bf16[2,672,512]{2,1,0:T(8,128)(2,1)}, bf16[2,672,512]{2,1,0:T(8,128)(2,1)}, u32[]{:S(2)}, u32[]{:S(2)}) collective-permute-start(bf16[2,672,512]{2,1,0:T(8,128)(2,1)} %get-tuple-element.81), channel_id=1, source_target_pairs={{0,16},{4,20},{8,24},{12,28},{16,0},{20,4},{24,8},{28,12},{1,17},{... | collective-permute-start | bytes 4128776 | tf_op jit(solution)/shard_map/cond/branch_1_fun/ppermute | solution.py:275
  120.0 5.4 %collective-permute-start.4 = (bf16[4,672,512]{2,1,0:T(8,128)(2,1)}, bf16[4,672,512]{2,1,0:T(8,128)(2,1)}, u32[]{:S(2)}, u32[]{:S(2)}) collective-permute-start(bf16[4,672,512]{2,1,0:T(8,128)(2,1)} %get-tuple-element.74), channel_id=1, source_target_pairs={{0,4},{4,0},{8,12},{12,8},{16,20},{20,16},{24,28},{28,24},{1,5},{5... | collective-permute-start | bytes 8257544 | tf_op jit(solution)/shard_map/cond/branch_1_fun/cond/branch_1_fun/ppermute | solution.py:275
  120.0 9.4 %collective-permute-start.5 = (bf16[4,672,512]{2,1,0:T(8,128)(2,1)}, bf16[4,672,512]{2,1,0:T(8,128)(2,1)}, u32[]{:S(2)}, u32[]{:S(2)}) collective-permute-start(bf16[4,672,512]{2,1,0:T(8,128)(2,1)} %get-tuple-element.75), channel_id=1, source_target_pairs={{0,4},{4,0},{8,12},{12,8},{16,20},{20,16},{24,28},{28,24},{1,5},{5... | collective-permute-start | bytes 8257544 | tf_op jit(solution)/shard_map/cond/branch_1_fun/cond/branch_1_fun/ppermute | solution.py:275
  129.4 14.7 %copy-start.1 = (bf16[512,512]{1,0:T(8,128)(2,1)S(1)}, bf16[512,512]{1,0:T(8,128)(2,1)}, u32[]{:S(2)}) copy-start(bf16[512,512]{1,0:T(8,128)(2,1)} %get-tuple-element.92.refs_5_.refs_6_) | copy-start | bytes 1572868 | tf_op jit(solution)/shard_map/cond
  133.7 35.6 %collective-permute-start.10 = (bf16[2,672,512]{2,1,0:T(8,128)(2,1)}, bf16[2,672,512]{2,1,0:T(8,128)(2,1)S(1)}, u32[]{:S(2)}, u32[]{:S(2)}) collective-permute-start(bf16[2,672,512]{2,1,0:T(8,128)(2,1)} %get-tuple-element.88), channel_id=1, source_target_pairs={{0,8},{4,12},{8,0},{12,4},{16,24},{20,28},{24,16},{28,20},{1,9},{5... | collective-permute-start | bytes 4128776 | tf_op jit(solution)/shard_map/cond/branch_1_fun/ppermute | solution.py:275
  133.7 39.7 %collective-permute-start.11 = (bf16[2,672,512]{2,1,0:T(8,128)(2,1)}, bf16[2,672,512]{2,1,0:T(8,128)(2,1)S(1)}, u32[]{:S(2)}, u32[]{:S(2)}) collective-permute-start(bf16[2,672,512]{2,1,0:T(8,128)(2,1)} %get-tuple-element.89), channel_id=1, source_target_pairs={{0,16},{4,20},{8,24},{12,28},{16,0},{20,4},{24,8},{28,12},{1,17},{... | collective-permute-start | bytes 4128776 | tf_op jit(solution)/shard_map/cond/branch_1_fun/ppermute | solution.py:275
  144.1 30.5 %copy-start.2 = (bf16[512,512]{1,0:T(8,128)(2,1)S(1)}, bf16[512,512]{1,0:T(8,128)(2,1)}, u32[]{:S(2)}) copy-start(bf16[512,512]{1,0:T(8,128)(2,1)} %get-tuple-element.82.refs_1_) | copy-start | bytes 1572868 | tf_op jit(solution)/shard_map/cond
  144.1 30.5 %copy-start.3 = (bf16[512,512]{1,0:T(8,128)(2,1)S(1)}, bf16[512,512]{1,0:T(8,128)(2,1)}, u32[]{:S(2)}) copy-start(bf16[512,512]{1,0:T(8,128)(2,1)} %get-tuple-element.85.refs_4_.refs_5_.refs_6_) | copy-start | bytes 1572868 | tf_op jit(solution)/shard_map/cond
  147.8 40.4 %collective-permute-start.8 = (bf16[1,672,512]{2,1,0:T(8,128)(2,1)}, bf16[1,672,512]{2,1,0:T(8,128)(2,1)S(1)}, u32[]{:S(2)}, u32[]{:S(2)}) collective-permute-start(bf16[1,672,512]{2,1,0:T(8,128)(2,1)} %get-tuple-element.95), channel_id=1, source_target_pairs={{0,16},{4,20},{8,24},{12,28},{16,0},{20,4},{24,8},{28,12},{1,17},{... | collective-permute-start | bytes 2064392 | tf_op jit(solution)/shard_map/cond/branch_1_fun/ppermute | solution.py:275
  149.9 38.3 %collective-permute-start.9 = (bf16[1,672,512]{2,1,0:T(8,128)(2,1)}, bf16[1,672,512]{2,1,0:T(8,128)(2,1)}, u32[]{:S(2)}, u32[]{:S(2)}) collective-permute-start(bf16[1,672,512]{2,1,0:T(8,128)(2,1)} %get-tuple-element.96), channel_id=1, source_target_pairs={{0,8},{4,12},{8,0},{12,4},{16,24},{20,28},{24,16},{28,20},{1,9},{5... | collective-permute-start | bytes 2064392 | tf_op jit(solution)/shard_map/cond/branch_1_fun/ppermute | solution.py:275
  169.3 4.1 %copy-start.4 = (bf16[2,672,512]{2,1,0:T(8,128)(2,1)}, bf16[2,672,512]{2,1,0:T(8,128)(2,1)S(1)}, u32[]{:S(2)}) copy-start(bf16[2,672,512]{2,1,0:T(8,128)(2,1)S(1)} %collective-permute-done.10.refs_3_) | copy-start | bytes 4128772 | tf_op jit(solution)/shard_map/cond
  173.5 1.1 copy-start.5
  178.2 23.9 %collective-permute-start.12 = (bf16[1,672,512]{2,1,0:T(8,128)(2,1)}, bf16[1,672,512]{2,1,0:T(8,128)(2,1)S(1)}, u32[]{:S(2)}, u32[]{:S(2)}) collective-permute-start(bf16[1,672,512]{2,1,0:T(8,128)(2,1)} %get-tuple-element.101), channel_id=1, source_target_pairs={{0,16},{4,20},{8,24},{12,28},{16,0},{20,4},{24,8},{28,12},{1,17},{... | collective-permute-start | bytes 2064392 | tf_op jit(solution)/shard_map/cond/branch_1_fun/ppermute | solution.py:275
  180.3 21.9 %collective-permute-start.13 = (bf16[1,672,512]{2,1,0:T(8,128)(2,1)}, bf16[1,672,512]{2,1,0:T(8,128)(2,1)S(1)}, u32[]{:S(2)}, u32[]{:S(2)}) collective-permute-start(bf16[1,672,512]{2,1,0:T(8,128)(2,1)} %get-tuple-element.102), channel_id=1, source_target_pairs={{0,8},{4,12},{8,0},{12,4},{16,24},{20,28},{24,16},{28,20},{1,9},{5... | collective-permute-start | bytes 2064392 | tf_op jit(solution)/shard_map/cond/branch_1_fun/ppermute | solution.py:275
  188.2 0.8 copy-start.6
  202.1 0.8 copy-start.7
  203.0 0.9 copy-start.8
Sparse Core Ops, SparseCore 0:
  105.9 103.1 reduce-scatter.1

commit v4 on v3

--- a/solution.py
+++ b/solution.py
@@ -43,10 +43,10 @@
     key_iota = lax.broadcasted_iota(jnp.int32, (TILE, 1), 0)
     query_iota = lax.broadcasted_iota(jnp.int32, (1, TILE), 1)
     query_iota = jnp.concatenate([query_iota] * groups, axis=1)
-    for t in range(per_piece):
+    factor = SCALE * math.log2(math.e)
+
+    def scores(t):
         here = slice(t * TILE, (t + 1) * TILE)
-        score_ref = score_scr.at[t % 2]
-        pgrad_ref = pgrad_scr.at[t % 2]
         q2 = jnp.concatenate([q_ref[here, j * HD : (j + 1) * HD] for j in range(groups)], axis=0)
         g2 = jnp.concatenate([g_ref[here, j * HD : (j + 1) * HD] for j in range(groups)], axis=0)
         lowest = jnp.concatenate([lowest_ref[:, here]] * groups, axis=1)
@@ -57,28 +57,33 @@
             if b == behind:
                 allowed = allowed & (key_iota <= query_iota)
             s = jnp.where(allowed, s, FAR)
-            score_ref[b * TILE : (b + 1) * TILE, :] = s
+            score_scr[t % 2, b * TILE : (b + 1) * TILE, :] = s
             top = jnp.maximum(top, jnp.max(s, axis=0, keepdims=True))
-        factor = SCALE * math.log2(math.e)
+        return q2, g2, top
+
+    def weights(t, q2, g2, top):
         total = jnp.zeros((1, lanes), jnp.float32)
         delta = jnp.zeros((1, lanes), jnp.float32)
         for b in range(behind + 1):
             at = slice(b * TILE, (b + 1) * TILE)
-            weight = jnp.exp2((score_ref[at, :] - top) * factor)
+            weight = jnp.exp2((score_scr[t % 2, at, :] - top) * factor)
             pgrad = dot(key_tile(t + b, 1), g2, NT)
-            score_ref[at, :] = weight
-            pgrad_ref[at, :] = pgrad
+            score_scr[t % 2, at, :] = weight
+            pgrad_scr[t % 2, at, :] = pgrad
             total = total + jnp.sum(weight, axis=0, keepdims=True)
             delta = delta + jnp.sum(weight * pgrad, axis=0, keepdims=True)
         inverse = 1.0 / total
-        delta = delta * inverse
+        return q2, g2, inverse, delta * inverse
+
+    def grads(t, q2, g2, inverse, delta):
+        here = slice(t * TILE, (t + 1) * TILE)
         dq = jnp.zeros((HD, lanes), jnp.float32)
         for b in range(behind + 1):
             at = slice(b * TILE, (b + 1) * TILE)
             e = t + b
             to = slice(e * TILE, (e + 1) * TILE)
-            prob = score_ref[at, :] * inverse
-            sgrad = (prob * (pgrad_ref[at, :] - delta)).astype(jnp.bfloat16)
+            prob = score_scr[t % 2, at, :] * inverse
+            sgrad = (prob * (pgrad_scr[t % 2, at, :] - delta)).astype(jnp.bfloat16)
             dv = dot(prob.astype(jnp.bfloat16), g2)
             dk = dot(sgrad, q2)
             if t == 0 or b == behind:
@@ -91,6 +96,13 @@
         dq = (dq * SCALE).T.astype(jnp.bfloat16)
         for j in range(groups):
             dq_ref[here, j * HD : (j + 1) * HD] = dq[j * TILE : (j + 1) * TILE, :]
+
+    held = scores(0)
+    for t in range(per_piece):
+        held = weights(t, *held)
+        later = scores(t + 1) if t + 1 < per_piece else None
+        grads(t, *held)
+        held = later
     for d in range(depth):
         at = slice(d * rows, (d + 1) * rows)
         halo_refs[d][0] = (dk_scr[at, :] * SCALE).astype(jnp.bfloat16)

time: 217 us -> 215 us (level)
  no operation moved by 1% of the time
where the time goes in v4:
time: 215 us
  Pallas kernels  88.3 us (41%)
  waiting for transfers between devices  71.3 us (33%)
  starting transfers between devices  31.5 us (15%)
  between operations  14.2 us (7%)
  local copies, waits for them, and re-layouts  5.58 us (3%)
  other arithmetic  3.83 us (2%)
    ppermute x13, waiting for transfers between devices, swapped(): return lax.ppermute(block, 'seq', [(i, i ^ bit) for i in range(size)])  68.3 us
    pallas_call x8, Pallas kernels, paired_products(): pl.pallas_call(functools.partial(paired_kernel, len(arrived), joined), gr...  38.5 us
    pallas_call x2, Pallas kernels, attention(): pl.pallas_call(functools.partial(attention_kernel, groups, depth), grid=(...  23.7 us
    pallas_call x1, Pallas kernels, input_term(): pl.pallas_call(functools.partial(term_kernel, sets), grid=(parts,), in_sp...  18.2 us
    ppermute x7, starting transfers between devices, shifted(): lax.ppermute(block, 'seq', [(i, i + distance) for i in range(size) if 0 <...  16.5 us
    ppermute x13, starting transfers between devices, swapped(): return lax.ppermute(block, 'seq', [(i, i ^ bit) for i in range(size)])  15 us
    pallas_call x1, Pallas kernels, arranged(): pl.pallas_call(arrange_kernel, grid_spec=pltpu.PrefetchScalarGridSpec(num...  7.87 us
  transfers between devices with their start and end apart: 21, of which 13 were waited for; matrix products, arithmetic and copies ran while one was open for 1% of the time, Pallas kernels for 33%

profile of v4, /device:TPU:0, one launch (start us, length us, event | category | flops | bytes accessed | tf_op | source)
XLA Modules:
  0.0 214.7 jit_solution(18062892050747484298)
XLA Ops:
  7.2 1.1 slice_bitcast_fusion.2
  9.1 5.7 %collective-permute-start.14 = (bf16[2,512,256]{2,1,0:T(8,128)(2,1)}, bf16[2,512,256]{2,1,0:T(8,128)(2,1)}, u32[]{:S(2)}, u32[]{:S(2)}) collective-permute-start(bf16[2,512,256]{2,1,0:T(8,128)(2,1)} %pad_maximum_fusion.refs_2_), channel_id=1, source_target_pairs={{0,8},{4,12},{8,16},{12,20},{16,24},{20,28},{1,9},{5,13},{9,17},{1... | collective-permute-start | bytes 1572872 | tf_op jit(solution)/shard_map/ppermute | solution.py:292
  14.8 1.2 broadcast_xor_fusion.order_ref
  15.9 7.9 %arranged_input.1 = (bf16[4,672,512]{2,1,0:T(8,128)(2,1)}, bf16[4,672,512]{2,1,0:T(8,128)(2,1)S(1)}) custom-call(s32[8]{0:T(128)} %broadcast_xor_fusion.order_ref, bf16[512,5376]{1,0:T(8,128)(2,1)} %x_ref), custom_call_target="tpu_custom_call" | custom-call | tf_op jit(solution)/shard_map/arranged_input/pallas_call | solution.py:170
  23.9 0.9 pad_maximum_fusion.1.refs_2_
  24.8 3.4 %collective-permute-start.16 = (bf16[2,512,256]{2,1,0:T(8,128)(2,1)}, bf16[2,512,256]{2,1,0:T(8,128)(2,1)}, u32[]{:S(2)}, u32[]{:S(2)}) collective-permute-start(bf16[2,512,256]{2,1,0:T(8,128)(2,1)} %pad_maximum_fusion.1.refs_2_), channel_id=1, source_target_pairs={{0,8},{4,12},{8,16},{12,20},{16,24},{20,28},{1,9},{5,13},{9,17},{1... | collective-permute-start | bytes 1572872 | tf_op jit(solution)/shard_map/ppermute | solution.py:292
  28.2 2.1 collective-permute-start.17
  30.5 1.7 collective-permute-start.15
  33.0 0.8 collective-permute-done.15.refs_1_
  34.6 12.0 %attention_grads.2 = (bf16[512,512]{1,0:T(8,128)(2,1)S(1)}, bf16[2,512,256]{2,1,0:T(8,128)(2,1)}, bf16[2,512,256]{2,1,0:T(8,128)(2,1)}, f32[2,512,256]{2,1,0:T(8,128)}) custom-call(s32[1,512]{1,0:T(1,128)} %subtract_add_fusion.lowest_ref, bf16[512,1024]{1,0:T(8,128)(2,1)} %q_ref.3, bf16[512,1024]{1,0:T(8,128)(2,1)} %g_ref.3, ...), custom_call_target="tpu_custom_call" | custom-call | tf_op jit(solution)/shard_map/attention_grads/pallas_call | solution.py:123
  46.6 1.3 collective-permute-start.19
  47.9 1.5 collective-permute-start.18
  49.4 11.7 %attention_grads.3 = (bf16[512,512]{1,0:T(8,128)(2,1)}, bf16[2,512,256]{2,1,0:T(8,128)(2,1)}, bf16[2,512,256]{2,1,0:T(8,128)(2,1)}, f32[2,512,256]{2,1,0:T(8,128)}) custom-call(s32[1,512]{1,0:T(1,128)} %subtract_add_fusion.lowest_ref, bf16[512,1024]{1,0:T(8,128)(2,1)} %q_ref.3, bf16[512,1024]{1,0:T(8,128)(2,1)} %g_ref.3, ...), custom_call_target="tpu_custom_call" | custom-call | tf_op jit(solution)/shard_map/attention_grads/pallas_call | solution.py:123
  61.1 1.9 collective-permute-done.19.refs_4_
  63.0 23.9 %conditional.4 = (bf16[2,512,256]{2,1,0:T(8,128)(2,1)}, bf16[2,512,256]{2,1,0:T(8,128)(2,1)}, bf16[4,672,512]{2,1,0:T(8,128)(2,1)}, bf16[4,672,512]{2,1,0:T(8,12...) conditional(s32[]{:T(128)} %convert_element_type.10, () %tuple.62, ...), branch_computations={%region_2.3_spmd, %region_3.6_spmd} | conditional | flops 1 | bytes 28311856 | solution.py:362
  63.0 1.3 collective-permute-start.2
  64.3 1.3 collective-permute-start.3
  65.6 21.3 %conditional = (bf16[4,672,512]{2,1,0:T(8,128)(2,1)}, bf16[4,672,512]{2,1,0:T(8,128)(2,1)}, bf16[2,672,512]{2,1,0:T(8,128)(2,1)}, bf16[2,672,512]{2,1,0:T(8,128)(2,1)}) conditional(s32[]{:T(128)} %convert_element_type.3, () %tuple.28, (bf16[4,672,512]{2,1,0:T(8,128)(2,1)}, bf16[512,512]{1,0:T(8,128)(2,1)S(1)}, bf16[512,512]{1,0:T(8,128)(2,1)}, ...), branch_computations={%region_4.4_spmd, %region_5.5_spmd} | conditional | bytes 24117388 | solution.py:362
  65.6 7.1 %projection_products.8 = (bf16[4,672,512]{2,1,0:T(8,128)(2,1)}, bf16[4,672,512]{2,1,0:T(8,128)(2,1)}) custom-call(bf16[4,672,512]{2,1,0:T(8,128)(2,1)} %get-tuple-element.50.refs_0_.refs_2_, bf16[512,512]{1,0:T(8,128)(2,1)S(1)} %get-tuple-element.51.refs_1_, bf16[4,672,512]{2,1,0:T(8,128)(2,1)} %get-tuple-element.50.refs_0_.refs_2_, ...), custom_call_target="tpu_custom_call" | custom-call | tf_op jit(solution)/shard_map/cond/branch_1_fun/cond/branch_1_fun/projection_products/pallas_call | solution.py:228
  72.7 1.1 collective-permute-start
  73.9 5.1 %collective-permute-done.refs_2_ = bf16[4,672,512]{2,1,0:T(8,128)(2,1)} collective-permute-done((bf16[4,672,512]{2,1,0:T(8,128)(2,1)}, bf16[4,672,512]{2,1,0:T(8,128)(2,1)}, u32[]{:S(2)}, u32[]{:S(2)}) %collective-permute-start) | collective-permute-done | bytes 2752544 | tf_op jit(solution)/shard_map/cond/branch_1_fun/cond/branch_1_fun/ppermute | solution.py:287
  78.9 3.9 %collective-permute-done.1.refs_5_ = bf16[4,672,512]{2,1,0:T(8,128)(2,1)} collective-permute-done((bf16[4,672,512]{2,1,0:T(8,128)(2,1)}, bf16[4,672,512]{2,1,0:T(8,128)(2,1)}, u32[]{:S(2)}, u32[]{:S(2)}) %collective-permute-start.1) | collective-permute-done | bytes 2752544 | tf_op jit(solution)/shard_map/cond/branch_1_fun/cond/branch_1_fun/ppermute | solution.py:287
  82.9 4.1 %projection_products.9 = (bf16[2,672,512]{2,1,0:T(8,128)(2,1)}, bf16[2,672,512]{2,1,0:T(8,128)(2,1)}) custom-call(bf16[4,672,512]{2,1,0:T(8,128)(2,1)S(1)} %get-tuple-element.55.refs_0_.refs_3_, bf16[512,512]{1,0:T(8,128)(2,1)S(1)} %get-tuple-element.51.refs_1_, bf16[4,672,512]{2,1,0:T(8,128)(2,1)} %collective-permute-done.refs_2_, ...), custom_call_target="tpu_custom_call" | custom-call | tf_op jit(solution)/shard_map/cond/branch_1_fun/cond/branch_1_fun/projection_products/pallas_call | solution.py:228
  87.0 18.2 %input_term.1 = (bf16[4,1344,512]{2,1,0:T(8,128)(2,1)}, bf16[512,512]{1,0:T(8,128)(2,1)}, bf16[512,512]{1,0:T(8,128)(2,1)}) custom-call(bf16[512,512]{1,0:T(8,128)(2,1)S(1)} %get-tuple-element.230.refs_0_, bf16[512,512]{1,0:T(8,128)(2,1)} %get-tuple-element.231.refs_1_, f32[2,512,256]{2,1,0:T(8,128)} %get-tuple-element.213.refs_2_, ...), custom_call_target="tpu_custom_call" | custom-call | tf_op jit(solution)/shard_map/input_term/pallas_call | solution.py:273
  105.2 101.5 %conditional.5 = (bf16[672,1024]{1,0:T(8,128)(2,1)}, bf16[672,512]{1,0:T(8,128)(2,1)}, bf16[672,512]{1,0:T(8,128)(2,1)}) conditional(s32[]{:T(128)} %convert_element_type.10, () %tuple.65, (bf16[2,672,512]{2,1,0:T(8,128)(2,1)}, bf16[2,672,512]{2,1,0:T(8,128)(2,1)}, pred[]{:T(512)}, bf16[4,672,512]{2,1,0:T(8,128)(2,1)}, bf16[512,512]{1,0:T(8,128)(2,1)}, ...), branch_computations={%region_7.8_spmd, %region_8.11_spmd} | conditional | flops 1 | bytes 80609968 | solution.py:362
  105.2 2.4 %collective-permute-start.6 = (bf16[2,672,512]{2,1,0:T(8,128)(2,1)}, bf16[2,672,512]{2,1,0:T(8,128)(2,1)}, u32[]{:S(2)}, u32[]{:S(2)}) collective-permute-start(bf16[2,672,512]{2,1,0:T(8,128)(2,1)} %get-tuple-element.80), channel_id=1, source_target_pairs={{0,8},{4,12},{8,0},{12,4},{16,24},{20,28},{24,16},{28,20},{1,9},{5... | collective-permute-start | bytes 4128776 | tf_op jit(solution)/shard_map/cond/branch_1_fun/ppermute | solution.py:287
  107.6 3.9 %collective-permute-start.7 = (bf16[2,672,512]{2,1,0:T(8,128)(2,1)}, bf16[2,672,512]{2,1,0:T(8,128)(2,1)}, u32[]{:S(2)}, u32[]{:S(2)}) collective-permute-start(bf16[2,672,512]{2,1,0:T(8,128)(2,1)} %get-tuple-element.81), channel_id=1, source_target_pairs={{0,16},{4,20},{8,24},{12,28},{16,0},{20,4},{24,8},{28,12},{1,17},{... | collective-permute-start | bytes 4128776 | tf_op jit(solution)/shard_map/cond/branch_1_fun/ppermute | solution.py:287
  111.5 16.6 %conditional.1 = (bf16[4,672,512]{2,1,0:T(8,128)(2,1)}, bf16[4,672,512]{2,1,0:T(8,128)(2,1)}) conditional(s32[]{:T(128)} %convert_element_type.8, () %tuple.35, (bf16[4,672,512]{2,1,0:T(8,128)(2,1)}, bf16[512,512]{1,0:T(8,128)(2,1)}, bf16[512,512]{1,0:T(8,128)(2,1)}) %tuple.36), branch_computations={%region_9.9_spmd, %region_10.10_spmd} | conditional | bytes 22020192 | solution.py:362
  111.5 7.2 %projection_products.10 = (bf16[4,672,512]{2,1,0:T(8,128)(2,1)}, bf16[4,672,512]{2,1,0:T(8,128)(2,1)}) custom-call(bf16[4,672,512]{2,1,0:T(8,128)(2,1)} %get-tuple-element.71.refs_0_.refs_2_, bf16[512,512]{1,0:T(8,128)(2,1)} %get-tuple-element.72.refs_1_, bf16[4,672,512]{2,1,0:T(8,128)(2,1)} %get-tuple-element.71.refs_0_.refs_2_, ...), custom_call_target="tpu_custom_call" | custom-call | tf_op jit(solution)/shard_map/cond/branch_1_fun/cond/branch_1_fun/projection_products/pallas_call | solution.py:228
  119.3 4.9 %collective-permute-done.4 = bf16[4,672,512]{2,1,0:T(8,128)(2,1)} collective-permute-done((bf16[4,672,512]{2,1,0:T(8,128)(2,1)}, bf16[4,672,512]{2,1,0:T(8,128)(2,1)}, u32[]{:S(2)}, u32[]{:S(2)}) %collective-permute-start.4) | collective-permute-done | bytes 2752544 | tf_op jit(solution)/shard_map/cond/branch_1_fun/cond/branch_1_fun/ppermute | solution.py:287
  124.2 3.9 %collective-permute-done.5 = bf16[4,672,512]{2,1,0:T(8,128)(2,1)} collective-permute-done((bf16[4,672,512]{2,1,0:T(8,128)(2,1)}, bf16[4,672,512]{2,1,0:T(8,128)(2,1)}, u32[]{:S(2)}, u32[]{:S(2)}) %collective-permute-start.5) | collective-permute-done | bytes 2752544 | tf_op jit(solution)/shard_map/cond/branch_1_fun/cond/branch_1_fun/ppermute | solution.py:287
  128.1 4.4 %projection_products.11 = (bf16[2,672,512]{2,1,0:T(8,128)(2,1)}, bf16[2,672,512]{2,1,0:T(8,128)(2,1)}) custom-call(bf16[4,672,512]{2,1,0:T(8,128)(2,1)S(1)} %get-tuple-element.76.refs_0_.refs_3_.refs_4_.refs_5_, bf16[512,512]{1,0:T(8,128)(2,1)} %get-tuple-element.82.refs_1_, bf16[4,672,512]{2,1,0:T(8,128)(2,1)} %get-tuple-element.109.refs_2_, ...), custom_call_target="tpu_custom_call" | custom-call | tf_op jit(solution)/shard_map/cond/branch_1_fun/projection_products/pallas_call | solution.py:228
  132.6 6.4 %collective-permute-done.6.refs_3_ = bf16[2,672,512]{2,1,0:T(8,128)(2,1)} collective-permute-done((bf16[2,672,512]{2,1,0:T(8,128)(2,1)}, bf16[2,672,512]{2,1,0:T(8,128)(2,1)}, u32[]{:S(2)}, u32[]{:S(2)}) %collective-permute-start.6) | collective-permute-done | bytes 1376288 | tf_op jit(solution)/shard_map/cond/branch_1_fun/ppermute | solution.py:287
  139.0 3.9 %collective-permute-done.7.refs_7_.refs_8_ = bf16[2,672,512]{2,1,0:T(8,128)(2,1)} collective-permute-done((bf16[2,672,512]{2,1,0:T(8,128)(2,1)}, bf16[2,672,512]{2,1,0:T(8,128)(2,1)}, u32[]{:S(2)}, u32[]{:S(2)}) %collective-permute-start.7) | collective-permute-done | bytes 1376288 | tf_op jit(solution)/shard_map/cond/branch_1_fun/ppermute | solution.py:287
  142.8 3.7 %projection_products.12 = (bf16[1,672,512]{2,1,0:T(8,128)(2,1)}, bf16[1,672,512]{2,1,0:T(8,128)(2,1)}) custom-call(bf16[4,672,512]{2,1,0:T(8,128)(2,1)S(1)} %get-tuple-element.76.refs_0_.refs_3_.refs_4_.refs_5_, bf16[512,512]{1,0:T(8,128)(2,1)S(1)} %get-tuple-element.77.refs_1_, bf16[4,672,512]{2,1,0:T(8,128)(2,1)} %get-tuple-element.103.refs_2_, ...), custom_call_target="tpu_custom_call" | custom-call | tf_op jit(solution)/shard_map/cond/branch_1_fun/projection_products/pallas_call | solution.py:228
  146.6 2.1 collective-permute-start.8
  148.7 19.7 %collective-permute-done.10.refs_3_ = bf16[2,672,512]{2,1,0:T(8,128)(2,1)S(1)} collective-permute-done((bf16[2,672,512]{2,1,0:T(8,128)(2,1)}, bf16[2,672,512]{2,1,0:T(8,128)(2,1)S(1)}, u32[]{:S(2)}, u32[]{:S(2)}) %collective-permute-start.10) | collective-permute-done | bytes 1376288 | tf_op jit(solution)/shard_map/cond/branch_1_fun/ppermute | solution.py:287
  168.4 3.9 %collective-permute-done.11.refs_7_.refs_8_ = bf16[2,672,512]{2,1,0:T(8,128)(2,1)S(1)} collective-permute-done((bf16[2,672,512]{2,1,0:T(8,128)(2,1)}, bf16[2,672,512]{2,1,0:T(8,128)(2,1)S(1)}, u32[]{:S(2)}, u32[]{:S(2)}) %collective-permute-start.11) | collective-permute-done | bytes 1376288 | tf_op jit(solution)/shard_map/cond/branch_1_fun/ppermute | solution.py:287
  172.2 1.1 copy-done.5
  173.3 3.7 %projection_products.13 = (bf16[1,672,512]{2,1,0:T(8,128)(2,1)}, bf16[1,672,512]{2,1,0:T(8,128)(2,1)}) custom-call(bf16[4,672,512]{2,1,0:T(8,128)(2,1)S(1)} %get-tuple-element.76.refs_0_.refs_3_.refs_4_.refs_5_, bf16[512,512]{1,0:T(8,128)(2,1)S(1)} %copy-done.2, bf16[4,672,512]{2,1,0:T(8,128)(2,1)} %get-tuple-element.109.refs_2_, ...), custom_call_target="tpu_custom_call" | custom-call | tf_op jit(solution)/shard_map/cond/branch_1_fun/projection_products/pallas_call | solution.py:228
  177.0 2.1 collective-permute-start.12
  179.0 1.0 collective-permute-start.13
  180.1 6.9 %collective-permute-done.8.refs_4_ = bf16[1,672,512]{2,1,0:T(8,128)(2,1)S(1)} collective-permute-done((bf16[1,672,512]{2,1,0:T(8,128)(2,1)}, bf16[1,672,512]{2,1,0:T(8,128)(2,1)S(1)}, u32[]{:S(2)}, u32[]{:S(2)}) %collective-permute-start.8) | collective-permute-done | bytes 688160 | tf_op jit(solution)/shard_map/cond/branch_1_fun/ppermute | solution.py:287
  187.8 4.3 %projection_products.14 = bf16[672,1024]{1,0:T(8,128)(2,1)} custom-call(bf16[4,672,512]{2,1,0:T(8,128)(2,1)S(1)} %get-tuple-element.76.refs_0_.refs_3_.refs_4_.refs_5_, bf16[512,512]{1,0:T(8,128)(2,1)S(1)} %get-tuple-element.77.refs_1_, bf16[4,672,512]{2,1,0:T(8,128)(2,1)} %get-tuple-element.103.refs_2_, ...), custom_call_target="tpu_custom_call" | custom-call | tf_op jit(solution)/shard_map/cond/branch_1_fun/projection_products/pallas_call | solution.py:228
  192.1 8.8 %collective-permute-done.12.refs_4_ = bf16[1,672,512]{2,1,0:T(8,128)(2,1)S(1)} collective-permute-done((bf16[1,672,512]{2,1,0:T(8,128)(2,1)}, bf16[1,672,512]{2,1,0:T(8,128)(2,1)S(1)}, u32[]{:S(2)}, u32[]{:S(2)}) %collective-permute-start.12) | collective-permute-done | bytes 688160 | tf_op jit(solution)/shard_map/cond/branch_1_fun/ppermute | solution.py:287
  201.8 0.9 copy-done.8
  202.6 4.1 %projection_products.15 = (bf16[1,672,512]{2,1,0:T(8,128)(2,1)}, bf16[1,672,512]{2,1,0:T(8,128)(2,1)}) custom-call(bf16[4,672,512]{2,1,0:T(8,128)(2,1)S(1)} %get-tuple-element.76.refs_0_.refs_3_.refs_4_.refs_5_, bf16[512,512]{1,0:T(8,128)(2,1)S(1)} %copy-done.2, bf16[4,672,512]{2,1,0:T(8,128)(2,1)} %get-tuple-element.109.refs_2_, ...), custom_call_target="tpu_custom_call" | custom-call | tf_op jit(solution)/shard_map/cond/branch_1_fun/projection_products/pallas_call | solution.py:228
  206.7 1.1 reduce-scatter.2.cloned.1.call-done
  (49 shorter events, 5.0 us)
Async XLA Ops:
  7.2 200.7 %reduce-scatter.2.cloned.1.call-start = ((), (), s32[]{:S(2)}) async-start(), calls=%async_computation.1 | async-start | bytes 6881280 | tf_op jit(solution)/shard_map/reduce_scatter | solution.py:464
  9.1 21.3 %collective-permute-start.14 = (bf16[2,512,256]{2,1,0:T(8,128)(2,1)}, bf16[2,512,256]{2,1,0:T(8,128)(2,1)}, u32[]{:S(2)}, u32[]{:S(2)}) collective-permute-start(bf16[2,512,256]{2,1,0:T(8,128)(2,1)} %pad_maximum_fusion.refs_2_), channel_id=1, source_target_pairs={{0,8},{4,12},{8,16},{12,20},{16,24},{20,28},{1,9},{5,13},{9,17},{1... | collective-permute-start | bytes 1572872 | tf_op jit(solution)/shard_map/ppermute | solution.py:292
  15.9 7.9 %copy-start.10 = (bf16[512,512]{1,0:T(8,128)(2,1)S(1)}, bf16[512,512]{1,0:T(8,128)(2,1)}, u32[]{:S(2)}) copy-start(bf16[512,512]{1,0:T(8,128)(2,1)} %param.21) | copy-start | bytes 1572868
  15.9 7.9 %copy-start.11 = (bf16[512,512]{1,0:T(8,128)(2,1)S(1)}, bf16[512,512]{1,0:T(8,128)(2,1)}, u32[]{:S(2)}) copy-start(bf16[512,512]{1,0:T(8,128)(2,1)} %param.20) | copy-start | bytes 1572868
  15.9 14.3 %copy-start.12 = (s32[8]{0:T(128)S(1)}, s32[8]{0:T(128)}, u32[]{:S(2)}) copy-start(s32[8]{0:T(128)} %param.26) | copy-start | bytes 100
  24.8 24.6 %collective-permute-start.16 = (bf16[2,512,256]{2,1,0:T(8,128)(2,1)}, bf16[2,512,256]{2,1,0:T(8,128)(2,1)}, u32[]{:S(2)}, u32[]{:S(2)}) collective-permute-start(bf16[2,512,256]{2,1,0:T(8,128)(2,1)} %pad_maximum_fusion.1.refs_2_), channel_id=1, source_target_pairs={{0,8},{4,12},{8,16},{12,20},{16,24},{20,28},{1,9},{5,13},{9,17},{1... | collective-permute-start | bytes 1572872 | tf_op jit(solution)/shard_map/ppermute | solution.py:292
  28.2 21.3 %collective-permute-start.17 = (bf16[2,512,256]{2,1,0:T(8,128)(2,1)}, bf16[2,512,256]{2,1,0:T(8,128)(2,1)}, u32[]{:S(2)}, u32[]{:S(2)}) collective-permute-start(bf16[2,512,256]{2,1,0:T(8,128)(2,1)} %pad_maximum_fusion.1.refs_2_), channel_id=1, source_target_pairs={{0,4},{4,8},{8,12},{12,16},{16,20},{20,24},{24,28},{1,5},{5,9},{9,... | collective-permute-start | bytes 1572872 | tf_op jit(solution)/shard_map/ppermute | solution.py:292
  30.5 3.3 %collective-permute-start.15 = (bf16[2,512,256]{2,1,0:T(8,128)(2,1)S(1)}, bf16[2,512,256]{2,1,0:T(8,128)(2,1)S(1)}, u32[]{:S(2)}, u32[]{:S(2)}) collective-permute-start(bf16[2,512,256]{2,1,0:T(8,128)(2,1)S(1)} %broadcast_select_fusion), channel_id=1, source_target_pairs={{0,4},{4,0},{8,12},{12,8},{16,20},{20,16},{24,28},{28,24},{1,5},{5... | collective-permute-start | bytes 1572872 | tf_op jit(solution)/shard_map/ppermute | solution.py:287
  33.8 0.8 copy-start.9
  46.6 16.4 %collective-permute-start.19 = (bf16[2,512,256]{2,1,0:T(8,128)(2,1)}, bf16[2,512,256]{2,1,0:T(8,128)(2,1)}, u32[]{:S(2)}, u32[]{:S(2)}) collective-permute-start(bf16[2,512,256]{2,1,0:T(8,128)(2,1)} %get-tuple-element.188), channel_id=1, source_target_pairs={{8,0},{12,4},{16,8},{20,12},{24,16},{28,20},{9,1},{13,5},{17,9},{2... | collective-permute-start | bytes 1572872 | tf_op jit(solution)/shard_map/ppermute | solution.py:292
  47.9 39.1 %collective-permute-start.18 = (bf16[2,512,256]{2,1,0:T(8,128)(2,1)}, bf16[2,512,256]{2,1,0:T(8,128)(2,1)}, u32[]{:S(2)}, u32[]{:S(2)}) collective-permute-start(bf16[2,512,256]{2,1,0:T(8,128)(2,1)} %get-tuple-element.189), channel_id=1, source_target_pairs={{4,0},{8,4},{12,8},{16,12},{20,16},{24,20},{28,24},{5,1},{9,5},{13... | collective-permute-start | bytes 1572872 | tf_op jit(solution)/shard_map/ppermute | solution.py:292
  63.0 23.9 %collective-permute-start.2 = (bf16[2,512,256]{2,1,0:T(8,128)(2,1)}, bf16[2,512,256]{2,1,0:T(8,128)(2,1)}, u32[]{:S(2)}, u32[]{:S(2)}) collective-permute-start(bf16[2,512,256]{2,1,0:T(8,128)(2,1)} %get-tuple-element.58), channel_id=1, source_target_pairs={{4,0},{8,4},{12,8},{16,12},{20,16},{24,20},{28,24},{5,1},{9,5},{13... | collective-permute-start | bytes 1572872 | tf_op jit(solution)/shard_map/cond/branch_1_fun/ppermute | solution.py:292
  64.3 22.7 %collective-permute-start.3 = (bf16[2,512,256]{2,1,0:T(8,128)(2,1)}, bf16[2,512,256]{2,1,0:T(8,128)(2,1)}, u32[]{:S(2)}, u32[]{:S(2)}) collective-permute-start(bf16[2,512,256]{2,1,0:T(8,128)(2,1)} %get-tuple-element.59), channel_id=1, source_target_pairs={{8,0},{12,4},{16,8},{20,12},{24,16},{28,20},{9,1},{13,5},{17,9},{2... | collective-permute-start | bytes 1572872 | tf_op jit(solution)/shard_map/cond/branch_1_fun/ppermute | solution.py:292
  65.6 17.3 %copy-start = (bf16[512,512]{1,0:T(8,128)(2,1)S(1)}, bf16[512,512]{1,0:T(8,128)(2,1)}, u32[]{:S(2)}) copy-start(bf16[512,512]{1,0:T(8,128)(2,1)} %get-tuple-element.52.refs_3_.refs_4_) | copy-start | bytes 1572868 | tf_op jit(solution)/shard_map/cond/branch_1_fun/cond
  72.7 6.2 %collective-permute-start = (bf16[4,672,512]{2,1,0:T(8,128)(2,1)}, bf16[4,672,512]{2,1,0:T(8,128)(2,1)}, u32[]{:S(2)}, u32[]{:S(2)}) collective-permute-start(bf16[4,672,512]{2,1,0:T(8,128)(2,1)} %get-tuple-element.53), channel_id=1, source_target_pairs={{0,4},{4,0},{8,12},{12,8},{16,20},{20,16},{24,28},{28,24},{1,5},{5... | collective-permute-start | bytes 8257544 | tf_op jit(solution)/shard_map/cond/branch_1_fun/cond/branch_1_fun/ppermute | solution.py:287
  73.9 9.0 %collective-permute-start.1 = (bf16[4,672,512]{2,1,0:T(8,128)(2,1)}, bf16[4,672,512]{2,1,0:T(8,128)(2,1)}, u32[]{:S(2)}, u32[]{:S(2)}) collective-permute-start(bf16[4,672,512]{2,1,0:T(8,128)(2,1)} %get-tuple-element.54), channel_id=1, source_target_pairs={{0,4},{4,0},{8,12},{12,8},{16,20},{20,16},{24,28},{28,24},{1,5},{5... | collective-permute-start | bytes 8257544 | tf_op jit(solution)/shard_map/cond/branch_1_fun/cond/branch_1_fun/ppermute | solution.py:287
  105.2 33.8 %collective-permute-start.6 = (bf16[2,672,512]{2,1,0:T(8,128)(2,1)}, bf16[2,672,512]{2,1,0:T(8,128)(2,1)}, u32[]{:S(2)}, u32[]{:S(2)}) collective-permute-start(bf16[2,672,512]{2,1,0:T(8,128)(2,1)} %get-tuple-element.80), channel_id=1, source_target_pairs={{0,8},{4,12},{8,0},{12,4},{16,24},{20,28},{24,16},{28,20},{1,9},{5... | collective-permute-start | bytes 4128776 | tf_op jit(solution)/shard_map/cond/branch_1_fun/ppermute | solution.py:287
  107.6 35.2 %collective-permute-start.7 = (bf16[2,672,512]{2,1,0:T(8,128)(2,1)}, bf16[2,672,512]{2,1,0:T(8,128)(2,1)}, u32[]{:S(2)}, u32[]{:S(2)}) collective-permute-start(bf16[2,672,512]{2,1,0:T(8,128)(2,1)} %get-tuple-element.81), channel_id=1, source_target_pairs={{0,16},{4,20},{8,24},{12,28},{16,0},{20,4},{24,8},{28,12},{1,17},{... | collective-permute-start | bytes 4128776 | tf_op jit(solution)/shard_map/cond/branch_1_fun/ppermute | solution.py:287
  118.7 5.4 %collective-permute-start.4 = (bf16[4,672,512]{2,1,0:T(8,128)(2,1)}, bf16[4,672,512]{2,1,0:T(8,128)(2,1)}, u32[]{:S(2)}, u32[]{:S(2)}) collective-permute-start(bf16[4,672,512]{2,1,0:T(8,128)(2,1)} %get-tuple-element.74), channel_id=1, source_target_pairs={{0,4},{4,0},{8,12},{12,8},{16,20},{20,16},{24,28},{28,24},{1,5},{5... | collective-permute-start | bytes 8257544 | tf_op jit(solution)/shard_map/cond/branch_1_fun/cond/branch_1_fun/ppermute | solution.py:287
  118.7 9.4 %collective-permute-start.5 = (bf16[4,672,512]{2,1,0:T(8,128)(2,1)}, bf16[4,672,512]{2,1,0:T(8,128)(2,1)}, u32[]{:S(2)}, u32[]{:S(2)}) collective-permute-start(bf16[4,672,512]{2,1,0:T(8,128)(2,1)} %get-tuple-element.75), channel_id=1, source_target_pairs={{0,4},{4,0},{8,12},{12,8},{16,20},{20,16},{24,28},{28,24},{1,5},{5... | collective-permute-start | bytes 8257544 | tf_op jit(solution)/shard_map/cond/branch_1_fun/cond/branch_1_fun/ppermute | solution.py:287
  128.1 14.7 %copy-start.1 = (bf16[512,512]{1,0:T(8,128)(2,1)S(1)}, bf16[512,512]{1,0:T(8,128)(2,1)}, u32[]{:S(2)}) copy-start(bf16[512,512]{1,0:T(8,128)(2,1)} %get-tuple-element.92.refs_5_.refs_6_) | copy-start | bytes 1572868 | tf_op jit(solution)/shard_map/cond
  132.5 35.9 %collective-permute-start.10 = (bf16[2,672,512]{2,1,0:T(8,128)(2,1)}, bf16[2,672,512]{2,1,0:T(8,128)(2,1)S(1)}, u32[]{:S(2)}, u32[]{:S(2)}) collective-permute-start(bf16[2,672,512]{2,1,0:T(8,128)(2,1)} %get-tuple-element.88), channel_id=1, source_target_pairs={{0,8},{4,12},{8,0},{12,4},{16,24},{20,28},{24,16},{28,20},{1,9},{5... | collective-permute-start | bytes 4128776 | tf_op jit(solution)/shard_map/cond/branch_1_fun/ppermute | solution.py:287
  132.5 39.7 %collective-permute-start.11 = (bf16[2,672,512]{2,1,0:T(8,128)(2,1)}, bf16[2,672,512]{2,1,0:T(8,128)(2,1)S(1)}, u32[]{:S(2)}, u32[]{:S(2)}) collective-permute-start(bf16[2,672,512]{2,1,0:T(8,128)(2,1)} %get-tuple-element.89), channel_id=1, source_target_pairs={{0,16},{4,20},{8,24},{12,28},{16,0},{20,4},{24,8},{28,12},{1,17},{... | collective-permute-start | bytes 4128776 | tf_op jit(solution)/shard_map/cond/branch_1_fun/ppermute | solution.py:287
  142.8 30.5 %copy-start.2 = (bf16[512,512]{1,0:T(8,128)(2,1)S(1)}, bf16[512,512]{1,0:T(8,128)(2,1)}, u32[]{:S(2)}) copy-start(bf16[512,512]{1,0:T(8,128)(2,1)} %get-tuple-element.82.refs_1_) | copy-start | bytes 1572868 | tf_op jit(solution)/shard_map/cond
  142.8 30.5 %copy-start.3 = (bf16[512,512]{1,0:T(8,128)(2,1)S(1)}, bf16[512,512]{1,0:T(8,128)(2,1)}, u32[]{:S(2)}) copy-start(bf16[512,512]{1,0:T(8,128)(2,1)} %get-tuple-element.85.refs_4_.refs_5_.refs_6_) | copy-start | bytes 1572868 | tf_op jit(solution)/shard_map/cond
  146.6 40.4 %collective-permute-start.8 = (bf16[1,672,512]{2,1,0:T(8,128)(2,1)}, bf16[1,672,512]{2,1,0:T(8,128)(2,1)S(1)}, u32[]{:S(2)}, u32[]{:S(2)}) collective-permute-start(bf16[1,672,512]{2,1,0:T(8,128)(2,1)} %get-tuple-element.95), channel_id=1, source_target_pairs={{0,16},{4,20},{8,24},{12,28},{16,0},{20,4},{24,8},{28,12},{1,17},{... | collective-permute-start | bytes 2064392 | tf_op jit(solution)/shard_map/cond/branch_1_fun/ppermute | solution.py:287
  148.6 38.4 %collective-permute-start.9 = (bf16[1,672,512]{2,1,0:T(8,128)(2,1)}, bf16[1,672,512]{2,1,0:T(8,128)(2,1)}, u32[]{:S(2)}, u32[]{:S(2)}) collective-permute-start(bf16[1,672,512]{2,1,0:T(8,128)(2,1)} %get-tuple-element.96), channel_id=1, source_target_pairs={{0,8},{4,12},{8,0},{12,4},{16,24},{20,28},{24,16},{28,20},{1,9},{5... | collective-permute-start | bytes 2064392 | tf_op jit(solution)/shard_map/cond/branch_1_fun/ppermute | solution.py:287
  168.4 3.9 %copy-start.4 = (bf16[2,672,512]{2,1,0:T(8,128)(2,1)}, bf16[2,672,512]{2,1,0:T(8,128)(2,1)S(1)}, u32[]{:S(2)}) copy-start(bf16[2,672,512]{2,1,0:T(8,128)(2,1)S(1)} %collective-permute-done.10.refs_3_) | copy-start | bytes 4128772 | tf_op jit(solution)/shard_map/cond
  172.2 1.1 copy-start.5
  177.0 23.9 %collective-permute-start.12 = (bf16[1,672,512]{2,1,0:T(8,128)(2,1)}, bf16[1,672,512]{2,1,0:T(8,128)(2,1)S(1)}, u32[]{:S(2)}, u32[]{:S(2)}) collective-permute-start(bf16[1,672,512]{2,1,0:T(8,128)(2,1)} %get-tuple-element.101), channel_id=1, source_target_pairs={{0,16},{4,20},{8,24},{12,28},{16,0},{20,4},{24,8},{28,12},{1,17},{... | collective-permute-start | bytes 2064392 | tf_op jit(solution)/shard_map/cond/branch_1_fun/ppermute | solution.py:287
  179.0 21.9 %collective-permute-start.13 = (bf16[1,672,512]{2,1,0:T(8,128)(2,1)}, bf16[1,672,512]{2,1,0:T(8,128)(2,1)S(1)}, u32[]{:S(2)}, u32[]{:S(2)}) collective-permute-start(bf16[1,672,512]{2,1,0:T(8,128)(2,1)} %get-tuple-element.102), channel_id=1, source_target_pairs={{0,8},{4,12},{8,0},{12,4},{16,24},{20,28},{24,16},{28,20},{1,9},{5... | collective-permute-start | bytes 2064392 | tf_op jit(solution)/shard_map/cond/branch_1_fun/ppermute | solution.py:287
  187.0 0.8 copy-start.6
  200.9 0.8 copy-start.7
  201.8 0.9 copy-start.8
Sparse Core Ops, SparseCore 0:
  105.3 102.4 reduce-scatter.1

commit v5 on v4

--- a/solution.py
+++ b/solution.py
@@ -140,7 +140,7 @@
     )(lowest, query, out_grad, *pieces)
 
 
-def arrange_kernel(order_ref, x_ref, first_ref, second_ref, scratch):
+def arrange_kernel(offsets, me_ref, x_ref, first_ref, second_ref, scratch):
     width = first_ref.shape[1]
     step = pl.program_id(0)
     half = pl.num_programs(0) // 2
@@ -152,7 +152,7 @@
             at = slice(i * tile, (i + 1) * tile)
             scratch[at, :] = x_ref[:, at].T
 
-    start = pl.multiple_of(order_ref[step] * width, 16)
+    start = pl.multiple_of((listed(offsets, step) ^ me_ref[0]) * width, 16)
 
     @pl.when(step < half)
     def _():
@@ -163,26 +163,27 @@
         second_ref[0] = scratch[pl.ds(start, width), :]
 
 
-def arranged(array, order, count):
+def arranged(array, me, offsets):
     rows, cols = array.shape
+    count = len(offsets)
     width, half = cols // count, count // 2
     out = jax.ShapeDtypeStruct((half, width, rows), array.dtype)
     return pl.pallas_call(
-        arrange_kernel,
+        functools.partial(arrange_kernel, offsets),
         grid_spec=pltpu.PrefetchScalarGridSpec(
             num_scalar_prefetch=1,
             grid=(count,),
-            in_specs=[pl.BlockSpec((rows, cols), lambda i, order_ref: (0, 0))],
+            in_specs=[pl.BlockSpec((rows, cols), lambda i, me_ref: (0, 0))],
             out_specs=[
-                pl.BlockSpec((1, width, rows), lambda i, order_ref: (jnp.minimum(i, half - 1), 0, 0)),
-                pl.BlockSpec((1, width, rows), lambda i, order_ref: (jnp.maximum(i - half, 0), 0, 0)),
+                pl.BlockSpec((1, width, rows), lambda i, me_ref: (jnp.minimum(i, half - 1), 0, 0)),
+                pl.BlockSpec((1, width, rows), lambda i, me_ref: (jnp.maximum(i - half, 0), 0, 0)),
             ],
             scratch_shapes=[pltpu.VMEM((cols, rows), array.dtype)],
         ),
         out_shape=[out, out],
         compiler_params=pltpu.CompilerParams(vmem_limit_bytes=VMEM_BYTES),
         name="arranged_input",
-    )(order, array)
+    )(me.reshape(1), array)
 
 
 def listed(values, index):
@@ -192,10 +193,12 @@
     return total
 
 
-def paired_kernel(count, joined, *refs):
-    outs = refs[2 * (2 + count) :]
+def paired_kernel(count, shared, joined, *refs):
+    sides = 2 * [refs[:1]] if shared else [refs[:1], refs[2 + count : 3 + count]]
+    sides = [(*x, *refs[i * (1 + count) + (1 if shared else i + 1) :][: 1 + count]) for i, x in enumerate(sides)]
+    outs = refs[2 * (1 + count) + (1 if shared else 2) :]
     for side in range(2):
-        x_ref, g_ref, *arrived = refs[side * (2 + count) : (side + 1) * (2 + count)]
+        x_ref, g_ref, *arrived = sides[side]
         value = dot(x_ref[0], g_ref[...])
         for ref in arrived:
             value = value + ref[0].astype(jnp.float32)
@@ -209,14 +212,19 @@
 
 def paired_products(sides, joined=False):
     specs, operands = [], []
-    for inputs, grads, arrived, at in sides:
-        for array, where in zip([inputs, *arrived], at):
-            spec = pl.BlockSpec((1,) + array.shape[1:], lambda i, where=where: (listed(where, i), 0, 0))
-            specs.append(spec)
-            operands.append(array)
-        place = len(specs) - len(arrived)
-        specs.insert(place, pl.BlockSpec(grads.shape, lambda i: (0, 0)))
-        operands.insert(place, grads)
+
+    def blocks(array, where):
+        specs.append(pl.BlockSpec((1,) + array.shape[1:], lambda i: (listed(where, i), 0, 0)))
+        operands.append(array)
+
+    shared = sides[0][0] is sides[1][0] and sides[0][3][0] == sides[1][3][0]
+    for side, (inputs, grads, arrived, at) in enumerate(sides):
+        if side == 0 or not shared:
+            blocks(inputs, at[0])
+        specs.append(pl.BlockSpec(grads.shape, lambda i: (0, 0)))
+        operands.append(grads)
+        for array, where in zip(arrived, at[1:]):
+            blocks(array, where)
     inputs, grads, arrived, at = sides[0]
     count, width, cols = len(at[0]), inputs.shape[1], grads.shape[1]
     if joined:
@@ -226,7 +234,7 @@
         out_specs = [pl.BlockSpec((1, width, cols), lambda i: (i, 0, 0))] * 2
         out_shape = [jax.ShapeDtypeStruct((count, width, cols), jnp.bfloat16)] * 2
     return pl.pallas_call(
-        functools.partial(paired_kernel, len(arrived), joined),
+        functools.partial(paired_kernel, len(arrived), shared, joined),
         grid=(count,),
         in_specs=specs,
         out_specs=out_specs,
@@ -395,7 +403,7 @@
     even = [2 * gray(i) for i in range(1, seq_size // 2)] + [0]
     offsets = [o ^ 1 for o in even] + even
     layer_input = order.after(layer_input)
-    odds, evens = order.did(arranged(layer_input, me ^ jnp.array(offsets, jnp.int32), seq_size))
+    odds, evens = order.did(arranged(layer_input, me, offsets))
     pieces = []
     for c in range(1, sets):
         keys, values = order.after(keys, values)

time: 215 us -> 213 us (level)
  transfers between devices with their start and end apart: 21 -> 21, of which waited for: 13 -> 13; matrix products, arithmetic and copies ran while one was open for 1% -> 1% of each run, Pallas kernels for 33% -> 32%
where the time goes in v5:
time: 213 us; the launch traced here: 212 us
  Pallas kernels  86.2 us (40%)
  waiting for transfers between devices  72 us (34%)
  starting transfers between devices  31.5 us (15%)
  between operations  14.2 us (7%)
  local copies, waits for them, and re-layouts  5.58 us (3%)
  other arithmetic  2.67 us (1%)
    ppermute x13, waiting for transfers between devices, swapped(): return lax.ppermute(block, 'seq', [(i, i ^ bit) for i in range(size)])  69 us
    pallas_call x8, Pallas kernels, paired_products(): pl.pallas_call(functools.partial(paired_kernel, len(arrived), shared, joi...  37.1 us
    pallas_call x2, Pallas kernels, attention(): pl.pallas_call(functools.partial(attention_kernel, groups, depth), grid=(...  23.7 us
    pallas_call x1, Pallas kernels, input_term(): pl.pallas_call(functools.partial(term_kernel, sets), grid=(parts,), in_sp...  18.2 us
    ppermute x7, starting transfers between devices, shifted(): lax.ppermute(block, 'seq', [(i, i + distance) for i in range(size) if 0 <...  16.5 us
    ppermute x13, starting transfers between devices, swapped(): return lax.ppermute(block, 'seq', [(i, i ^ bit) for i in range(size)])  15 us
    pallas_call x1, Pallas kernels, arranged(): pl.pallas_call(functools.partial(arrange_kernel, offsets), grid_spec=pltp...  7.15 us
  transfers between devices with their start and end apart: 21, of which 13 were waited for; matrix products, arithmetic and copies ran while one was open for 1% of the time, Pallas kernels for 32%

profile of v5, /device:TPU:0, one launch (start us, length us, event | category | flops | bytes accessed | tf_op | source)
XLA Modules:
  0.0 212.2 jit_solution(2702606886770888465)
XLA Ops:
  7.2 1.1 slice_bitcast_fusion.2
  9.1 5.7 %collective-permute-start.14 = (bf16[2,512,256]{2,1,0:T(8,128)(2,1)}, bf16[2,512,256]{2,1,0:T(8,128)(2,1)}, u32[]{:S(2)}, u32[]{:S(2)}) collective-permute-start(bf16[2,512,256]{2,1,0:T(8,128)(2,1)} %pad_maximum_fusion.refs_2_), channel_id=1, source_target_pairs={{0,8},{4,12},{8,16},{12,20},{16,24},{20,28},{1,9},{5,13},{9,17},{1... | collective-permute-start | bytes 1572872 | tf_op jit(solution)/shard_map/ppermute | solution.py:300
  14.8 7.2 %arranged_input.1 = (bf16[4,672,512]{2,1,0:T(8,128)(2,1)}, bf16[4,672,512]{2,1,0:T(8,128)(2,1)S(1)}) custom-call(s32[1]{0:T(128)} %bitcast.7.me_ref, bf16[512,5376]{1,0:T(8,128)(2,1)} %x_ref), custom_call_target="tpu_custom_call" | custom-call | tf_op jit(solution)/shard_map/arranged_input/pallas_call | solution.py:171
  22.0 0.9 pad_maximum_fusion.1.refs_2_
  22.9 3.5 %collective-permute-start.16 = (bf16[2,512,256]{2,1,0:T(8,128)(2,1)}, bf16[2,512,256]{2,1,0:T(8,128)(2,1)}, u32[]{:S(2)}, u32[]{:S(2)}) collective-permute-start(bf16[2,512,256]{2,1,0:T(8,128)(2,1)} %pad_maximum_fusion.1.refs_2_), channel_id=1, source_target_pairs={{0,8},{4,12},{8,16},{12,20},{16,24},{20,28},{1,9},{5,13},{9,17},{1... | collective-permute-start | bytes 1572872 | tf_op jit(solution)/shard_map/ppermute | solution.py:300
  26.3 2.1 collective-permute-start.17
  28.7 1.7 collective-permute-start.15
  31.1 0.8 collective-permute-done.15.refs_1_
  32.8 12.0 %attention_grads.2 = (bf16[512,512]{1,0:T(8,128)(2,1)S(1)}, bf16[2,512,256]{2,1,0:T(8,128)(2,1)}, bf16[2,512,256]{2,1,0:T(8,128)(2,1)}, f32[2,512,256]{2,1,0:T(8,128)}) custom-call(s32[1,512]{1,0:T(1,128)} %subtract_add_fusion.lowest_ref, bf16[512,1024]{1,0:T(8,128)(2,1)} %q_ref.3, bf16[512,1024]{1,0:T(8,128)(2,1)} %g_ref.3, ...), custom_call_target="tpu_custom_call" | custom-call | tf_op jit(solution)/shard_map/attention_grads/pallas_call | solution.py:123
  44.8 1.3 collective-permute-start.19
  46.0 1.5 collective-permute-start.18
  47.6 11.7 %attention_grads.3 = (bf16[512,512]{1,0:T(8,128)(2,1)}, bf16[2,512,256]{2,1,0:T(8,128)(2,1)}, bf16[2,512,256]{2,1,0:T(8,128)(2,1)}, f32[2,512,256]{2,1,0:T(8,128)}) custom-call(s32[1,512]{1,0:T(1,128)} %subtract_add_fusion.lowest_ref, bf16[512,1024]{1,0:T(8,128)(2,1)} %q_ref.3, bf16[512,1024]{1,0:T(8,128)(2,1)} %g_ref.3, ...), custom_call_target="tpu_custom_call" | custom-call | tf_op jit(solution)/shard_map/attention_grads/pallas_call | solution.py:123
  59.3 1.9 collective-permute-done.19.refs_4_
  61.2 23.3 %conditional.4 = (bf16[2,512,256]{2,1,0:T(8,128)(2,1)}, bf16[2,512,256]{2,1,0:T(8,128)(2,1)}, bf16[4,672,512]{2,1,0:T(8,128)(2,1)}, bf16[4,672,512]{2,1,0:T(8,12...) conditional(s32[]{:T(128)} %convert_element_type.10, () %tuple.62, ...), branch_computations={%region_2.3_spmd, %region_3.6_spmd} | conditional | flops 1 | bytes 28311856 | solution.py:370
  61.2 1.3 collective-permute-start.2
  62.4 1.3 collective-permute-start.3
  63.8 20.7 %conditional = (bf16[4,672,512]{2,1,0:T(8,128)(2,1)}, bf16[4,672,512]{2,1,0:T(8,128)(2,1)}, bf16[2,672,512]{2,1,0:T(8,128)(2,1)}, bf16[2,672,512]{2,1,0:T(8,128)(2,1)}) conditional(s32[]{:T(128)} %convert_element_type.3, () %tuple.28, (bf16[4,672,512]{2,1,0:T(8,128)(2,1)}, bf16[512,512]{1,0:T(8,128)(2,1)S(1)}, bf16[512,512]{1,0:T(8,128)(2,1)}, ...), branch_computations={%region_4.4_spmd, %region_5.5_spmd} | conditional | bytes 24117388 | solution.py:370
  63.8 6.5 %projection_products.8 = (bf16[4,672,512]{2,1,0:T(8,128)(2,1)}, bf16[4,672,512]{2,1,0:T(8,128)(2,1)}) custom-call(bf16[4,672,512]{2,1,0:T(8,128)(2,1)} %get-tuple-element.50.refs_0_, bf16[512,512]{1,0:T(8,128)(2,1)S(1)} %get-tuple-element.51.refs_1_, bf16[512,512]{1,0:T(8,128)(2,1)} %get-tuple-element.52.refs_2_.refs_4_), custom_call_target="tpu_custom_call" | custom-call | tf_op jit(solution)/shard_map/cond/branch_1_fun/cond/branch_1_fun/projection_products/pallas_call | solution.py:236
  70.3 1.1 collective-permute-start
  71.4 5.1 %collective-permute-done.refs_2_ = bf16[4,672,512]{2,1,0:T(8,128)(2,1)} collective-permute-done((bf16[4,672,512]{2,1,0:T(8,128)(2,1)}, bf16[4,672,512]{2,1,0:T(8,128)(2,1)}, u32[]{:S(2)}, u32[]{:S(2)}) %collective-permute-start) | collective-permute-done | bytes 2752544 | tf_op jit(solution)/shard_map/cond/branch_1_fun/cond/branch_1_fun/ppermute | solution.py:295
  76.5 3.9 %collective-permute-done.1.refs_5_ = bf16[4,672,512]{2,1,0:T(8,128)(2,1)} collective-permute-done((bf16[4,672,512]{2,1,0:T(8,128)(2,1)}, bf16[4,672,512]{2,1,0:T(8,128)(2,1)}, u32[]{:S(2)}, u32[]{:S(2)}) %collective-permute-start.1) | collective-permute-done | bytes 2752544 | tf_op jit(solution)/shard_map/cond/branch_1_fun/cond/branch_1_fun/ppermute | solution.py:295
  80.4 4.1 %projection_products.9 = (bf16[2,672,512]{2,1,0:T(8,128)(2,1)}, bf16[2,672,512]{2,1,0:T(8,128)(2,1)}) custom-call(bf16[4,672,512]{2,1,0:T(8,128)(2,1)S(1)} %get-tuple-element.55.refs_0_.refs_3_, bf16[512,512]{1,0:T(8,128)(2,1)S(1)} %get-tuple-element.51.refs_1_, bf16[4,672,512]{2,1,0:T(8,128)(2,1)} %collective-permute-done.refs_2_, ...), custom_call_target="tpu_custom_call" | custom-call | tf_op jit(solution)/shard_map/cond/branch_1_fun/cond/branch_1_fun/projection_products/pallas_call | solution.py:236
  84.5 18.2 %input_term.1 = (bf16[4,1344,512]{2,1,0:T(8,128)(2,1)}, bf16[512,512]{1,0:T(8,128)(2,1)}, bf16[512,512]{1,0:T(8,128)(2,1)}) custom-call(bf16[512,512]{1,0:T(8,128)(2,1)S(1)} %get-tuple-element.230.refs_0_, bf16[512,512]{1,0:T(8,128)(2,1)} %get-tuple-element.231.refs_1_, f32[2,512,256]{2,1,0:T(8,128)} %get-tuple-element.213.refs_2_, ...), custom_call_target="tpu_custom_call" | custom-call | tf_op jit(solution)/shard_map/input_term/pallas_call | solution.py:281
  102.7 101.5 %conditional.5 = (bf16[672,1024]{1,0:T(8,128)(2,1)}, bf16[672,512]{1,0:T(8,128)(2,1)}, bf16[672,512]{1,0:T(8,128)(2,1)}) conditional(s32[]{:T(128)} %convert_element_type.10, () %tuple.65, (bf16[2,672,512]{2,1,0:T(8,128)(2,1)}, bf16[2,672,512]{2,1,0:T(8,128)(2,1)}, pred[]{:T(512)}, bf16[4,672,512]{2,1,0:T(8,128)(2,1)}, bf16[512,512]{1,0:T(8,128)(2,1)}, ...), branch_computations={%region_7.8_spmd, %region_8.11_spmd} | conditional | flops 1 | bytes 80609968 | solution.py:370
  102.7 2.4 %collective-permute-start.6 = (bf16[2,672,512]{2,1,0:T(8,128)(2,1)}, bf16[2,672,512]{2,1,0:T(8,128)(2,1)}, u32[]{:S(2)}, u32[]{:S(2)}) collective-permute-start(bf16[2,672,512]{2,1,0:T(8,128)(2,1)} %get-tuple-element.80), channel_id=1, source_target_pairs={{0,8},{4,12},{8,0},{12,4},{16,24},{20,28},{24,16},{28,20},{1,9},{5... | collective-permute-start | bytes 4128776 | tf_op jit(solution)/shard_map/cond/branch_1_fun/ppermute | solution.py:295
  105.2 3.9 %collective-permute-start.7 = (bf16[2,672,512]{2,1,0:T(8,128)(2,1)}, bf16[2,672,512]{2,1,0:T(8,128)(2,1)}, u32[]{:S(2)}, u32[]{:S(2)}) collective-permute-start(bf16[2,672,512]{2,1,0:T(8,128)(2,1)} %get-tuple-element.81), channel_id=1, source_target_pairs={{0,16},{4,20},{8,24},{12,28},{16,0},{20,4},{24,8},{28,12},{1,17},{... | collective-permute-start | bytes 4128776 | tf_op jit(solution)/shard_map/cond/branch_1_fun/ppermute | solution.py:295
  109.1 15.9 %conditional.1 = (bf16[4,672,512]{2,1,0:T(8,128)(2,1)}, bf16[4,672,512]{2,1,0:T(8,128)(2,1)}) conditional(s32[]{:T(128)} %convert_element_type.8, () %tuple.35, (bf16[4,672,512]{2,1,0:T(8,128)(2,1)}, bf16[512,512]{1,0:T(8,128)(2,1)}, bf16[512,512]{1,0:T(8,128)(2,1)}) %tuple.36), branch_computations={%region_9.9_spmd, %region_10.10_spmd} | conditional | bytes 22020192 | solution.py:370
  109.1 6.5 %projection_products.10 = (bf16[4,672,512]{2,1,0:T(8,128)(2,1)}, bf16[4,672,512]{2,1,0:T(8,128)(2,1)}) custom-call(bf16[4,672,512]{2,1,0:T(8,128)(2,1)} %get-tuple-element.71.refs_0_, bf16[512,512]{1,0:T(8,128)(2,1)} %get-tuple-element.72.refs_1_, bf16[512,512]{1,0:T(8,128)(2,1)} %get-tuple-element.73.refs_2_), custom_call_target="tpu_custom_call" | custom-call | tf_op jit(solution)/shard_map/cond/branch_1_fun/cond/branch_1_fun/projection_products/pallas_call | solution.py:236
  116.1 4.9 %collective-permute-done.4 = bf16[4,672,512]{2,1,0:T(8,128)(2,1)} collective-permute-done((bf16[4,672,512]{2,1,0:T(8,128)(2,1)}, bf16[4,672,512]{2,1,0:T(8,128)(2,1)}, u32[]{:S(2)}, u32[]{:S(2)}) %collective-permute-start.4) | collective-permute-done | bytes 2752544 | tf_op jit(solution)/shard_map/cond/branch_1_fun/cond/branch_1_fun/ppermute | solution.py:295
  121.0 3.9 %collective-permute-done.5 = bf16[4,672,512]{2,1,0:T(8,128)(2,1)} collective-permute-done((bf16[4,672,512]{2,1,0:T(8,128)(2,1)}, bf16[4,672,512]{2,1,0:T(8,128)(2,1)}, u32[]{:S(2)}, u32[]{:S(2)}) %collective-permute-start.5) | collective-permute-done | bytes 2752544 | tf_op jit(solution)/shard_map/cond/branch_1_fun/cond/branch_1_fun/ppermute | solution.py:295
  124.9 4.4 %projection_products.11 = (bf16[2,672,512]{2,1,0:T(8,128)(2,1)}, bf16[2,672,512]{2,1,0:T(8,128)(2,1)}) custom-call(bf16[4,672,512]{2,1,0:T(8,128)(2,1)S(1)} %get-tuple-element.76.refs_0_.refs_3_.refs_4_, bf16[512,512]{1,0:T(8,128)(2,1)} %get-tuple-element.82.refs_1_, bf16[4,672,512]{2,1,0:T(8,128)(2,1)} %get-tuple-element.109.refs_2_, ...), custom_call_target="tpu_custom_call" | custom-call | tf_op jit(solution)/shard_map/cond/branch_1_fun/projection_products/pallas_call | solution.py:236
  129.4 7.1 %collective-permute-done.6.refs_3_ = bf16[2,672,512]{2,1,0:T(8,128)(2,1)} collective-permute-done((bf16[2,672,512]{2,1,0:T(8,128)(2,1)}, bf16[2,672,512]{2,1,0:T(8,128)(2,1)}, u32[]{:S(2)}, u32[]{:S(2)}) %collective-permute-start.6) | collective-permute-done | bytes 1376288 | tf_op jit(solution)/shard_map/cond/branch_1_fun/ppermute | solution.py:295
  136.5 3.9 %collective-permute-done.7.refs_7_ = bf16[2,672,512]{2,1,0:T(8,128)(2,1)} collective-permute-done((bf16[2,672,512]{2,1,0:T(8,128)(2,1)}, bf16[2,672,512]{2,1,0:T(8,128)(2,1)}, u32[]{:S(2)}, u32[]{:S(2)}) %collective-permute-start.7) | collective-permute-done | bytes 1376288 | tf_op jit(solution)/shard_map/cond/branch_1_fun/ppermute | solution.py:295
  140.4 3.7 %projection_products.12 = (bf16[1,672,512]{2,1,0:T(8,128)(2,1)}, bf16[1,672,512]{2,1,0:T(8,128)(2,1)}) custom-call(bf16[4,672,512]{2,1,0:T(8,128)(2,1)S(1)} %get-tuple-element.76.refs_0_.refs_3_.refs_4_, bf16[512,512]{1,0:T(8,128)(2,1)S(1)} %get-tuple-element.77.refs_1_, bf16[4,672,512]{2,1,0:T(8,128)(2,1)} %get-tuple-element.103.refs_2_, ...), custom_call_target="tpu_custom_call" | custom-call | tf_op jit(solution)/shard_map/cond/branch_1_fun/projection_products/pallas_call | solution.py:236
  144.1 2.1 collective-permute-start.8
  146.2 19.7 %collective-permute-done.10.refs_3_ = bf16[2,672,512]{2,1,0:T(8,128)(2,1)S(1)} collective-permute-done((bf16[2,672,512]{2,1,0:T(8,128)(2,1)}, bf16[2,672,512]{2,1,0:T(8,128)(2,1)S(1)}, u32[]{:S(2)}, u32[]{:S(2)}) %collective-permute-start.10) | collective-permute-done | bytes 1376288 | tf_op jit(solution)/shard_map/cond/branch_1_fun/ppermute | solution.py:295
  165.9 3.9 %collective-permute-done.11.refs_7_ = bf16[2,672,512]{2,1,0:T(8,128)(2,1)S(1)} collective-permute-done((bf16[2,672,512]{2,1,0:T(8,128)(2,1)}, bf16[2,672,512]{2,1,0:T(8,128)(2,1)S(1)}, u32[]{:S(2)}, u32[]{:S(2)}) %collective-permute-start.11) | collective-permute-done | bytes 1376288 | tf_op jit(solution)/shard_map/cond/branch_1_fun/ppermute | solution.py:295
  169.8 1.1 copy-done.5
  170.9 3.7 %projection_products.13 = (bf16[1,672,512]{2,1,0:T(8,128)(2,1)}, bf16[1,672,512]{2,1,0:T(8,128)(2,1)}) custom-call(bf16[4,672,512]{2,1,0:T(8,128)(2,1)S(1)} %get-tuple-element.76.refs_0_.refs_3_.refs_4_, bf16[512,512]{1,0:T(8,128)(2,1)S(1)} %copy-done.2, bf16[4,672,512]{2,1,0:T(8,128)(2,1)} %get-tuple-element.109.refs_2_, bf16[2,672,512]{2,1,0:T(8,128)(2,1)} %copy-done.4, ...), custom_call_target="tpu_custom_call" | custom-call | tf_op jit(solution)/shard_map/cond/branch_1_fun/projection_products/pallas_call | solution.py:236
  174.5 2.1 collective-permute-start.12
  176.6 1.0 collective-permute-start.13
  177.6 6.9 %collective-permute-done.8.refs_4_ = bf16[1,672,512]{2,1,0:T(8,128)(2,1)S(1)} collective-permute-done((bf16[1,672,512]{2,1,0:T(8,128)(2,1)}, bf16[1,672,512]{2,1,0:T(8,128)(2,1)S(1)}, u32[]{:S(2)}, u32[]{:S(2)}) %collective-permute-start.8) | collective-permute-done | bytes 688160 | tf_op jit(solution)/shard_map/cond/branch_1_fun/ppermute | solution.py:295
  184.5 0.8 copy-done.6
  185.4 4.3 %projection_products.14 = bf16[672,1024]{1,0:T(8,128)(2,1)} custom-call(bf16[4,672,512]{2,1,0:T(8,128)(2,1)S(1)} %get-tuple-element.76.refs_0_.refs_3_.refs_4_, bf16[512,512]{1,0:T(8,128)(2,1)S(1)} %get-tuple-element.77.refs_1_, bf16[4,672,512]{2,1,0:T(8,128)(2,1)} %get-tuple-element.103.refs_2_, bf16[2,672,512]{2,1,0:T(8,128)(2,1)} %collective-permute-done.6.refs_3_, ...), custom_call_target="tpu_custom_call" | custom-call | tf_op jit(solution)/shard_map/cond/branch_1_fun/projection_products/pallas_call | solution.py:236
  189.6 8.8 %collective-permute-done.12.refs_4_ = bf16[1,672,512]{2,1,0:T(8,128)(2,1)S(1)} collective-permute-done((bf16[1,672,512]{2,1,0:T(8,128)(2,1)}, bf16[1,672,512]{2,1,0:T(8,128)(2,1)S(1)}, u32[]{:S(2)}, u32[]{:S(2)}) %collective-permute-start.12) | collective-permute-done | bytes 688160 | tf_op jit(solution)/shard_map/cond/branch_1_fun/ppermute | solution.py:295
  199.3 0.9 copy-done.8
  200.2 4.1 %projection_products.15 = (bf16[1,672,512]{2,1,0:T(8,128)(2,1)}, bf16[1,672,512]{2,1,0:T(8,128)(2,1)}) custom-call(bf16[4,672,512]{2,1,0:T(8,128)(2,1)S(1)} %get-tuple-element.76.refs_0_.refs_3_.refs_4_, bf16[512,512]{1,0:T(8,128)(2,1)S(1)} %copy-done.2, bf16[4,672,512]{2,1,0:T(8,128)(2,1)} %get-tuple-element.109.refs_2_, bf16[2,672,512]{2,1,0:T(8,128)(2,1)} %copy-done.4, ...), custom_call_target="tpu_custom_call" | custom-call | tf_op jit(solution)/shard_map/cond/branch_1_fun/projection_products/pallas_call | solution.py:236
  204.3 1.1 reduce-scatter.2.cloned.1.call-done
  (48 shorter events, 4.2 us)
Async XLA Ops:
  7.2 198.2 %reduce-scatter.2.cloned.1.call-start = ((), (), s32[]{:S(2)}) async-start(), calls=%async_computation.1 | async-start | bytes 6881280 | tf_op jit(solution)/shard_map/reduce_scatter | solution.py:472
  9.1 19.5 %collective-permute-start.14 = (bf16[2,512,256]{2,1,0:T(8,128)(2,1)}, bf16[2,512,256]{2,1,0:T(8,128)(2,1)}, u32[]{:S(2)}, u32[]{:S(2)}) collective-permute-start(bf16[2,512,256]{2,1,0:T(8,128)(2,1)} %pad_maximum_fusion.refs_2_), channel_id=1, source_target_pairs={{0,8},{4,12},{8,16},{12,20},{16,24},{20,28},{1,9},{5,13},{9,17},{1... | collective-permute-start | bytes 1572872 | tf_op jit(solution)/shard_map/ppermute | solution.py:300
  14.8 7.2 %copy-start.10 = (bf16[512,512]{1,0:T(8,128)(2,1)S(1)}, bf16[512,512]{1,0:T(8,128)(2,1)}, u32[]{:S(2)}) copy-start(bf16[512,512]{1,0:T(8,128)(2,1)} %param.20) | copy-start | bytes 1572868
  14.8 7.2 %copy-start.11 = (bf16[512,512]{1,0:T(8,128)(2,1)S(1)}, bf16[512,512]{1,0:T(8,128)(2,1)}, u32[]{:S(2)}) copy-start(bf16[512,512]{1,0:T(8,128)(2,1)} %param.19) | copy-start | bytes 1572868
  14.8 13.6 %copy-start.12 = (s32[8]{0:T(128)S(1)}, s32[8]{0:T(128)}, u32[]{:S(2)}) copy-start(s32[8]{0:T(128)} %param.25) | copy-start | bytes 100
  22.9 24.7 %collective-permute-start.16 = (bf16[2,512,256]{2,1,0:T(8,128)(2,1)}, bf16[2,512,256]{2,1,0:T(8,128)(2,1)}, u32[]{:S(2)}, u32[]{:S(2)}) collective-permute-start(bf16[2,512,256]{2,1,0:T(8,128)(2,1)} %pad_maximum_fusion.1.refs_2_), channel_id=1, source_target_pairs={{0,8},{4,12},{8,16},{12,20},{16,24},{20,28},{1,9},{5,13},{9,17},{1... | collective-permute-start | bytes 1572872 | tf_op jit(solution)/shard_map/ppermute | solution.py:300
  26.3 21.3 %collective-permute-start.17 = (bf16[2,512,256]{2,1,0:T(8,128)(2,1)}, bf16[2,512,256]{2,1,0:T(8,128)(2,1)}, u32[]{:S(2)}, u32[]{:S(2)}) collective-permute-start(bf16[2,512,256]{2,1,0:T(8,128)(2,1)} %pad_maximum_fusion.1.refs_2_), channel_id=1, source_target_pairs={{0,4},{4,8},{8,12},{12,16},{16,20},{20,24},{24,28},{1,5},{5,9},{9,... | collective-permute-start | bytes 1572872 | tf_op jit(solution)/shard_map/ppermute | solution.py:300
  28.7 3.3 %collective-permute-start.15 = (bf16[2,512,256]{2,1,0:T(8,128)(2,1)S(1)}, bf16[2,512,256]{2,1,0:T(8,128)(2,1)S(1)}, u32[]{:S(2)}, u32[]{:S(2)}) collective-permute-start(bf16[2,512,256]{2,1,0:T(8,128)(2,1)S(1)} %broadcast_select_fusion), channel_id=1, source_target_pairs={{0,4},{4,0},{8,12},{12,8},{16,20},{20,16},{24,28},{28,24},{1,5},{5... | collective-permute-start | bytes 1572872 | tf_op jit(solution)/shard_map/ppermute | solution.py:295
  32.0 0.8 copy-start.9
  44.8 16.4 %collective-permute-start.19 = (bf16[2,512,256]{2,1,0:T(8,128)(2,1)}, bf16[2,512,256]{2,1,0:T(8,128)(2,1)}, u32[]{:S(2)}, u32[]{:S(2)}) collective-permute-start(bf16[2,512,256]{2,1,0:T(8,128)(2,1)} %get-tuple-element.188), channel_id=1, source_target_pairs={{8,0},{12,4},{16,8},{20,12},{24,16},{28,20},{9,1},{13,5},{17,9},{2... | collective-permute-start | bytes 1572872 | tf_op jit(solution)/shard_map/ppermute | solution.py:300
  46.0 38.4 %collective-permute-start.18 = (bf16[2,512,256]{2,1,0:T(8,128)(2,1)}, bf16[2,512,256]{2,1,0:T(8,128)(2,1)}, u32[]{:S(2)}, u32[]{:S(2)}) collective-permute-start(bf16[2,512,256]{2,1,0:T(8,128)(2,1)} %get-tuple-element.189), channel_id=1, source_target_pairs={{4,0},{8,4},{12,8},{16,12},{20,16},{24,20},{28,24},{5,1},{9,5},{13... | collective-permute-start | bytes 1572872 | tf_op jit(solution)/shard_map/ppermute | solution.py:300
  61.2 23.3 %collective-permute-start.2 = (bf16[2,512,256]{2,1,0:T(8,128)(2,1)}, bf16[2,512,256]{2,1,0:T(8,128)(2,1)}, u32[]{:S(2)}, u32[]{:S(2)}) collective-permute-start(bf16[2,512,256]{2,1,0:T(8,128)(2,1)} %get-tuple-element.58), channel_id=1, source_target_pairs={{4,0},{8,4},{12,8},{16,12},{20,16},{24,20},{28,24},{5,1},{9,5},{13... | collective-permute-start | bytes 1572872 | tf_op jit(solution)/shard_map/cond/branch_1_fun/ppermute | solution.py:300
  62.4 22.0 %collective-permute-start.3 = (bf16[2,512,256]{2,1,0:T(8,128)(2,1)}, bf16[2,512,256]{2,1,0:T(8,128)(2,1)}, u32[]{:S(2)}, u32[]{:S(2)}) collective-permute-start(bf16[2,512,256]{2,1,0:T(8,128)(2,1)} %get-tuple-element.59), channel_id=1, source_target_pairs={{8,0},{12,4},{16,8},{20,12},{24,16},{28,20},{9,1},{13,5},{17,9},{2... | collective-permute-start | bytes 1572872 | tf_op jit(solution)/shard_map/cond/branch_1_fun/ppermute | solution.py:300
  63.8 16.7 %copy-start = (bf16[512,512]{1,0:T(8,128)(2,1)S(1)}, bf16[512,512]{1,0:T(8,128)(2,1)}, u32[]{:S(2)}) copy-start(bf16[512,512]{1,0:T(8,128)(2,1)} %get-tuple-element.52.refs_2_.refs_4_) | copy-start | bytes 1572868 | tf_op jit(solution)/shard_map/cond/branch_1_fun/cond
  70.3 6.2 %collective-permute-start = (bf16[4,672,512]{2,1,0:T(8,128)(2,1)}, bf16[4,672,512]{2,1,0:T(8,128)(2,1)}, u32[]{:S(2)}, u32[]{:S(2)}) collective-permute-start(bf16[4,672,512]{2,1,0:T(8,128)(2,1)} %get-tuple-element.53), channel_id=1, source_target_pairs={{0,4},{4,0},{8,12},{12,8},{16,20},{20,16},{24,28},{28,24},{1,5},{5... | collective-permute-start | bytes 8257544 | tf_op jit(solution)/shard_map/cond/branch_1_fun/cond/branch_1_fun/ppermute | solution.py:295
  71.4 9.0 %collective-permute-start.1 = (bf16[4,672,512]{2,1,0:T(8,128)(2,1)}, bf16[4,672,512]{2,1,0:T(8,128)(2,1)}, u32[]{:S(2)}, u32[]{:S(2)}) collective-permute-start(bf16[4,672,512]{2,1,0:T(8,128)(2,1)} %get-tuple-element.54), channel_id=1, source_target_pairs={{0,4},{4,0},{8,12},{12,8},{16,20},{20,16},{24,28},{28,24},{1,5},{5... | collective-permute-start | bytes 8257544 | tf_op jit(solution)/shard_map/cond/branch_1_fun/cond/branch_1_fun/ppermute | solution.py:295
  102.7 33.8 %collective-permute-start.6 = (bf16[2,672,512]{2,1,0:T(8,128)(2,1)}, bf16[2,672,512]{2,1,0:T(8,128)(2,1)}, u32[]{:S(2)}, u32[]{:S(2)}) collective-permute-start(bf16[2,672,512]{2,1,0:T(8,128)(2,1)} %get-tuple-element.80), channel_id=1, source_target_pairs={{0,8},{4,12},{8,0},{12,4},{16,24},{20,28},{24,16},{28,20},{1,9},{5... | collective-permute-start | bytes 4128776 | tf_op jit(solution)/shard_map/cond/branch_1_fun/ppermute | solution.py:295
  105.2 35.2 %collective-permute-start.7 = (bf16[2,672,512]{2,1,0:T(8,128)(2,1)}, bf16[2,672,512]{2,1,0:T(8,128)(2,1)}, u32[]{:S(2)}, u32[]{:S(2)}) collective-permute-start(bf16[2,672,512]{2,1,0:T(8,128)(2,1)} %get-tuple-element.81), channel_id=1, source_target_pairs={{0,16},{4,20},{8,24},{12,28},{16,0},{20,4},{24,8},{28,12},{1,17},{... | collective-permute-start | bytes 4128776 | tf_op jit(solution)/shard_map/cond/branch_1_fun/ppermute | solution.py:295
  115.6 5.4 %collective-permute-start.4 = (bf16[4,672,512]{2,1,0:T(8,128)(2,1)}, bf16[4,672,512]{2,1,0:T(8,128)(2,1)}, u32[]{:S(2)}, u32[]{:S(2)}) collective-permute-start(bf16[4,672,512]{2,1,0:T(8,128)(2,1)} %get-tuple-element.74), channel_id=1, source_target_pairs={{0,4},{4,0},{8,12},{12,8},{16,20},{20,16},{24,28},{28,24},{1,5},{5... | collective-permute-start | bytes 8257544 | tf_op jit(solution)/shard_map/cond/branch_1_fun/cond/branch_1_fun/ppermute | solution.py:295
  115.6 9.4 %collective-permute-start.5 = (bf16[4,672,512]{2,1,0:T(8,128)(2,1)}, bf16[4,672,512]{2,1,0:T(8,128)(2,1)}, u32[]{:S(2)}, u32[]{:S(2)}) collective-permute-start(bf16[4,672,512]{2,1,0:T(8,128)(2,1)} %get-tuple-element.75), channel_id=1, source_target_pairs={{0,4},{4,0},{8,12},{12,8},{16,20},{20,16},{24,28},{28,24},{1,5},{5... | collective-permute-start | bytes 8257544 | tf_op jit(solution)/shard_map/cond/branch_1_fun/cond/branch_1_fun/ppermute | solution.py:295
  124.9 15.5 %copy-start.1 = (bf16[512,512]{1,0:T(8,128)(2,1)S(1)}, bf16[512,512]{1,0:T(8,128)(2,1)}, u32[]{:S(2)}) copy-start(bf16[512,512]{1,0:T(8,128)(2,1)} %get-tuple-element.92.refs_5_) | copy-start | bytes 1572868 | tf_op jit(solution)/shard_map/cond
  129.3 36.6 %collective-permute-start.10 = (bf16[2,672,512]{2,1,0:T(8,128)(2,1)}, bf16[2,672,512]{2,1,0:T(8,128)(2,1)S(1)}, u32[]{:S(2)}, u32[]{:S(2)}) collective-permute-start(bf16[2,672,512]{2,1,0:T(8,128)(2,1)} %get-tuple-element.88), channel_id=1, source_target_pairs={{0,8},{4,12},{8,0},{12,4},{16,24},{20,28},{24,16},{28,20},{1,9},{5... | collective-permute-start | bytes 4128776 | tf_op jit(solution)/shard_map/cond/branch_1_fun/ppermute | solution.py:295
  129.3 40.4 %collective-permute-start.11 = (bf16[2,672,512]{2,1,0:T(8,128)(2,1)}, bf16[2,672,512]{2,1,0:T(8,128)(2,1)S(1)}, u32[]{:S(2)}, u32[]{:S(2)}) collective-permute-start(bf16[2,672,512]{2,1,0:T(8,128)(2,1)} %get-tuple-element.89), channel_id=1, source_target_pairs={{0,16},{4,20},{8,24},{12,28},{16,0},{20,4},{24,8},{28,12},{1,17},{... | collective-permute-start | bytes 4128776 | tf_op jit(solution)/shard_map/cond/branch_1_fun/ppermute | solution.py:295
  140.4 30.5 %copy-start.2 = (bf16[512,512]{1,0:T(8,128)(2,1)S(1)}, bf16[512,512]{1,0:T(8,128)(2,1)}, u32[]{:S(2)}) copy-start(bf16[512,512]{1,0:T(8,128)(2,1)} %get-tuple-element.82.refs_1_) | copy-start | bytes 1572868 | tf_op jit(solution)/shard_map/cond
  140.4 30.5 %copy-start.3 = (bf16[512,512]{1,0:T(8,128)(2,1)S(1)}, bf16[512,512]{1,0:T(8,128)(2,1)}, u32[]{:S(2)}) copy-start(bf16[512,512]{1,0:T(8,128)(2,1)} %get-tuple-element.85.refs_4_.refs_5_) | copy-start | bytes 1572868 | tf_op jit(solution)/shard_map/cond
  144.1 40.4 %collective-permute-start.8 = (bf16[1,672,512]{2,1,0:T(8,128)(2,1)}, bf16[1,672,512]{2,1,0:T(8,128)(2,1)S(1)}, u32[]{:S(2)}, u32[]{:S(2)}) collective-permute-start(bf16[1,672,512]{2,1,0:T(8,128)(2,1)} %get-tuple-element.95), channel_id=1, source_target_pairs={{0,16},{4,20},{8,24},{12,28},{16,0},{20,4},{24,8},{28,12},{1,17},{... | collective-permute-start | bytes 2064392 | tf_op jit(solution)/shard_map/cond/branch_1_fun/ppermute | solution.py:295
  146.2 38.4 %collective-permute-start.9 = (bf16[1,672,512]{2,1,0:T(8,128)(2,1)}, bf16[1,672,512]{2,1,0:T(8,128)(2,1)}, u32[]{:S(2)}, u32[]{:S(2)}) collective-permute-start(bf16[1,672,512]{2,1,0:T(8,128)(2,1)} %get-tuple-element.96), channel_id=1, source_target_pairs={{0,8},{4,12},{8,0},{12,4},{16,24},{20,28},{24,16},{28,20},{1,9},{5... | collective-permute-start | bytes 2064392 | tf_op jit(solution)/shard_map/cond/branch_1_fun/ppermute | solution.py:295
  165.9 3.9 %copy-start.4 = (bf16[2,672,512]{2,1,0:T(8,128)(2,1)}, bf16[2,672,512]{2,1,0:T(8,128)(2,1)S(1)}, u32[]{:S(2)}) copy-start(bf16[2,672,512]{2,1,0:T(8,128)(2,1)S(1)} %collective-permute-done.10.refs_3_) | copy-start | bytes 4128772 | tf_op jit(solution)/shard_map/cond
  169.8 1.1 copy-start.5
  174.5 23.9 %collective-permute-start.12 = (bf16[1,672,512]{2,1,0:T(8,128)(2,1)}, bf16[1,672,512]{2,1,0:T(8,128)(2,1)S(1)}, u32[]{:S(2)}, u32[]{:S(2)}) collective-permute-start(bf16[1,672,512]{2,1,0:T(8,128)(2,1)} %get-tuple-element.101), channel_id=1, source_target_pairs={{0,16},{4,20},{8,24},{12,28},{16,0},{20,4},{24,8},{28,12},{1,17},{... | collective-permute-start | bytes 2064392 | tf_op jit(solution)/shard_map/cond/branch_1_fun/ppermute | solution.py:295
  176.6 21.9 %collective-permute-start.13 = (bf16[1,672,512]{2,1,0:T(8,128)(2,1)}, bf16[1,672,512]{2,1,0:T(8,128)(2,1)S(1)}, u32[]{:S(2)}, u32[]{:S(2)}) collective-permute-start(bf16[1,672,512]{2,1,0:T(8,128)(2,1)} %get-tuple-element.102), channel_id=1, source_target_pairs={{0,8},{4,12},{8,0},{12,4},{16,24},{20,28},{24,16},{28,20},{1,9},{5... | collective-permute-start | bytes 2064392 | tf_op jit(solution)/shard_map/cond/branch_1_fun/ppermute | solution.py:295
  184.5 0.8 copy-start.6
  198.5 0.8 copy-start.7
  199.3 0.9 copy-start.8
Sparse Core Ops, SparseCore 0:
  102.8 102.4 reduce-scatter.1

commit v6 on v5

--- a/solution.py
+++ b/solution.py
@@ -15,7 +15,7 @@
 TILE = 256
 SCALE = (D // H) ** (-0.5)
 FAR = -1e30
-VMEM_BYTES = 56 * 1024 * 1024
+VMEM_BYTES = 40 * 1024 * 1024
 
 NT = (((1,), (1,)), ((), ()))
 TN = (((0,), (0,)), ((), ()))

time: 213 us -> 216 us (1.014)
  Pallas kernels: 86.2 us -> 75.3 us
  waiting for transfers between devices: 72 us -> 82 us
  local copies, waits for them, and re-layouts: 5.58 us -> 11.9 us
    unnamed x8 -> x28, local copies, waits for them, and re-layouts: 0.8 us -> 10.8 us
    ppermute x13, waiting for transfers between devices: 69 us -> 76.7 us  [swapped(): return lax.ppermute(block, 'seq', [(i, i ^ bit) for i in range(size)])]
    pallas_call x8, Pallas kernels: 37.1 us -> 30.5 us  [paired_products(): pl.pallas_call(functools.partial(paired_kernel, len(arrived), shared, joi...]
    cond x18 -> x14, local copies, waits for them, and re-layouts: 3.67 us -> 0.03 us
  transfers between devices with their start and end apart: 21 -> 21, of which waited for: 13 -> 14; matrix products, arithmetic and copies ran while one was open for 1% -> 1% of each run, Pallas kernels for 32% -> 27%
where the time goes in v6:
time: 216 us; the launch traced here: 215 us
  waiting for transfers between devices  82 us (38%)
  Pallas kernels  75.3 us (35%)
  starting transfers between devices  30.3 us (14%)
  between operations  14.2 us (7%)
  local copies, waits for them, and re-layouts  11.9 us (6%)
    ppermute x13, waiting for transfers between devices, swapped(): return lax.ppermute(block, 'seq', [(i, i ^ bit) for i in range(size)])  76.7 us
    pallas_call x8, Pallas kernels, paired_products(): pl.pallas_call(functools.partial(paired_kernel, len(arrived), shared, joi...  30.5 us
    pallas_call x2, Pallas kernels, attention(): pl.pallas_call(functools.partial(attention_kernel, groups, depth), grid=(...  22.9 us
    ppermute x7, starting transfers between devices, shifted(): lax.ppermute(block, 'seq', [(i, i + distance) for i in range(size) if 0 <...  16.7 us
    pallas_call x1, Pallas kernels, input_term(): pl.pallas_call(functools.partial(term_kernel, sets), grid=(parts,), in_sp...  16.2 us
    ppermute x13, starting transfers between devices, swapped(): return lax.ppermute(block, 'seq', [(i, i ^ bit) for i in range(size)])  13.6 us
    unnamed x28, local copies, waits for them, and re-layouts  10.8 us
    pallas_call x1, Pallas kernels, arranged(): pl.pallas_call(functools.partial(arrange_kernel, offsets), grid_spec=pltp...  5.68 us
  transfers between devices with their start and end apart: 21, of which 14 were waited for; matrix products, arithmetic and copies ran while one was open for 1% of the time, Pallas kernels for 27%

profile of v6, /device:TPU:0, one launch (start us, length us, event | category | flops | bytes accessed | tf_op | source)
XLA Modules:
  0.0 215.4 jit_solution(1980976543079537868)
XLA Ops:
  7.2 1.1 slice_bitcast_fusion.2
  8.3 5.6 %collective-permute-start.14 = (bf16[2,512,256]{2,1,0:T(8,128)(2,1)S(1)}, bf16[2,512,256]{2,1,0:T(8,128)(2,1)}, u32[]{:S(2)}, u32[]{:S(2)}) collective-permute-start(bf16[2,512,256]{2,1,0:T(8,128)(2,1)S(1)} %pad_maximum_fusion.refs_2_), channel_id=1, source_target_pairs={{0,8},{4,12},{8,16},{12,20},{16,24},{20,28},{1,9},{5,13},{9,17},{1... | collective-permute-start | bytes 1572872 | tf_op jit(solution)/shard_map/ppermute | solution.py:300
  14.0 2.6 %copy-done = bf16[512,5376]{1,0:T(8,128)(2,1)S(1)} copy-done((bf16[512,5376]{1,0:T(8,128)(2,1)S(1)}, bf16[512,5376]{1,0:T(8,128)(2,1)}, u32[]{:S(2)}) %copy-start) | copy-done | bytes 5505048
  16.6 5.7 %arranged_input.1 = (bf16[4,672,512]{2,1,0:T(8,128)(2,1)}, bf16[4,672,512]{2,1,0:T(8,128)(2,1)}) custom-call(s32[1]{0:T(128)} %bitcast.7.me_ref, bf16[512,5376]{1,0:T(8,128)(2,1)S(1)} %copy-done), custom_call_target="tpu_custom_call" | custom-call | tf_op jit(solution)/shard_map/arranged_input/pallas_call | solution.py:171
  22.4 3.5 %collective-permute-start.16 = (bf16[2,512,256]{2,1,0:T(8,128)(2,1)S(1)}, bf16[2,512,256]{2,1,0:T(8,128)(2,1)}, u32[]{:S(2)}, u32[]{:S(2)}) collective-permute-start(bf16[2,512,256]{2,1,0:T(8,128)(2,1)S(1)} %pad_maximum_fusion.1.refs_2_), channel_id=1, source_target_pairs={{0,8},{4,12},{8,16},{12,20},{16,24},{20,28},{1,9},{5,13},{9,17},{1... | collective-permute-start | bytes 1572872 | tf_op jit(solution)/shard_map/ppermute | solution.py:300
  25.9 2.1 collective-permute-start.17
  28.2 1.0 broadcast_select_fusion
  30.2 1.4 collective-permute-done.15.refs_1_
  31.7 11.4 %attention_grads.2 = (bf16[512,512]{1,0:T(8,128)(2,1)}, bf16[2,512,256]{2,1,0:T(8,128)(2,1)}, bf16[2,512,256]{2,1,0:T(8,128)(2,1)}, f32[2,512,256]{2,1,0:T(8,128)S(1)}) custom-call(s32[1,512]{1,0:T(1,128)S(1)} %subtract_add_fusion.lowest_ref, bf16[512,1024]{1,0:T(8,128)(2,1)S(1)} %copy-done.3, bf16[512,1024]{1,0:T(8,128)(2,1)S(1)} %copy-done.4, ...), custom_call_target="tpu_custom_call" | custom-call | tf_op jit(solution)/shard_map/attention_grads/pallas_call | solution.py:123
  44.0 1.3 collective-permute-start.19
  45.3 1.5 collective-permute-start.18
  46.8 11.6 %attention_grads.3 = (bf16[512,512]{1,0:T(8,128)(2,1)}, bf16[2,512,256]{2,1,0:T(8,128)(2,1)}, bf16[2,512,256]{2,1,0:T(8,128)(2,1)}, f32[2,512,256]{2,1,0:T(8,128)S(1)}) custom-call(s32[1,512]{1,0:T(1,128)S(1)} %subtract_add_fusion.lowest_ref, bf16[512,1024]{1,0:T(8,128)(2,1)S(1)} %copy-done.3, bf16[512,1024]{1,0:T(8,128)(2,1)S(1)} %copy-done.4, ...), custom_call_target="tpu_custom_call" | custom-call | tf_op jit(solution)/shard_map/attention_grads/pallas_call | solution.py:123
  58.4 1.9 collective-permute-done.19.refs_4_
  60.3 23.0 %conditional.4 = (bf16[2,512,256]{2,1,0:T(8,128)(2,1)}, bf16[2,512,256]{2,1,0:T(8,128)(2,1)}, bf16[4,672,512]{2,1,0:T(8,128)(2,1)}, bf16[4,672,512]{2,1,0:T(8,12...) conditional(s32[]{:T(128)} %convert_element_type.10, () %tuple.62, ...), branch_computations={%region_2.3_spmd, %region_3.6_spmd} | conditional | flops 1 | bytes 41419112 | solution.py:370
  60.3 1.4 collective-permute-start.2
  61.7 1.3 collective-permute-start.3
  63.0 19.6 %conditional = (bf16[4,672,512]{2,1,0:T(8,128)(2,1)}, bf16[4,672,512]{2,1,0:T(8,128)(2,1)}, bf16[2,672,512]{2,1,0:T(8,128)(2,1)}, bf16[2,672,512]{2,1,0:T(8,128)(2,1)}) conditional(s32[]{:T(128)} %convert_element_type.3, () %tuple.28, (bf16[4,672,512]{2,1,0:T(8,128)(2,1)}, bf16[512,512]{1,0:T(8,128)(2,1)}, bf16[512,512]{1,0:T(8,128)(2,1)}, ...), branch_computations={%region_4.4_spmd, %region_5.5_spmd} | conditional | bytes 37224644 | solution.py:370
  63.1 5.4 %projection_products.8 = (bf16[4,672,512]{2,1,0:T(8,128)(2,1)S(1)}, bf16[4,672,512]{2,1,0:T(8,128)(2,1)S(1)}) custom-call(bf16[4,672,512]{2,1,0:T(8,128)(2,1)} %get-tuple-element.50.refs_0_, bf16[512,512]{1,0:T(8,128)(2,1)} %get-tuple-element.51.refs_1_, bf16[512,512]{1,0:T(8,128)(2,1)} %get-tuple-element.52.refs_2_.refs_4_), custom_call_target="tpu_custom_call" | custom-call | tf_op jit(solution)/shard_map/cond/branch_1_fun/cond/branch_1_fun/projection_products/pallas_call | solution.py:236
  68.5 1.2 collective-permute-start
  69.8 4.8 %collective-permute-done.refs_2_ = bf16[4,672,512]{2,1,0:T(8,128)(2,1)} collective-permute-done((bf16[4,672,512]{2,1,0:T(8,128)(2,1)S(1)}, bf16[4,672,512]{2,1,0:T(8,128)(2,1)}, u32[]{:S(2)}, u32[]{:S(2)}) %collective-permute-start) | collective-permute-done | bytes 2752544 | tf_op jit(solution)/shard_map/cond/branch_1_fun/cond/branch_1_fun/ppermute | solution.py:295
  74.5 3.9 %collective-permute-done.1.refs_5_ = bf16[4,672,512]{2,1,0:T(8,128)(2,1)} collective-permute-done((bf16[4,672,512]{2,1,0:T(8,128)(2,1)S(1)}, bf16[4,672,512]{2,1,0:T(8,128)(2,1)}, u32[]{:S(2)}, u32[]{:S(2)}) %collective-permute-start.1) | collective-permute-done | bytes 2752544 | tf_op jit(solution)/shard_map/cond/branch_1_fun/cond/branch_1_fun/ppermute | solution.py:295
  78.5 4.1 %projection_products.9 = (bf16[2,672,512]{2,1,0:T(8,128)(2,1)}, bf16[2,672,512]{2,1,0:T(8,128)(2,1)}) custom-call(bf16[4,672,512]{2,1,0:T(8,128)(2,1)S(1)} %copy-done.9, bf16[512,512]{1,0:T(8,128)(2,1)S(1)} %copy-done.12, bf16[4,672,512]{2,1,0:T(8,128)(2,1)} %collective-permute-done.refs_2_, bf16[4,672,512]{2,1,0:T(8,128)(2,1)S(1)} %copy-done.9, ...), custom_call_target="tpu_custom_call" | custom-call | tf_op jit(solution)/shard_map/cond/branch_1_fun/cond/branch_1_fun/projection_products/pallas_call | solution.py:236
  83.3 2.6 %copy-done.1 = bf16[5376,512]{1,0:T(8,128)(2,1)S(1)} copy-done((bf16[5376,512]{1,0:T(8,128)(2,1)S(1)}, bf16[5376,512]{1,0:T(8,128)(2,1)}, u32[]{:S(2)}) %copy-start.1) | copy-done | bytes 5505048
  85.8 1.2 copy-done.8
  87.1 16.2 %input_term.1 = (bf16[4,1344,512]{2,1,0:T(8,128)(2,1)S(1)}, bf16[512,512]{1,0:T(8,128)(2,1)}, bf16[512,512]{1,0:T(8,128)(2,1)}) custom-call(bf16[512,512]{1,0:T(8,128)(2,1)} %get-tuple-element.230.refs_0_, bf16[512,512]{1,0:T(8,128)(2,1)} %get-tuple-element.231.refs_1_, f32[2,512,256]{2,1,0:T(8,128)S(1)} %copy-done.6, ...), custom_call_target="tpu_custom_call" | custom-call | tf_op jit(solution)/shard_map/input_term/pallas_call | solution.py:281
  103.2 2.4 %copy-done.2 = bf16[4,1344,512]{2,1,0:T(8,128)(2,1)} copy-done((bf16[4,1344,512]{2,1,0:T(8,128)(2,1)}, bf16[4,1344,512]{2,1,0:T(8,128)(2,1)S(1)}, u32[]{:S(2)}) %copy-start.2) | copy-done | bytes 5505048
  105.7 1.0 copy-done.11
  106.7 99.0 %conditional.5 = (bf16[672,1024]{1,0:T(8,128)(2,1)}, bf16[672,512]{1,0:T(8,128)(2,1)}, bf16[672,512]{1,0:T(8,128)(2,1)}) conditional(s32[]{:T(128)} %convert_element_type.10, () %tuple.65, (bf16[2,672,512]{2,1,0:T(8,128)(2,1)}, bf16[2,672,512]{2,1,0:T(8,128)(2,1)}, pred[]{:T(512)}, bf16[4,672,512]{2,1,0:T(8,128)(2,1)}, bf16[512,512]{1,0:T(8,128)(2,1)}, ...), branch_computations={%region_7.8_spmd, %region_8.11_spmd} | conditional | flops 1 | bytes 72352320 | solution.py:370
  106.7 3.0 %collective-permute-start.6 = (bf16[2,672,512]{2,1,0:T(8,128)(2,1)}, bf16[2,672,512]{2,1,0:T(8,128)(2,1)S(1)}, u32[]{:S(2)}, u32[]{:S(2)}) collective-permute-start(bf16[2,672,512]{2,1,0:T(8,128)(2,1)} %get-tuple-element.80), channel_id=1, source_target_pairs={{0,8},{4,12},{8,0},{12,4},{16,24},{20,28},{24,16},{28,20},{1,9},{5... | collective-permute-start | bytes 4128776 | tf_op jit(solution)/shard_map/cond/branch_1_fun/ppermute | solution.py:295
  109.7 3.4 %collective-permute-start.7 = (bf16[2,672,512]{2,1,0:T(8,128)(2,1)}, bf16[2,672,512]{2,1,0:T(8,128)(2,1)S(1)}, u32[]{:S(2)}, u32[]{:S(2)}) collective-permute-start(bf16[2,672,512]{2,1,0:T(8,128)(2,1)} %get-tuple-element.81), channel_id=1, source_target_pairs={{0,16},{4,20},{8,24},{12,28},{16,0},{20,4},{24,8},{28,12},{1,17},{... | collective-permute-start | bytes 4128776 | tf_op jit(solution)/shard_map/cond/branch_1_fun/ppermute | solution.py:295
  113.1 14.7 %conditional.1 = (bf16[4,672,512]{2,1,0:T(8,128)(2,1)}, bf16[4,672,512]{2,1,0:T(8,128)(2,1)}) conditional(s32[]{:T(128)} %convert_element_type.8, () %tuple.35, (bf16[4,672,512]{2,1,0:T(8,128)(2,1)}, bf16[512,512]{1,0:T(8,128)(2,1)}, bf16[512,512]{1,0:T(8,128)(2,1)}) %tuple.36), branch_computations={%region_9.9_spmd, %region_10.10_spmd} | conditional | bytes 22020192 | solution.py:370
  113.1 5.4 %projection_products.10 = (bf16[4,672,512]{2,1,0:T(8,128)(2,1)S(1)}, bf16[4,672,512]{2,1,0:T(8,128)(2,1)S(1)}) custom-call(bf16[4,672,512]{2,1,0:T(8,128)(2,1)} %get-tuple-element.71.refs_0_, bf16[512,512]{1,0:T(8,128)(2,1)} %get-tuple-element.72.refs_1_, bf16[512,512]{1,0:T(8,128)(2,1)} %get-tuple-element.73.refs_2_), custom_call_target="tpu_custom_call" | custom-call | tf_op jit(solution)/shard_map/cond/branch_1_fun/cond/branch_1_fun/projection_products/pallas_call | solution.py:236
  119.1 4.7 %collective-permute-done.4 = bf16[4,672,512]{2,1,0:T(8,128)(2,1)} collective-permute-done((bf16[4,672,512]{2,1,0:T(8,128)(2,1)S(1)}, bf16[4,672,512]{2,1,0:T(8,128)(2,1)}, u32[]{:S(2)}, u32[]{:S(2)}) %collective-permute-start.4) | collective-permute-done | bytes 2752544 | tf_op jit(solution)/shard_map/cond/branch_1_fun/cond/branch_1_fun/ppermute | solution.py:295
  123.9 3.9 %collective-permute-done.5 = bf16[4,672,512]{2,1,0:T(8,128)(2,1)} collective-permute-done((bf16[4,672,512]{2,1,0:T(8,128)(2,1)S(1)}, bf16[4,672,512]{2,1,0:T(8,128)(2,1)}, u32[]{:S(2)}, u32[]{:S(2)}) %collective-permute-start.5) | collective-permute-done | bytes 2752544 | tf_op jit(solution)/shard_map/cond/branch_1_fun/cond/branch_1_fun/ppermute | solution.py:295
  127.8 4.2 %projection_products.11 = (bf16[2,672,512]{2,1,0:T(8,128)(2,1)S(1)}, bf16[2,672,512]{2,1,0:T(8,128)(2,1)S(1)}) custom-call(bf16[4,672,512]{2,1,0:T(8,128)(2,1)} %get-tuple-element.76.refs_0_.refs_3_.refs_4_, bf16[512,512]{1,0:T(8,128)(2,1)} %get-tuple-element.82.refs_1_, bf16[4,672,512]{2,1,0:T(8,128)(2,1)} %get-tuple-element.109.refs_2_, ...), custom_call_target="tpu_custom_call" | custom-call | tf_op jit(solution)/shard_map/cond/branch_1_fun/projection_products/pallas_call | solution.py:236
  132.2 8.8 %collective-permute-done.6.refs_3_ = bf16[2,672,512]{2,1,0:T(8,128)(2,1)S(1)} collective-permute-done((bf16[2,672,512]{2,1,0:T(8,128)(2,1)}, bf16[2,672,512]{2,1,0:T(8,128)(2,1)S(1)}, u32[]{:S(2)}, u32[]{:S(2)}) %collective-permute-start.6) | collective-permute-done | bytes 1376288 | tf_op jit(solution)/shard_map/cond/branch_1_fun/ppermute | solution.py:295
  141.0 3.4 %collective-permute-done.7.refs_7_ = bf16[2,672,512]{2,1,0:T(8,128)(2,1)S(1)} collective-permute-done((bf16[2,672,512]{2,1,0:T(8,128)(2,1)}, bf16[2,672,512]{2,1,0:T(8,128)(2,1)S(1)}, u32[]{:S(2)}, u32[]{:S(2)}) %collective-permute-start.7) | collective-permute-done | bytes 1376288 | tf_op jit(solution)/shard_map/cond/branch_1_fun/ppermute | solution.py:295
  144.3 2.4 %projection_products.12 = (bf16[1,672,512]{2,1,0:T(8,128)(2,1)S(1)}, bf16[1,672,512]{2,1,0:T(8,128)(2,1)S(1)}) custom-call(bf16[4,672,512]{2,1,0:T(8,128)(2,1)S(1)} %copy-done.10, bf16[512,512]{1,0:T(8,128)(2,1)S(1)} %get-tuple-element.77.refs_1_, bf16[4,672,512]{2,1,0:T(8,128)(2,1)} %get-tuple-element.103.refs_2_, ...), custom_call_target="tpu_custom_call" | custom-call | tf_op jit(solution)/shard_map/cond/branch_1_fun/projection_products/pallas_call | solution.py:236
  146.7 2.1 collective-permute-start.8
  148.9 21.6 %collective-permute-done.10.refs_3_ = bf16[2,672,512]{2,1,0:T(8,128)(2,1)S(1)} collective-permute-done((bf16[2,672,512]{2,1,0:T(8,128)(2,1)S(1)}, bf16[2,672,512]{2,1,0:T(8,128)(2,1)S(1)}, u32[]{:S(2)}, u32[]{:S(2)}) %collective-permute-start.10) | collective-permute-done | bytes 1376288 | tf_op jit(solution)/shard_map/cond/branch_1_fun/ppermute | solution.py:295
  170.4 3.4 %collective-permute-done.11.refs_7_ = bf16[2,672,512]{2,1,0:T(8,128)(2,1)S(1)} collective-permute-done((bf16[2,672,512]{2,1,0:T(8,128)(2,1)S(1)}, bf16[2,672,512]{2,1,0:T(8,128)(2,1)S(1)}, u32[]{:S(2)}, u32[]{:S(2)}) %collective-permute-start.11) | collective-permute-done | bytes 1376288 | tf_op jit(solution)/shard_map/cond/branch_1_fun/ppermute | solution.py:295
  173.8 2.3 %projection_products.13 = (bf16[1,672,512]{2,1,0:T(8,128)(2,1)S(1)}, bf16[1,672,512]{2,1,0:T(8,128)(2,1)S(1)}) custom-call(bf16[4,672,512]{2,1,0:T(8,128)(2,1)S(1)} %copy-done.10, bf16[512,512]{1,0:T(8,128)(2,1)S(1)} %copy-done.15, bf16[4,672,512]{2,1,0:T(8,128)(2,1)} %get-tuple-element.109.refs_2_, ...), custom_call_target="tpu_custom_call" | custom-call | tf_op jit(solution)/shard_map/cond/branch_1_fun/projection_products/pallas_call | solution.py:236
  176.1 2.1 collective-permute-start.12
  178.3 10.3 %collective-permute-done.8.refs_4_ = bf16[1,672,512]{2,1,0:T(8,128)(2,1)S(1)} collective-permute-done((bf16[1,672,512]{2,1,0:T(8,128)(2,1)S(1)}, bf16[1,672,512]{2,1,0:T(8,128)(2,1)S(1)}, u32[]{:S(2)}, u32[]{:S(2)}) %collective-permute-start.8) | collective-permute-done | bytes 688160 | tf_op jit(solution)/shard_map/cond/branch_1_fun/ppermute | solution.py:295
  188.6 3.4 %projection_products.14 = bf16[672,1024]{1,0:T(8,128)(2,1)} custom-call(bf16[4,672,512]{2,1,0:T(8,128)(2,1)S(1)} %copy-done.10, bf16[512,512]{1,0:T(8,128)(2,1)S(1)} %get-tuple-element.77.refs_1_, bf16[4,672,512]{2,1,0:T(8,128)(2,1)} %get-tuple-element.103.refs_2_, bf16[2,672,512]{2,1,0:T(8,128)(2,1)S(1)} %collective-permute-done.6.refs_3_, ...), custom_call_target="tpu_custom_call" | custom-call | tf_op jit(solution)/shard_map/cond/branch_1_fun/projection_products/pallas_call | solution.py:236
  192.0 10.5 %collective-permute-done.12.refs_4_ = bf16[1,672,512]{2,1,0:T(8,128)(2,1)S(1)} collective-permute-done((bf16[1,672,512]{2,1,0:T(8,128)(2,1)S(1)}, bf16[1,672,512]{2,1,0:T(8,128)(2,1)S(1)}, u32[]{:S(2)}, u32[]{:S(2)}) %collective-permute-start.12) | collective-permute-done | bytes 688160 | tf_op jit(solution)/shard_map/cond/branch_1_fun/ppermute | solution.py:295
  202.5 3.2 %projection_products.15 = (bf16[1,672,512]{2,1,0:T(8,128)(2,1)}, bf16[1,672,512]{2,1,0:T(8,128)(2,1)}) custom-call(bf16[4,672,512]{2,1,0:T(8,128)(2,1)S(1)} %copy-done.10, bf16[512,512]{1,0:T(8,128)(2,1)S(1)} %copy-done.15, bf16[4,672,512]{2,1,0:T(8,128)(2,1)} %get-tuple-element.109.refs_2_, bf16[2,672,512]{2,1,0:T(8,128)(2,1)S(1)} %collective-permute-done.10.refs_3_, ...), custom_call_target="tpu_custom_call" | custom-call | tf_op jit(solution)/shard_map/cond/branch_1_fun/projection_products/pallas_call | solution.py:236
  205.7 2.8 %reduce-scatter.2.cloned.1.call-done = bf16[1,1344,512]{2,1,0:T(8,128)(2,1)} async-done(((bf16[4,1344,512]{2,1,0:T(8,128)(2,1)}), bf16[1,1344,512]{2,1,0:T(8,128)(2,1)}) %reduce-scatter.2.cloned.1.call-update) | async-done | bytes 1376272 | tf_op jit(solution)/shard_map/reduce_scatter | solution.py:472
  (64 shorter events, 3.9 us)
Async XLA Ops:
  7.2 201.3 %reduce-scatter.2.cloned.1.call-start = ((), (), s32[]{:S(2)}) async-start(), calls=%async_computation.1 | async-start | bytes 6881280 | tf_op jit(solution)/shard_map/reduce_scatter | solution.py:472
  8.3 5.7 %copy-start.17 = (bf16[1,512,256]{2,1,0:T(8,128)(2,1)}, bf16[1,512,256]{2,1,0:T(8,128)(2,1)S(1)}, u32[]{:S(2)}) copy-start(bf16[1,512,256]{2,1,0:T(8,128)(2,1)S(1)} %get-tuple-element.236) | copy-start | bytes 786436
  8.3 19.8 %collective-permute-start.14 = (bf16[2,512,256]{2,1,0:T(8,128)(2,1)S(1)}, bf16[2,512,256]{2,1,0:T(8,128)(2,1)}, u32[]{:S(2)}, u32[]{:S(2)}) collective-permute-start(bf16[2,512,256]{2,1,0:T(8,128)(2,1)S(1)} %pad_maximum_fusion.refs_2_), channel_id=1, source_target_pairs={{0,8},{4,12},{8,16},{12,20},{16,24},{20,28},{1,9},{5,13},{9,17},{1... | collective-permute-start | bytes 1572872 | tf_op jit(solution)/shard_map/ppermute | solution.py:300
  14.0 2.6 %copy-start = (bf16[512,5376]{1,0:T(8,128)(2,1)S(1)}, bf16[512,5376]{1,0:T(8,128)(2,1)}, u32[]{:S(2)}) copy-start(bf16[512,5376]{1,0:T(8,128)(2,1)} %x_ref) | copy-start | bytes 16515076
  16.6 5.7 %copy-start.18 = (bf16[512,512]{1,0:T(8,128)(2,1)S(1)}, bf16[512,512]{1,0:T(8,128)(2,1)}, u32[]{:S(2)}) copy-start(bf16[512,512]{1,0:T(8,128)(2,1)} %param.20) | copy-start | bytes 1572868
  16.6 5.7 %copy-start.19 = (bf16[512,512]{1,0:T(8,128)(2,1)S(1)}, bf16[512,512]{1,0:T(8,128)(2,1)}, u32[]{:S(2)}) copy-start(bf16[512,512]{1,0:T(8,128)(2,1)} %param.19) | copy-start | bytes 1572868
  16.6 11.4 %copy-start.20 = (s32[8]{0:T(128)S(1)}, s32[8]{0:T(128)}, u32[]{:S(2)}) copy-start(s32[8]{0:T(128)} %param.25) | copy-start | bytes 100
  22.2 9.4 %copy-start.3 = (bf16[512,1024]{1,0:T(8,128)(2,1)S(1)}, bf16[512,1024]{1,0:T(8,128)(2,1)}, u32[]{:S(2)}) copy-start(bf16[512,1024]{1,0:T(8,128)(2,1)} %q_ref.3) | copy-start | bytes 3145732
  22.3 9.4 %copy-start.4 = (bf16[512,1024]{1,0:T(8,128)(2,1)S(1)}, bf16[512,1024]{1,0:T(8,128)(2,1)}, u32[]{:S(2)}) copy-start(bf16[512,1024]{1,0:T(8,128)(2,1)} %g_ref.3) | copy-start | bytes 3145732
  22.4 24.4 %collective-permute-start.16 = (bf16[2,512,256]{2,1,0:T(8,128)(2,1)S(1)}, bf16[2,512,256]{2,1,0:T(8,128)(2,1)}, u32[]{:S(2)}, u32[]{:S(2)}) collective-permute-start(bf16[2,512,256]{2,1,0:T(8,128)(2,1)S(1)} %pad_maximum_fusion.1.refs_2_), channel_id=1, source_target_pairs={{0,8},{4,12},{8,16},{12,20},{16,24},{20,28},{1,9},{5,13},{9,17},{1... | collective-permute-start | bytes 1572872 | tf_op jit(solution)/shard_map/ppermute | solution.py:300
  25.9 20.9 %collective-permute-start.17 = (bf16[2,512,256]{2,1,0:T(8,128)(2,1)S(1)}, bf16[2,512,256]{2,1,0:T(8,128)(2,1)}, u32[]{:S(2)}, u32[]{:S(2)}) collective-permute-start(bf16[2,512,256]{2,1,0:T(8,128)(2,1)S(1)} %pad_maximum_fusion.1.refs_2_), channel_id=1, source_target_pairs={{0,4},{4,8},{8,12},{12,16},{16,20},{20,24},{24,28},{1,5},{5,9},{9,... | collective-permute-start | bytes 1572872 | tf_op jit(solution)/shard_map/ppermute | solution.py:300
  29.2 2.4 %collective-permute-start.15 = (bf16[2,512,256]{2,1,0:T(8,128)(2,1)S(1)}, bf16[2,512,256]{2,1,0:T(8,128)(2,1)S(1)}, u32[]{:S(2)}, u32[]{:S(2)}) collective-permute-start(bf16[2,512,256]{2,1,0:T(8,128)(2,1)S(1)} %broadcast_select_fusion), channel_id=1, source_target_pairs={{0,4},{4,0},{8,12},{12,8},{16,20},{20,16},{24,28},{28,24},{1,5},{5... | collective-permute-start | bytes 1572872 | tf_op jit(solution)/shard_map/ppermute | solution.py:295
  43.0 1.0 copy-start.5
  44.0 16.3 %collective-permute-start.19 = (bf16[2,512,256]{2,1,0:T(8,128)(2,1)}, bf16[2,512,256]{2,1,0:T(8,128)(2,1)S(1)}, u32[]{:S(2)}, u32[]{:S(2)}) collective-permute-start(bf16[2,512,256]{2,1,0:T(8,128)(2,1)} %get-tuple-element.188), channel_id=1, source_target_pairs={{8,0},{12,4},{16,8},{20,12},{24,16},{28,20},{9,1},{13,5},{17,9},{2... | collective-permute-start | bytes 1572872 | tf_op jit(solution)/shard_map/ppermute | solution.py:300
  45.3 38.0 %collective-permute-start.18 = (bf16[2,512,256]{2,1,0:T(8,128)(2,1)}, bf16[2,512,256]{2,1,0:T(8,128)(2,1)}, u32[]{:S(2)}, u32[]{:S(2)}) collective-permute-start(bf16[2,512,256]{2,1,0:T(8,128)(2,1)} %get-tuple-element.189), channel_id=1, source_target_pairs={{4,0},{8,4},{12,8},{16,12},{20,16},{24,20},{28,24},{5,1},{9,5},{13... | collective-permute-start | bytes 1572872 | tf_op jit(solution)/shard_map/ppermute | solution.py:300
  58.4 1.9 copy-start.7
  60.3 23.0 %copy-start.6 = (f32[2,512,256]{2,1,0:T(8,128)S(1)}, f32[2,512,256]{2,1,0:T(8,128)}, u32[]{:S(2)}) copy-start(f32[2,512,256]{2,1,0:T(8,128)} %copy-done.5) | copy-start | bytes 3145732
  60.3 22.3 %collective-permute-start.2 = (bf16[2,512,256]{2,1,0:T(8,128)(2,1)}, bf16[2,512,256]{2,1,0:T(8,128)(2,1)}, u32[]{:S(2)}, u32[]{:S(2)}) collective-permute-start(bf16[2,512,256]{2,1,0:T(8,128)(2,1)} %get-tuple-element.58), channel_id=1, source_target_pairs={{4,0},{8,4},{12,8},{16,12},{20,16},{24,20},{28,24},{5,1},{9,5},{13... | collective-permute-start | bytes 1572872 | tf_op jit(solution)/shard_map/cond/branch_1_fun/ppermute | solution.py:300
  61.7 21.5 %collective-permute-start.3 = (bf16[2,512,256]{2,1,0:T(8,128)(2,1)}, bf16[2,512,256]{2,1,0:T(8,128)(2,1)}, u32[]{:S(2)}, u32[]{:S(2)}) collective-permute-start(bf16[2,512,256]{2,1,0:T(8,128)(2,1)} %get-tuple-element.59), channel_id=1, source_target_pairs={{8,0},{12,4},{16,8},{20,12},{24,16},{28,20},{9,1},{13,5},{17,9},{2... | collective-permute-start | bytes 1572872 | tf_op jit(solution)/shard_map/cond/branch_1_fun/ppermute | solution.py:300
  63.0 15.4 %copy-start.9 = (bf16[4,672,512]{2,1,0:T(8,128)(2,1)S(1)}, bf16[4,672,512]{2,1,0:T(8,128)(2,1)}, u32[]{:S(2)}) copy-start(bf16[4,672,512]{2,1,0:T(8,128)(2,1)} %get-tuple-element.55.refs_0_.refs_3_) | copy-start | bytes 8257540 | tf_op jit(solution)/shard_map/cond/branch_1_fun/cond
  63.1 15.4 %copy-start.12 = (bf16[512,512]{1,0:T(8,128)(2,1)S(1)}, bf16[512,512]{1,0:T(8,128)(2,1)}, u32[]{:S(2)}) copy-start(bf16[512,512]{1,0:T(8,128)(2,1)} %get-tuple-element.51.refs_1_) | copy-start | bytes 1572868 | tf_op jit(solution)/shard_map/cond/branch_1_fun/cond
  63.1 15.4 %copy-start.13 = (bf16[512,512]{1,0:T(8,128)(2,1)S(1)}, bf16[512,512]{1,0:T(8,128)(2,1)}, u32[]{:S(2)}) copy-start(bf16[512,512]{1,0:T(8,128)(2,1)} %get-tuple-element.52.refs_2_.refs_4_) | copy-start | bytes 1572868 | tf_op jit(solution)/shard_map/cond/branch_1_fun/cond
  68.5 6.0 %collective-permute-start = (bf16[4,672,512]{2,1,0:T(8,128)(2,1)S(1)}, bf16[4,672,512]{2,1,0:T(8,128)(2,1)}, u32[]{:S(2)}, u32[]{:S(2)}) collective-permute-start(bf16[4,672,512]{2,1,0:T(8,128)(2,1)S(1)} %get-tuple-element.53), channel_id=1, source_target_pairs={{0,4},{4,0},{8,12},{12,8},{16,20},{20,16},{24,28},{28,24},{1,5},{5... | collective-permute-start | bytes 8257544 | tf_op jit(solution)/shard_map/cond/branch_1_fun/cond/branch_1_fun/ppermute | solution.py:295
  69.7 8.8 %collective-permute-start.1 = (bf16[4,672,512]{2,1,0:T(8,128)(2,1)S(1)}, bf16[4,672,512]{2,1,0:T(8,128)(2,1)}, u32[]{:S(2)}, u32[]{:S(2)}) collective-permute-start(bf16[4,672,512]{2,1,0:T(8,128)(2,1)S(1)} %get-tuple-element.54), channel_id=1, source_target_pairs={{0,4},{4,0},{8,12},{12,8},{16,20},{20,16},{24,28},{28,24},{1,5},{5... | collective-permute-start | bytes 8257544 | tf_op jit(solution)/shard_map/cond/branch_1_fun/cond/branch_1_fun/ppermute | solution.py:295
  83.3 2.6 %copy-start.1 = (bf16[5376,512]{1,0:T(8,128)(2,1)S(1)}, bf16[5376,512]{1,0:T(8,128)(2,1)}, u32[]{:S(2)}) copy-start(bf16[5376,512]{1,0:T(8,128)(2,1)} %refs_9_.1) | copy-start | bytes 16515076
  85.8 1.2 copy-start.8
  103.2 2.4 %copy-start.2 = (bf16[4,1344,512]{2,1,0:T(8,128)(2,1)}, bf16[4,1344,512]{2,1,0:T(8,128)(2,1)S(1)}, u32[]{:S(2)}) copy-start(bf16[4,1344,512]{2,1,0:T(8,128)(2,1)S(1)} %get-tuple-element.219) | copy-start | bytes 16515076
  105.7 1.0 copy-start.11
  106.7 34.2 %collective-permute-start.6 = (bf16[2,672,512]{2,1,0:T(8,128)(2,1)}, bf16[2,672,512]{2,1,0:T(8,128)(2,1)S(1)}, u32[]{:S(2)}, u32[]{:S(2)}) collective-permute-start(bf16[2,672,512]{2,1,0:T(8,128)(2,1)} %get-tuple-element.80), channel_id=1, source_target_pairs={{0,8},{4,12},{8,0},{12,4},{16,24},{20,28},{24,16},{28,20},{1,9},{5... | collective-permute-start | bytes 4128776 | tf_op jit(solution)/shard_map/cond/branch_1_fun/ppermute | solution.py:295
  109.7 34.6 %collective-permute-start.7 = (bf16[2,672,512]{2,1,0:T(8,128)(2,1)}, bf16[2,672,512]{2,1,0:T(8,128)(2,1)S(1)}, u32[]{:S(2)}, u32[]{:S(2)}) collective-permute-start(bf16[2,672,512]{2,1,0:T(8,128)(2,1)} %get-tuple-element.81), channel_id=1, source_target_pairs={{0,16},{4,20},{8,24},{12,28},{16,0},{20,4},{24,8},{28,12},{1,17},{... | collective-permute-start | bytes 4128776 | tf_op jit(solution)/shard_map/cond/branch_1_fun/ppermute | solution.py:295
  118.6 5.3 %collective-permute-start.4 = (bf16[4,672,512]{2,1,0:T(8,128)(2,1)S(1)}, bf16[4,672,512]{2,1,0:T(8,128)(2,1)}, u32[]{:S(2)}, u32[]{:S(2)}) collective-permute-start(bf16[4,672,512]{2,1,0:T(8,128)(2,1)S(1)} %get-tuple-element.74), channel_id=1, source_target_pairs={{0,4},{4,0},{8,12},{12,8},{16,20},{20,16},{24,28},{28,24},{1,5},{5... | collective-permute-start | bytes 8257544 | tf_op jit(solution)/shard_map/cond/branch_1_fun/cond/branch_1_fun/ppermute | solution.py:295
  118.7 9.2 %collective-permute-start.5 = (bf16[4,672,512]{2,1,0:T(8,128)(2,1)S(1)}, bf16[4,672,512]{2,1,0:T(8,128)(2,1)}, u32[]{:S(2)}, u32[]{:S(2)}) collective-permute-start(bf16[4,672,512]{2,1,0:T(8,128)(2,1)S(1)} %get-tuple-element.75), channel_id=1, source_target_pairs={{0,4},{4,0},{8,12},{12,8},{16,20},{20,16},{24,28},{28,24},{1,5},{5... | collective-permute-start | bytes 8257544 | tf_op jit(solution)/shard_map/cond/branch_1_fun/cond/branch_1_fun/ppermute | solution.py:295
  127.8 16.5 %copy-start.10 = (bf16[4,672,512]{2,1,0:T(8,128)(2,1)S(1)}, bf16[4,672,512]{2,1,0:T(8,128)(2,1)}, u32[]{:S(2)}) copy-start(bf16[4,672,512]{2,1,0:T(8,128)(2,1)} %get-tuple-element.76.refs_0_.refs_3_.refs_4_) | copy-start | bytes 8257540 | tf_op jit(solution)/shard_map/cond
  127.8 16.5 %copy-start.14 = (bf16[512,512]{1,0:T(8,128)(2,1)S(1)}, bf16[512,512]{1,0:T(8,128)(2,1)}, u32[]{:S(2)}) copy-start(bf16[512,512]{1,0:T(8,128)(2,1)} %get-tuple-element.92.refs_5_) | copy-start | bytes 1572868 | tf_op jit(solution)/shard_map/cond
  132.0 38.4 %collective-permute-start.10 = (bf16[2,672,512]{2,1,0:T(8,128)(2,1)S(1)}, bf16[2,672,512]{2,1,0:T(8,128)(2,1)S(1)}, u32[]{:S(2)}, u32[]{:S(2)}) collective-permute-start(bf16[2,672,512]{2,1,0:T(8,128)(2,1)S(1)} %get-tuple-element.88), channel_id=1, source_target_pairs={{0,8},{4,12},{8,0},{12,4},{16,24},{20,28},{24,16},{28,20},{1,9},{5... | collective-permute-start | bytes 4128776 | tf_op jit(solution)/shard_map/cond/branch_1_fun/ppermute | solution.py:295
  132.1 41.7 %collective-permute-start.11 = (bf16[2,672,512]{2,1,0:T(8,128)(2,1)S(1)}, bf16[2,672,512]{2,1,0:T(8,128)(2,1)S(1)}, u32[]{:S(2)}, u32[]{:S(2)}) collective-permute-start(bf16[2,672,512]{2,1,0:T(8,128)(2,1)S(1)} %get-tuple-element.89), channel_id=1, source_target_pairs={{0,16},{4,20},{8,24},{12,28},{16,0},{20,4},{24,8},{28,12},{1,17},{... | collective-permute-start | bytes 4128776 | tf_op jit(solution)/shard_map/cond/branch_1_fun/ppermute | solution.py:295
  144.3 29.5 %copy-start.15 = (bf16[512,512]{1,0:T(8,128)(2,1)S(1)}, bf16[512,512]{1,0:T(8,128)(2,1)}, u32[]{:S(2)}) copy-start(bf16[512,512]{1,0:T(8,128)(2,1)} %get-tuple-element.82.refs_1_) | copy-start | bytes 1572868 | tf_op jit(solution)/shard_map/cond
  144.3 29.5 %copy-start.16 = (bf16[512,512]{1,0:T(8,128)(2,1)S(1)}, bf16[512,512]{1,0:T(8,128)(2,1)}, u32[]{:S(2)}) copy-start(bf16[512,512]{1,0:T(8,128)(2,1)} %get-tuple-element.85.refs_4_.refs_5_) | copy-start | bytes 1572868 | tf_op jit(solution)/shard_map/cond
  146.7 41.8 %collective-permute-start.8 = (bf16[1,672,512]{2,1,0:T(8,128)(2,1)S(1)}, bf16[1,672,512]{2,1,0:T(8,128)(2,1)S(1)}, u32[]{:S(2)}, u32[]{:S(2)}) collective-permute-start(bf16[1,672,512]{2,1,0:T(8,128)(2,1)S(1)} %get-tuple-element.95), channel_id=1, source_target_pairs={{0,16},{4,20},{8,24},{12,28},{16,0},{20,4},{24,8},{28,12},{1,17},{... | collective-permute-start | bytes 2064392 | tf_op jit(solution)/shard_map/cond/branch_1_fun/ppermute | solution.py:295
  148.9 39.7 %collective-permute-start.9 = (bf16[1,672,512]{2,1,0:T(8,128)(2,1)S(1)}, bf16[1,672,512]{2,1,0:T(8,128)(2,1)S(1)}, u32[]{:S(2)}, u32[]{:S(2)}) collective-permute-start(bf16[1,672,512]{2,1,0:T(8,128)(2,1)S(1)} %get-tuple-element.96), channel_id=1, source_target_pairs={{0,8},{4,12},{8,0},{12,4},{16,24},{20,28},{24,16},{28,20},{1,9},{5... | collective-permute-start | bytes 2064392 | tf_op jit(solution)/shard_map/cond/branch_1_fun/ppermute | solution.py:295
  176.1 26.4 %collective-permute-start.12 = (bf16[1,672,512]{2,1,0:T(8,128)(2,1)S(1)}, bf16[1,672,512]{2,1,0:T(8,128)(2,1)S(1)}, u32[]{:S(2)}, u32[]{:S(2)}) collective-permute-start(bf16[1,672,512]{2,1,0:T(8,128)(2,1)S(1)} %get-tuple-element.101), channel_id=1, source_target_pairs={{0,16},{4,20},{8,24},{12,28},{16,0},{20,4},{24,8},{28,12},{1,17},{... | collective-permute-start | bytes 2064392 | tf_op jit(solution)/shard_map/cond/branch_1_fun/ppermute | solution.py:295
  178.3 24.2 %collective-permute-start.13 = (bf16[1,672,512]{2,1,0:T(8,128)(2,1)S(1)}, bf16[1,672,512]{2,1,0:T(8,128)(2,1)S(1)}, u32[]{:S(2)}, u32[]{:S(2)}) collective-permute-start(bf16[1,672,512]{2,1,0:T(8,128)(2,1)S(1)} %get-tuple-element.102), channel_id=1, source_target_pairs={{0,8},{4,12},{8,0},{12,4},{16,24},{20,28},{24,16},{28,20},{1,9},{5... | collective-permute-start | bytes 2064392 | tf_op jit(solution)/shard_map/cond/branch_1_fun/ppermute | solution.py:295
Sparse Core Ops, SparseCore 0:
  105.8 102.6 reduce-scatter.1
